TPU v7x, 512 devices: a whole 4x4x16 slice. The times are simulated.
512 devices in a mesh: row: 16 (over x, y_hi, core), col: 32 (over z, y_lo).
Axes of the slice: x: 4, y: 4 (y_hi: 2, y_lo: 2; y = y_hi * 2 + y_lo), z: 16, core: 2. Of those that a mesh axis runs over, the one named last changes fastest.
Arguments:
- covariance: float32 [16384, 16384], P('row', 'col'), may hold values from -6 to 6
- courant_table: float32 [8, 128], replicated, may hold values from -0.45 to 0.45
- step_wind_rows: int32 [2, 3], replicated, may hold values from 0 to 7
- barriers: int32 [4], replicated, may hold values from 1 to 127
- tracer_a_mixing: float32 [128, 128, 128], P('row'), may hold values from -1 to 2
- tracer_b_mixing: float32 [128, 128, 128], P('col'), may hold values from -1 to 2
Outputs:
- forecast: float32 [16384, 16384], P('col', 'row')
All inputs are finite; a program needn't handle non-finite values.
Results may differ from a plain program's by a relative error of at most 0.00016.
Values sent between devices are 32-bit elements; how exact they have to be, the bound alone decides.
No kernel may reach another device: no remote copies, remote signals or barrier semaphores. Data moves between devices by JAX's collectives and lax.ppermute only.
A program may use at most 64 MiB of HBM per device.

v0:
```python
import jax
import jax.numpy as jnp
from jax import lax
from jax.sharding import PartitionSpec as P

LAT = 128
STEPS = 3


def extended_2(cells, sides, width):
    for axis, dim in sides:
        count = lax.axis_size(axis)
        ends = count - 1
        head = lax.slice_in_dim(cells, 0, width, axis=dim)
        tail = lax.slice_in_dim(cells, cells.shape[dim] - width, cells.shape[dim], axis=dim)
        cells = jnp.concatenate(
            [
                lax.ppermute(tail, axis, [(i, (i + 1) % count) for i in range(ends)]),
                cells,
                lax.ppermute(head, axis, [((i + 1) % count, i) for i in range(ends)]),
            ],
            axis=dim,
        )
    return cells


def advance(extended, vertical_mixer, table_row, barriers, anchor, lat_count):
    edges = anchor + lax.iota(jnp.int32, lat_count + 1)
    inside = (edges >= 1) & (edges <= LAT - 1)
    courant = jnp.take(table_row, jnp.clip(edges, 0, LAT - 1))
    blocked = jnp.any(edges[:, None] == barriers[None, :], axis=1)
    courant = jnp.where(inside, courant * jnp.where(blocked, 0.25, 1.0), 0.0)
    spread = jnp.where(inside, 0.15, 0.0).astype(jnp.float32)[:, None, None]
    forward = jnp.maximum(courant, 0.0)[:, None, None]
    backward = jnp.maximum(-courant, 0.0)[:, None, None]
    fluxes = (
        forward * extended[:-1] - backward * extended[1:] + spread * (extended[:-1] - extended[1:])
    )
    shifted = extended[1:-1] + fluxes[:-1] - fluxes[1:]
    return jnp.einsum("lij,ljc->lic", vertical_mixer, shifted, precision=lax.Precision.HIGHEST)


def sweep_deep(padded, vertical_mixer, courant_table, rows_per_step, barriers, anchor, lat_rows):
    field = padded
    for moment in range(STEPS):
        margin = STEPS - 1 - moment
        lat_count = lat_rows + 2 * margin
        field = advance(
            field,
            vertical_mixer[moment : moment + lat_count],
            courant_table[rows_per_step[moment]],
            barriers,
            anchor - margin,
            lat_count,
        )
    return field


def per_device(
    covariance, courant_table, step_wind_rows, barriers, tracer_a_mixing, tracer_b_mixing
):
    lat_rows = tracer_a_mixing.shape[0]
    lat_cols = tracer_b_mixing.shape[0]
    levels = tracer_a_mixing.shape[1]
    columns = covariance.shape[1]
    field = covariance.reshape(lat_rows, levels, columns)
    anchor_a = lax.axis_index("row") * lat_rows
    padded = extended_2(field, (("row", 0),), STEPS)
    vertical_mixer = extended_2(tracer_a_mixing, (("row", 0),), STEPS - 1)
    field = sweep_deep(
        padded, vertical_mixer, courant_table, step_wind_rows[0], barriers, anchor_a, lat_rows
    )
    reversed_order = field.reshape(lat_rows * levels, columns).T
    field = reversed_order.reshape(lat_cols, levels, lat_rows * levels)
    anchor_b = lax.axis_index("col") * lat_cols
    padded = extended_2(field, (("col", 0),), STEPS)
    vertical_mixer = extended_2(tracer_b_mixing, (("col", 0),), STEPS - 1)
    field = sweep_deep(
        padded, vertical_mixer, courant_table, step_wind_rows[1], barriers, anchor_b, lat_cols
    )
    return field.reshape(lat_cols * levels, lat_rows * levels)


def solution(mesh):
    placed = (P("row", "col"), P(), P(), P(), P("row", None, None), P("col", None, None))
    return jax.shard_map(
        per_device, mesh=mesh, in_specs=placed, out_specs=P("col", "row"), check_vma=False
    )
```

profile of v0, /device:TPU:391, one launch (start us, length us, event | category | flops | bytes accessed | tf_op | source)
XLA Modules:
  0.0 150.1 jit_solution(2676540966062497145)
XLA Ops:
  0.0 2.7 %fusion.41 = (f32[384,512]{1,0:T(8,128)}, f32[384,512]{1,0:T(8,128)}) fusion(f32[1024,512]{1,0:T(8,128)} %param.8), kind=kLoop, calls=%fused_computation.131 | loop fusion | bytes 3145728 | tf_op jit(solution)/shard_map/slice | solution.py:15
  2.7 5.5 %collective-permute-start.4 = (f32[3,128,512]{2,1,0:T(8,128)}, f32[3,128,512]{2,1,0:T(8,128)}, u32[]{:S(2)}, u32[]{:S(2)}) collective-permute-start(f32[3,128,512]{2,1,0:T(8,128)} %bitcast), channel_id=1, source_target_pairs={{0,32},{32,64},{64,96},{96,128},{128,160},{160,192},{192,224},{224... | collective-permute-start | bytes 2359304 | tf_op jit(solution)/shard_map/ppermute | solution.py:18
  8.3 1.9 %collective-permute-start.5 = (f32[3,128,512]{2,1,0:T(8,128)}, f32[3,128,512]{2,1,0:T(8,128)}, u32[]{:S(2)}, u32[]{:S(2)}) collective-permute-start(f32[3,128,512]{2,1,0:T(8,128)} %bitcast.2), channel_id=1, source_target_pairs={{32,0},{64,32},{96,64},{128,96},{160,128},{192,160},{224,192},{256... | collective-permute-start | bytes 2359304 | tf_op jit(solution)/shard_map/ppermute | solution.py:20
  10.9 5.1 %collective-permute-start.2 = (f32[2,128,128]{2,1,0:T(8,128)S(1)}, f32[2,128,128]{2,1,0:T(8,128)S(1)}, u32[]{:S(2)}, u32[]{:S(2)}) collective-permute-start(f32[2,128,128]{2,1,0:T(8,128)S(1)} %get-tuple-element.25), channel_id=1, source_target_pairs={{0,32},{32,64},{64,96},{96,128},{128,160},{160,192},{192,224},{224... | collective-permute-start | bytes 393224 | tf_op jit(solution)/shard_map/ppermute | solution.py:18
  16.0 1.9 %collective-permute-start.3 = (f32[2,128,128]{2,1,0:T(8,128)}, f32[2,128,128]{2,1,0:T(8,128)S(1)}, u32[]{:S(2)}, u32[]{:S(2)}) collective-permute-start(f32[2,128,128]{2,1,0:T(8,128)} %get-tuple-element.24), channel_id=1, source_target_pairs={{32,0},{64,32},{96,64},{128,96},{160,128},{192,160},{224,192},{256... | collective-permute-start | bytes 393224 | tf_op jit(solution)/shard_map/ppermute | solution.py:20
  18.7 2.3 %collective-permute-start = (f32[2,128,128]{2,1,0:T(8,128)}, f32[2,128,128]{2,1,0:T(8,128)S(1)}, u32[]{:S(2)}, u32[]{:S(2)}) collective-permute-start(f32[2,128,128]{2,1,0:T(8,128)} %get-tuple-element.27), channel_id=1, source_target_pairs={{0,1},{1,2},{2,3},{3,4},{4,5},{5,6},{6,7},{7,8},{8,9},{9,10},{10,1... | collective-permute-start | bytes 393224 | tf_op jit(solution)/shard_map/ppermute | solution.py:18
  37.9 5.1 %collective-permute-start.1 = (f32[2,128,128]{2,1,0:T(8,128)}, f32[2,128,128]{2,1,0:T(8,128)S(1)}, u32[]{:S(2)}, u32[]{:S(2)}) collective-permute-start(f32[2,128,128]{2,1,0:T(8,128)} %get-tuple-element.26), channel_id=1, source_target_pairs={{1,0},{2,1},{3,2},{4,3},{5,4},{6,5},{7,6},{8,7},{9,8},{10,9},{11,1... | collective-permute-start | bytes 393224 | tf_op jit(solution)/shard_map/ppermute | solution.py:20
  43.1 1.8 %pad_maximum_fusion.1 = f32[14,128,512]{2,1,0:T(8,128)S(1)} fusion(f32[3,128,512]{2,1,0:T(8,128)} %collective-permute-done.5, f32[8,128,512]{2,1,0:T(8,128)S(1)} %bitcast.49, f32[3,128,512]{2,1,0:T(8,128)} %collective-permute-done.4), kind=kLoop, calls=%fused_computation.12 | loop fusion | flops 1835008 | bytes 7340032 | tf_op jit(solution)/shard_map/concatenate | solution.py:16
  45.7 2.9 %fusion.4 = f32[12,128,512]{2,1,0:T(8,128)S(1)} fusion(f32[12,128,128]{2,1,0:T(8,128)S(1)} %constant_dynamic-update-slice_fusion.3, f32[13,128,512]{2,1,0:T(8,128)S(1)} %multiply_add_fusion.2, f32[14,128,512]{2,1,0:T(8,128)S(1)} %pad_maximum_fusion.1), kind=kOutput, calls=%fused_computation.20 | convolution fusion | flops 1209532416 | bytes 13369344 | tf_op jit(solution)/shard_map/lij,ljc->lic/dot_general | solution.py:40
  49.3 2.5 %fusion.6 = f32[10,128,512]{2,1,0:T(8,128)S(1)} fusion(f32[12,128,128]{2,1,0:T(8,128)S(1)} %constant_dynamic-update-slice_fusion.3, f32[11,128,512]{2,1,0:T(8,128)S(1)} %multiply_add_fusion.3, f32[12,128,512]{2,1,0:T(8,128)S(1)} %fusion.4), kind=kOutput, calls=%fused_computation.25 | convolution fusion | flops 1007943680 | bytes 11272192 | tf_op jit(solution)/shard_map/lij,ljc->lic/dot_general | solution.py:40
  52.4 2.1 %fusion.10 = f32[8,512,128]{1,2,0:T(8,128)S(1)} fusion(f32[8,128,128]{2,1,0:T(8,128)S(1)} %copy-done.1, f32[9,128,512]{2,1,0:T(8,128)S(1)} %multiply_add_fusion.5, f32[10,128,512]{2,1,0:T(8,128)S(1)} %fusion.6), kind=kOutput, calls=%fused_computation.35 | convolution fusion | flops 806354944 | bytes 8912896 | tf_op jit(solution)/shard_map/lij,ljc->lic/dot_general | solution.py:40
  54.5 1.9 %fusion.40 = (f32[384,1024]{0,1:T(8,128)}, f32[384,1024]{0,1:T(8,128)}) fusion(f32[512,1024]{0,1:T(8,128)S(1)} %bitcast.46), kind=kLoop, calls=%fused_computation.130 | loop fusion | bytes 6291456 | tf_op jit(solution)/shard_map/slice | solution.py:15
  56.4 3.0 %copy.13 = f32[384,1024]{1,0:T(8,128)} copy(f32[384,1024]{0,1:T(8,128)} %get-tuple-element.20) | data formatting | bytes 3145728 | tf_op jit(solution)/shard_map/slice | solution.py:15
  59.5 1.9 %collective-permute-start.6 = (f32[3,128,1024]{2,1,0:T(8,128)}, f32[3,128,1024]{2,1,0:T(8,128)}, u32[]{:S(2)}, u32[]{:S(2)}) collective-permute-start(f32[3,128,1024]{2,1,0:T(8,128)} %bitcast.50), channel_id=1, source_target_pairs={{0,1},{1,2},{2,3},{3,4},{4,5},{5,6},{6,7},{7,8},{8,9},{9,10},{10,1... | collective-permute-start | bytes 4718600 | tf_op jit(solution)/shard_map/ppermute | solution.py:18
  61.4 3.0 %copy.15 = f32[384,1024]{1,0:T(8,128)} copy(f32[384,1024]{0,1:T(8,128)} %get-tuple-element.21) | data formatting | bytes 3145728 | tf_op jit(solution)/shard_map/slice | solution.py:14
  64.4 5.5 %collective-permute-start.7 = (f32[3,128,1024]{2,1,0:T(8,128)}, f32[3,128,1024]{2,1,0:T(8,128)}, u32[]{:S(2)}, u32[]{:S(2)}) collective-permute-start(f32[3,128,1024]{2,1,0:T(8,128)} %bitcast.51), channel_id=1, source_target_pairs={{1,0},{2,1},{3,2},{4,3},{5,4},{6,5},{7,6},{8,7},{9,8},{10,9},{11,1... | collective-permute-start | bytes 4718600 | tf_op jit(solution)/shard_map/ppermute | solution.py:20
  70.1 1.8 %copy.14 = f32[512,1024]{1,0:T(8,128)} copy(f32[512,1024]{0,1:T(8,128)S(1)} %bitcast.47) | data formatting | bytes 4194304 | tf_op jit(solution)/shard_map/transpose | solution.py:73
  71.9 54.7 %collective-permute-done.6 = f32[3,128,1024]{2,1,0:T(8,128)} collective-permute-done((f32[3,128,1024]{2,1,0:T(8,128)}, f32[3,128,1024]{2,1,0:T(8,128)}, u32[]{:S(2)}, u32[]{:S(2)}) %collective-permute-start.6) | collective-permute-done | bytes 1572896 | tf_op jit(solution)/shard_map/ppermute | solution.py:18
  126.5 7.2 %collective-permute-done.7 = f32[3,128,1024]{2,1,0:T(8,128)} collective-permute-done((f32[3,128,1024]{2,1,0:T(8,128)}, f32[3,128,1024]{2,1,0:T(8,128)}, u32[]{:S(2)}, u32[]{:S(2)}) %collective-permute-start.7) | collective-permute-done | bytes 1572896 | tf_op jit(solution)/shard_map/ppermute | solution.py:20
  133.8 3.0 %pad_maximum_fusion = f32[10,128,1024]{2,1,0:T(8,128)S(1)} fusion(f32[3,128,1024]{2,1,0:T(8,128)} %collective-permute-done.7, f32[4,128,1024]{2,1,0:T(8,128)} %bitcast.48, f32[3,128,1024]{2,1,0:T(8,128)} %collective-permute-done.6), kind=kLoop, calls=%fused_computation.6 | loop fusion | flops 2621440 | bytes 10485760 | tf_op jit(solution)/shard_map/concatenate | solution.py:16
  136.8 1.3 multiply_add_fusion
  138.1 4.0 %fusion = f32[8,128,1024]{2,1,0:T(8,128)S(1)} fusion(f32[8,128,128]{2,1,0:T(8,128)S(1)} %constant_dynamic-update-slice_fusion, f32[9,128,1024]{2,1,0:T(8,128)S(1)} %multiply_add_fusion, f32[10,128,1024]{2,1,0:T(8,128)S(1)} %pad_maximum_fusion), kind=kOutput, calls=%fused_computation.9 | convolution fusion | flops 1612709888 | bytes 17301504 | tf_op jit(solution)/shard_map/lij,ljc->lic/dot_general | solution.py:40
  143.1 3.0 %fusion.2 = f32[6,128,1024]{2,1,0:T(8,128)S(1)} fusion(f32[8,128,128]{2,1,0:T(8,128)S(1)} %constant_dynamic-update-slice_fusion, f32[7,128,1024]{2,1,0:T(8,128)S(1)} %multiply_add_fusion.1, f32[8,128,1024]{2,1,0:T(8,128)S(1)} %fusion), kind=kOutput, calls=%fused_computation.16 | convolution fusion | flops 1209532416 | bytes 13107200 | tf_op jit(solution)/shard_map/lij,ljc->lic/dot_general | solution.py:40
  146.7 3.4 %fusion.8 = f32[4,1024,128]{1,2,0:T(8,128)} fusion(f32[4,128,128]{2,1,0:T(8,128)S(1)} %copy-done.2, f32[5,128,1024]{2,1,0:T(8,128)S(1)} %multiply_add_fusion.4, f32[6,128,1024]{2,1,0:T(8,128)S(1)} %fusion.2), kind=kOutput, calls=%fused_computation.31 | convolution fusion | flops 806354944 | bytes 8650752 | tf_op jit(solution)/shard_map/lij,ljc->lic/dot_general | solution.py:40
  (76 shorter events, 10.5 us)
Async XLA Ops:
  0.0 10.2 %copy-start.1 = (f32[8,128,128]{2,1,0:T(8,128)S(1)}, f32[8,128,128]{2,1,0:T(8,128)}, u32[]{:S(2)}) copy-start(f32[8,128,128]{2,1,0:T(8,128)} %param.12) | copy-start | bytes 1572868
  0.0 17.9 %copy-start.2 = (f32[4,128,128]{2,1,0:T(8,128)S(1)}, f32[4,128,128]{2,1,0:T(8,128)}, u32[]{:S(2)}) copy-start(f32[4,128,128]{2,1,0:T(8,128)} %param.13) | copy-start | bytes 786436
  0.0 21.0 %copy-start.3 = (s32[2,3]{1,0:T(2,128)S(1)}, s32[2,3]{1,0:T(2,128)}, u32[]{:S(2)}) copy-start(s32[2,3]{1,0:T(2,128)} %param.10) | copy-start | bytes 76
  0.0 33.3 %copy-start.4 = (f32[8,128]{1,0:T(8,128)S(1)}, f32[8,128]{1,0:T(8,128)}, u32[]{:S(2)}) copy-start(f32[8,128]{1,0:T(8,128)} %param.9) | copy-start | bytes 12292
  0.0 34.0 %copy-start.5 = (s32[4]{0:T(128)S(1)}, s32[4]{0:T(128)}, u32[]{:S(2)}) copy-start(s32[4]{0:T(128)} %param.11) | copy-start | bytes 52
  2.7 40.4 %copy-start = (f32[1024,512]{1,0:T(8,128)S(1)}, f32[1024,512]{1,0:T(8,128)}, u32[]{:S(2)}) copy-start(f32[1024,512]{1,0:T(8,128)} %param.8) | copy-start | bytes 6291460
  2.7 40.4 %collective-permute-start.4 = (f32[3,128,512]{2,1,0:T(8,128)}, f32[3,128,512]{2,1,0:T(8,128)}, u32[]{:S(2)}, u32[]{:S(2)}) collective-permute-start(f32[3,128,512]{2,1,0:T(8,128)} %bitcast), channel_id=1, source_target_pairs={{0,32},{32,64},{64,96},{96,128},{128,160},{160,192},{192,224},{224... | collective-permute-start | bytes 2359304 | tf_op jit(solution)/shard_map/ppermute | solution.py:18
  8.3 34.9 %collective-permute-start.5 = (f32[3,128,512]{2,1,0:T(8,128)}, f32[3,128,512]{2,1,0:T(8,128)}, u32[]{:S(2)}, u32[]{:S(2)}) collective-permute-start(f32[3,128,512]{2,1,0:T(8,128)} %bitcast.2), channel_id=1, source_target_pairs={{32,0},{64,32},{96,64},{128,96},{160,128},{192,160},{224,192},{256... | collective-permute-start | bytes 2359304 | tf_op jit(solution)/shard_map/ppermute | solution.py:20
  10.9 27.1 %collective-permute-start.2 = (f32[2,128,128]{2,1,0:T(8,128)S(1)}, f32[2,128,128]{2,1,0:T(8,128)S(1)}, u32[]{:S(2)}, u32[]{:S(2)}) collective-permute-start(f32[2,128,128]{2,1,0:T(8,128)S(1)} %get-tuple-element.25), channel_id=1, source_target_pairs={{0,32},{32,64},{64,96},{96,128},{128,160},{160,192},{192,224},{224... | collective-permute-start | bytes 393224 | tf_op jit(solution)/shard_map/ppermute | solution.py:18
  16.0 27.1 %collective-permute-start.3 = (f32[2,128,128]{2,1,0:T(8,128)}, f32[2,128,128]{2,1,0:T(8,128)S(1)}, u32[]{:S(2)}, u32[]{:S(2)}) collective-permute-start(f32[2,128,128]{2,1,0:T(8,128)} %get-tuple-element.24), channel_id=1, source_target_pairs={{32,0},{64,32},{96,64},{128,96},{160,128},{192,160},{224,192},{256... | collective-permute-start | bytes 393224 | tf_op jit(solution)/shard_map/ppermute | solution.py:20
  18.7 51.3 %collective-permute-start = (f32[2,128,128]{2,1,0:T(8,128)}, f32[2,128,128]{2,1,0:T(8,128)S(1)}, u32[]{:S(2)}, u32[]{:S(2)}) collective-permute-start(f32[2,128,128]{2,1,0:T(8,128)} %get-tuple-element.27), channel_id=1, source_target_pairs={{0,1},{1,2},{2,3},{3,4},{4,5},{5,6},{6,7},{7,8},{8,9},{9,10},{10,1... | collective-permute-start | bytes 393224 | tf_op jit(solution)/shard_map/ppermute | solution.py:18
  37.9 32.1 %collective-permute-start.1 = (f32[2,128,128]{2,1,0:T(8,128)}, f32[2,128,128]{2,1,0:T(8,128)S(1)}, u32[]{:S(2)}, u32[]{:S(2)}) collective-permute-start(f32[2,128,128]{2,1,0:T(8,128)} %get-tuple-element.26), channel_id=1, source_target_pairs={{1,0},{2,1},{3,2},{4,3},{5,4},{6,5},{7,6},{8,7},{9,8},{10,9},{11,1... | collective-permute-start | bytes 393224 | tf_op jit(solution)/shard_map/ppermute | solution.py:20
  59.5 67.1 %collective-permute-start.6 = (f32[3,128,1024]{2,1,0:T(8,128)}, f32[3,128,1024]{2,1,0:T(8,128)}, u32[]{:S(2)}, u32[]{:S(2)}) collective-permute-start(f32[3,128,1024]{2,1,0:T(8,128)} %bitcast.50), channel_id=1, source_target_pairs={{0,1},{1,2},{2,3},{3,4},{4,5},{5,6},{6,7},{7,8},{8,9},{9,10},{10,1... | collective-permute-start | bytes 4718600 | tf_op jit(solution)/shard_map/ppermute | solution.py:18
  64.4 69.4 %collective-permute-start.7 = (f32[3,128,1024]{2,1,0:T(8,128)}, f32[3,128,1024]{2,1,0:T(8,128)}, u32[]{:S(2)}, u32[]{:S(2)}) collective-permute-start(f32[3,128,1024]{2,1,0:T(8,128)} %bitcast.51), channel_id=1, source_target_pairs={{1,0},{2,1},{3,2},{4,3},{5,4},{6,5},{7,6},{8,7},{9,8},{10,9},{11,1... | collective-permute-start | bytes 4718600 | tf_op jit(solution)/shard_map/ppermute | solution.py:20
where the time goes:
time: 151 us; the launch traced here: 150 us
  waiting for transfers between devices  61.9 us (41%)
  starting transfers between devices  29.2 us (19%)
  local copies, waits for them, and re-layouts  18.6 us (12%)
  matrix products  17.9 us (12%)
  between operations  12.1 us (8%)
  other arithmetic  10.4 us (7%)
    ppermute x4, waiting for transfers between devices, extended_2(): lax.ppermute(tail, axis, [(i, (i + 1) % count) for i in range(ends)])  54.7 us
    dot_general x6, matrix products, advance(): jnp.einsum('lij,ljc->lic', vertical_mixer, shifted, precision=lax.Precisi...  17.9 us
    ppermute x4, starting transfers between devices, extended_2(): lax.ppermute(tail, axis, [(i, (i + 1) % count) for i in range(ends)])  14.8 us
    ppermute x4, starting transfers between devices, extended_2(): lax.ppermute(head, axis, [((i + 1) % count, i) for i in range(ends)])  14.4 us
    slice x3, local copies, waits for them, and re-layouts, extended_2(): lax.slice_in_dim(cells, cells.shape[dim] - width, cells.shape[dim], axis=...  7.64 us
    ppermute x4, waiting for transfers between devices, extended_2(): lax.ppermute(head, axis, [((i + 1) % count, i) for i in range(ends)])  7.25 us
    add x6, other arithmetic, advance(): forward * extended[:-1] - backward * extended[1:]  4.97 us
    concatenate x2, other arithmetic, extended_2(): jnp.concatenate([lax.ppermute(tail, axis, [(i, (i + 1) % count) for i in...  4.77 us
  transfers between devices with their start and end apart: 8, of which 2 were waited for; matrix products, arithmetic and copies ran while one was open for 19% of the time, Pallas kernels for 0%

commit v1 on v0

v1 whole, which is shorter than its diff:
```python
import functools
import itertools

import jax
import jax.numpy as jnp
from jax import lax
from jax.experimental import pallas as pl
from jax.experimental.pallas import tpu as pltpu
from jax.sharding import PartitionSpec as P

LAT = 128
LEV = 128
STEPS = 3
SPREAD = 0.15
WINDOW = 14
F32, BF16 = jnp.float32, jnp.bfloat16
AXES = ("row", "col")
ANY = pl.BlockSpec(memory_space=pl.ANY)
SMEM = pl.BlockSpec(memory_space=pltpu.SMEM)
VMEM = pl.BlockSpec(memory_space=pltpu.VMEM)


def pairs(move, x_size, z_size):
    number = lambda x, h, k, z, l: ((x * 2 + h) * 2 + k) * (2 * z_size) + z * 2 + l
    listed = []
    for x, h, k, z, l in itertools.product(range(x_size), range(2), range(2), range(z_size), range(2)):
        to = move(x, h, k, z, l)
        if to is not None and 0 <= to[0] < x_size and 0 <= to[3] < z_size:
            listed.append((number(x, h, k, z, l), number(*to)))
    return listed


def row_shift(x, h, k, by):
    at = (x * 2 + h) * 2 + k + by
    return at // 4, (at // 2) % 2, at % 2


def swap_y(x, h, k, z, l):
    return x, h, k, z, 1 - l


def near_z(x, h, k, z, l):
    return x, h, k, z + (1 if l else -1), l


def far_z(x, h, k, z, l):
    return x, h, k, z + (-1 if l else 1), l


def mats_group(x, h, k, z, l):
    return x, 1 - h, k, z, 1 - l


def mats_far(x, h, k, z, l):
    return x, 1 - h, k, z + (1 if l else -1), 1 - l


def mats_row(by, x, h, k, z, l):
    tx, th, tk = row_shift(x, h, k, by)
    return tx, th, tk, z, (l if (tx, th) == (x, h) else 1 - l)


def halo_same(x, h, k, z, l):
    return *row_shift(x, h, k, 1 if l else -1), z, l


def halo_cross(x, h, k, z, l):
    tx, th, tk = row_shift(x, h, k, 1 if l else -1)
    return None if (tx, th) == (x, h) else (tx, th, tk, z, 1 - l)


def relay_core(x, h, k, z, l):
    return (x, h, 1 - k, z, l) if k == l else None


def side():
    return lax.rem(lax.axis_index("col"), 2)


def turned(l, q, count):
    return jnp.where(l == 1, q, count - 1 - q)


def rows_of(l, chunk):
    return l * 768 if chunk == 0 else 256 + l * 256


def run_copies(copies, sems):
    started = []
    for i, (src, dst) in enumerate(copies):
        copy = pltpu.make_async_copy(src, dst, sems.at[i])
        copy.start()
        started.append(copy)
    for copy in started:
        copy.wait()


def lanes(start):
    return pl.ds(pl.multiple_of(start * LEV, LEV), LEV)


def rows(start, size):
    return pl.ds(pl.multiple_of(start, LEV), size)


def pack_first(cov, out, sems):
    l = side()
    at = rows_of(1 - l, 0)
    run_copies([(cov.at[rows(at, 256), lanes(l + i)], out.at[i]) for i in range(3)], sems)


def pack_rest(cov, mix, second, single, near, edge, sems):
    l = side()
    at = rows_of(1 - l, 1)
    copies = [(cov.at[rows(at, 256), lanes(l + i)], second.at[i]) for i in range(3)]
    for c in range(2):
        copies.append((cov.at[rows(rows_of(1 - l, c), 256), lanes(3 - 3 * l)], single.at[c]))
        for i in range(3):
            copies.append((cov.at[rows(rows_of(l, c), 256), lanes(l + i)], near.at[3 * c + i]))
    for m in range(2):
        copies.append((mix.at[2 * l + m], near.at[6, pl.ds(m * LEV, LEV)]))
        copies.append((mix.at[2 * l + m], edge.at[m]))
    run_copies(copies, sems)


def write_coefficients(l, base, tracer, table, winds, barriers, coef, flow):
    def interface(step, n):
        g = base + n - 3
        inside = (g >= 1) & (g <= LAT - 1)
        c = table[winds[tracer, step], jnp.clip(g, 0, LAT - 1)]
        blocked = barriers[0] == g
        for b in range(1, 4):
            blocked = blocked | (barriers[b] == g)
        c = c * jnp.where(blocked, 0.25, 1.0)
        flow[0, n] = jnp.where(inside, jnp.maximum(c, 0.0) + SPREAD, 0.0)
        flow[1, n] = jnp.where(inside, jnp.maximum(-c, 0.0) + SPREAD, 0.0)

    for step in range(STEPS):
        lax.fori_loop(0, WINDOW + 1, lambda n, _: interface(step, n), None)

        def place(p, _):
            n = turned(l, p, WINDOW)
            below, above = flow[0, n], flow[1, n + 1]
            coef[step * 48 + p] = jnp.where(l == 1, below, above)
            coef[step * 48 + 16 + p] = 1.0 - flow[1, n] - flow[0, n + 1]
            coef[step * 48 + 32 + p] = jnp.where(l == 1, above, below)

        lax.fori_loop(0, WINDOW, place, None)


def write_weight(weights, at, mixer):
    turned_mixer = mixer.T
    high = turned_mixer.astype(BF16)
    low = (turned_mixer - high.astype(F32)).astype(BF16)
    for half in range(2):
        weights[at, half * LEV : (half + 1) * LEV, :LEV] = high
        weights[at, half * LEV : (half + 1) * LEV, LEV:] = low


def prepare_b(table, winds, barriers, near, group, own, far, weights, coef, flow):
    l = side()
    base = lax.axis_index("col") // 2 * 8
    write_coefficients(l, base, 1, table, winds, barriers, coef, flow)
    for q in range(2):
        m = turned(l, q, 2)
        write_weight(weights, q, near[0, pl.ds(pl.multiple_of(m * LEV, LEV), LEV), :])
        write_weight(weights, 10 + q, far[m])
    for q in range(4):
        b = turned(l, q, 4)
        write_weight(weights, 2 + q, group[b])
        write_weight(weights, 6 + q, own[b])


def prepare_a(table, winds, barriers, own, before, after, weights, coef, flow):
    l = side()
    base = lax.axis_index("row") * 8
    write_coefficients(l, base, 0, table, winds, barriers, coef, flow)
    for q in range(8):
        write_weight(weights, 2 + q, own[turned(l, q, 8)])
    for q in range(2):
        write_weight(weights, q, jnp.where(l == 1, before[q], after[1 - q]))
        write_weight(weights, 10 + q, jnp.where(l == 1, after[q], before[1 - q]))


def step_latitude(step, p, source, weights, coef):
    y = (
        coef[step * 48 + p] * source[p - 1]
        + coef[step * 48 + 16 + p] * source[p]
        + coef[step * 48 + 32 + p] * source[p + 1]
    )
    high = y.astype(BF16)
    low = (y - high.astype(F32)).astype(BF16)
    both = jnp.dot(
        jnp.concatenate([high, low], axis=1), weights[p - 1], preferred_element_type=F32
    )
    return both[:, :LEV] + both[:, LEV:]


def first_steps(window, other, weights, coef):
    def first(p, _):
        other[p] = step_latitude(0, p, window, weights, coef)

    def second(p, _):
        window[p] = step_latitude(1, p, other, weights, coef)

    lax.fori_loop(1, WINDOW - 1, first, None)
    lax.fori_loop(2, WINDOW - 2, second, None)


def sweep_b(chunk, *refs):
    if chunk == 0:
        coef, weights, cov, pair, single, near, far, kept, sent, window, other, sems = refs
    else:
        (coef, weights, cov, pair, single, near, far, kept_before, sent_before,
         kept, sent, same, cross, window, other, sems, late) = refs
    l = side()
    copies = []
    for q in range(3):
        t = turned(l, q, 3)
        copies.append((near.at[3 * chunk + t], window.at[q]))
        copies.append((pair.at[t], window.at[3 + q]))
        copies.append((far.at[t], window.at[11 + q]))
    copies.append((single.at[chunk], window.at[6]))
    for q in range(4):
        copies.append((cov.at[rows(rows_of(l, chunk), 256), lanes(turned(l, q, 4))], window.at[7 + q]))
    run_copies(copies, sems)
    first_steps(window, other, weights, coef)

    def finish(p, target, q):
        z = step_latitude(2, p, window, weights, coef)
        b = turned(l, q, 4)
        for i in range(2):
            u = turned(l, i, 2)
            target[u, rows(b * LEV, LEV), :] = z[i * LEV : (i + 1) * LEV].T

    lax.fori_loop(0, 4, lambda q, _: finish(3 + q, sent, q), None)
    lax.fori_loop(0, 4, lambda q, _: finish(7 + q, kept, q), None)
    if chunk == 1:
        run_copies(
            [
                (kept_before, same.at[pl.ds(1, 2)]),
                (sent_before, cross.at[pl.ds(1, 2)]),
                (kept.at[1], same.at[0]),
                (sent.at[1], cross.at[0]),
            ],
            late,
        )


def sweep_a(coef, weights, kept_0, kept_1, got_0, got_1, same, cross, relay_0, relay_1, out,
            window, other, sems):
    l = side()
    k = lax.rem(lax.axis_index("row"), 2)
    copies = [(same.at[q], window.at[q]) for q in range(3)]
    for u in range(2):
        copies.append((kept_1.at[u], window.at[7 + u]))
        copies.append((kept_0.at[u], window.at[9 + u]))
        copies.append((got_0.at[u], window.at[4 - u]))
        copies.append((got_1.at[u], window.at[6 - u]))
    across = [(cross.at[q], window.at[13 - q]) for q in range(3)]
    inside = [(relay_1.at[1], window.at[13])] + [(relay_0.at[u], window.at[12 - u]) for u in range(2)]

    @pl.when(k == l)
    def _():
        run_copies(across, sems)

    @pl.when(k != l)
    def _():
        run_copies(inside, sems)

    run_copies(copies, sems)
    first_steps(window, other, weights, coef)

    def finish(p, _):
        out[:, lanes(turned(l, p - 3, 8))] = step_latitude(2, p, window, weights, coef)

    lax.fori_loop(3, WINDOW - 3, finish, None)


def call(kernel, outs, in_specs, out_specs, scratch, flops, name):
    return pl.pallas_call(
        kernel,
        out_shape=outs,
        in_specs=in_specs,
        out_specs=out_specs,
        scratch_shapes=scratch,
        compiler_params=pltpu.CompilerParams(vmem_limit_bytes=40 * 1024 * 1024),
        cost_estimate=pl.CostEstimate(flops=flops, bytes_accessed=2**21, transcendentals=0),
        name=name,
    )


def shaped(*dims, dtype=F32):
    return jax.ShapeDtypeStruct(dims, dtype)


def per_device(x_size, z_size, covariance, table, winds, barriers, mix_a, mix_b):
    send = lambda value, move: lax.ppermute(value, AXES, pairs(move, x_size, z_size))
    dma = lambda n: pltpu.SemaphoreType.DMA((n,))

    out_0 = call(pack_first, shaped(3, 256, LEV), [ANY], ANY, [dma(3)], 0, "pack_first")(covariance)
    pair_0 = send(out_0, swap_y)
    out_1, out_single, out_near, edge = call(
        pack_rest,
        (shaped(3, 256, LEV), shaped(2, 256, LEV), shaped(7, 256, LEV), shaped(2, LEV, LEV)),
        [ANY, ANY], (ANY,) * 4, [dma(15)], 0, "pack_rest",
    )(covariance, mix_b)
    near = send(out_near, near_z)
    pair_1 = send(out_1, swap_y)
    far_0 = send(pair_0, far_z)
    single = send(out_single, swap_y)
    far_1 = send(pair_1, far_z)
    group = send(mix_b, mats_group)
    edge_far = send(edge, mats_far)
    before = send(mix_a[6:8], functools.partial(mats_row, 1))
    after = send(mix_a[0:2], functools.partial(mats_row, -1))

    prep_outs = (shaped(12, 256, 256, dtype=BF16), shaped(144))
    prep_scratch = [pltpu.SMEM((2, 16), F32)]
    weights_b, coef_b = call(
        prepare_b, prep_outs, [SMEM] * 3 + [VMEM] * 4, (VMEM, SMEM), prep_scratch, 10**8, "prepare_b"
    )(table, winds, barriers, near[6:7], group, mix_b, edge_far)
    weights_a, coef_a = call(
        prepare_a, prep_outs, [SMEM] * 3 + [VMEM] * 3, (VMEM, SMEM), prep_scratch, 10**8, "prepare_a"
    )(table, winds, barriers, mix_a, before, after)

    block = shaped(2, 512, LEV)
    field = pltpu.VMEM((WINDOW, 256, LEV), F32)
    kept_0, sent_0 = call(
        functools.partial(sweep_b, 0), (block,) * 2, [SMEM, VMEM] + [ANY] * 5, (VMEM,) * 2,
        [field, field, dma(14)], 2 * 10**9, "sweep_b0",
    )(coef_b, weights_b, covariance, pair_0, single, near, far_0)
    got_0 = send(sent_0, swap_y)
    kept_1, sent_1, out_same, out_cross = call(
        functools.partial(sweep_b, 1), (block,) * 2 + (shaped(3, 512, LEV),) * 2,
        [SMEM, VMEM] + [ANY] * 7, (VMEM, VMEM, ANY, ANY),
        [field, field, dma(14), dma(4)], 2 * 10**9, "sweep_b1",
    )(coef_b, weights_b, covariance, pair_1, single, near, far_1, kept_0, sent_0)
    got_1 = send(sent_1, swap_y)
    same = send(out_same, halo_same)
    cross = send(out_cross, halo_cross)
    relay_0 = send(got_0, relay_core)
    relay_1 = send(got_1, relay_core)

    field = pltpu.VMEM((WINDOW, 512, LEV), F32)
    return call(
        sweep_a, shaped(512, 1024), [SMEM, VMEM] + [ANY] * 8, VMEM, [field, field, dma(11)],
        4 * 10**9, "sweep_a",
    )(coef_a, weights_a, kept_0, kept_1, got_0, got_1, same, cross, relay_0, relay_1)


def solution(mesh):
    placed = (P("row", "col"), P(), P(), P(), P("row", None, None), P("col", None, None))
    return jax.shard_map(
        functools.partial(per_device, mesh.shape["row"] // 4, mesh.shape["col"] // 2),
        mesh=mesh, in_specs=placed, out_specs=P("col", "row"), check_vma=False,
    )
```

time: 151 us -> 124 us (0.82)
  the two profiles are of different devices: /device:TPU:391 before, /device:TPU:249 now
where the time goes in v1:
time: 124 us; the launch traced here: 123 us
  starting transfers between devices  65 us (52%)
  Pallas kernels  33.4 us (27%)
  waiting for transfers between devices  21.9 us (18%)
  local copies, waits for them, and re-layouts  2.6 us (2%)
    ppermute x16, starting transfers between devices, per_device(): lax.ppermute(value, AXES, pairs(move, x_size, z_size))  65 us
    ppermute x16, waiting for transfers between devices, per_device(): lax.ppermute(value, AXES, pairs(move, x_size, z_size))  21.9 us
    pallas_call x1, Pallas kernels, per_device(): call(sweep_a, shaped(512, 1024), [SMEM, VMEM] + [ANY] * 8, VMEM, [field,...  9.47 us
    pallas_call x1, Pallas kernels, per_device(): call(functools.partial(sweep_b, 1), (block,) * 2 + (shaped(3, 512, LEV),)...  9.09 us
    pallas_call x1, Pallas kernels, per_device(): call(functools.partial(sweep_b, 0), (block,) * 2, [SMEM, VMEM] + [ANY] *...  8.94 us
    pallas_call x1, Pallas kernels, per_device(): call(prepare_a, prep_outs, [SMEM] * 3 + [VMEM] * 3, (VMEM, SMEM), prep_sc...  2.57 us
    unnamed x16, local copies, waits for them, and re-layouts  2.57 us
  transfers between devices with their start and end apart: 16, of which 6 were waited for; matrix products, arithmetic and copies ran while one was open for 0% of the time, Pallas kernels for 11%

profile of v1, /device:TPU:249, one launch (start us, length us, event | category | flops | bytes accessed | tf_op | source)
XLA Modules:
  0.0 123.2 jit_solution(12133534231056066826)
XLA Ops:
  3.3 4.9 %collective-permute-start.2 = (f32[7,256,128]{2,1,0:T(8,128)S(1)}, f32[7,256,128]{2,1,0:T(8,128)S(1)}, u32[]{:S(2)}, u32[]{:S(2)}) collective-permute-start(f32[7,256,128]{2,1,0:T(8,128)S(1)} %get-tuple-element.21), channel_id=1, source_target_pairs={{1,3},{2,0},{3,5},{4,2},{5,7},{6,4},{7,9},{8,6},{9,11},{10,8},{11,... | collective-permute-start | bytes 2752520 | tf_op jit(solution)/shard_map/ppermute | solution.py:298
  8.3 1.9 %collective-permute-start.5 = (f32[3,256,128]{2,1,0:T(8,128)S(1)}, f32[3,256,128]{2,1,0:T(8,128)S(1)}, u32[]{:S(2)}, u32[]{:S(2)}) collective-permute-start(f32[3,256,128]{2,1,0:T(8,128)S(1)} %pack_first.1), channel_id=1, source_target_pairs={{0,1},{1,0},{2,3},{3,2},{4,5},{5,4},{6,7},{7,6},{8,9},{9,8},{10,11... | collective-permute-start | bytes 1179656 | tf_op jit(solution)/shard_map/ppermute | solution.py:298
  10.2 3.4 %collective-permute-start.8 = (f32[3,256,128]{2,1,0:T(8,128)S(1)}, f32[3,256,128]{2,1,0:T(8,128)S(1)}, u32[]{:S(2)}, u32[]{:S(2)}) collective-permute-start(f32[3,256,128]{2,1,0:T(8,128)S(1)} %get-tuple-element.27), channel_id=1, source_target_pairs={{0,1},{1,0},{2,3},{3,2},{4,5},{5,4},{6,7},{7,6},{8,9},{9,8},{10,11... | collective-permute-start | bytes 1179656 | tf_op jit(solution)/shard_map/ppermute | solution.py:298
  13.6 6.3 %collective-permute-done.5.refs_3_ = f32[3,256,128]{2,1,0:T(8,128)S(1)} collective-permute-done((f32[3,256,128]{2,1,0:T(8,128)S(1)}, f32[3,256,128]{2,1,0:T(8,128)S(1)}, u32[]{:S(2)}, u32[]{:S(2)}) %collective-permute-start.5) | collective-permute-done | bytes 393248 | tf_op jit(solution)/shard_map/ppermute | solution.py:298
  19.9 1.9 %collective-permute-start.7 = (f32[3,256,128]{2,1,0:T(8,128)S(1)}, f32[3,256,128]{2,1,0:T(8,128)S(1)}, u32[]{:S(2)}, u32[]{:S(2)}) collective-permute-start(f32[3,256,128]{2,1,0:T(8,128)S(1)} %collective-permute-done.5.refs_3_), channel_id=1, source_target_pairs={{0,2},{2,4},{3,1},{4,6},{5,3},{6,8},{7,5},{8,10},{9,7},{10,12},{11... | collective-permute-start | bytes 1179656 | tf_op jit(solution)/shard_map/ppermute | solution.py:298
  21.8 2.7 %collective-permute-start.3 = (f32[4,128,128]{2,1,0:T(8,128)S(1)}, f32[4,128,128]{2,1,0:T(8,128)S(1)}, u32[]{:S(2)}, u32[]{:S(2)}) collective-permute-start(f32[4,128,128]{2,1,0:T(8,128)S(1)} %copy-done.4), channel_id=1, source_target_pairs={{0,65},{1,64},{2,67},{3,66},{4,69},{5,68},{6,71},{7,70},{8,73},{9,... | collective-permute-start | bytes 786440 | tf_op jit(solution)/shard_map/ppermute | solution.py:298
  24.5 2.1 %collective-permute-start.6 = (f32[2,256,128]{2,1,0:T(8,128)S(1)}, f32[2,256,128]{2,1,0:T(8,128)S(1)}, u32[]{:S(2)}, u32[]{:S(2)}) collective-permute-start(f32[2,256,128]{2,1,0:T(8,128)S(1)} %get-tuple-element.25), channel_id=1, source_target_pairs={{0,1},{1,0},{2,3},{3,2},{4,5},{5,4},{6,7},{7,6},{8,9},{9,8},{10,11... | collective-permute-start | bytes 786440 | tf_op jit(solution)/shard_map/ppermute | solution.py:298
  30.2 4.3 %collective-permute-start.4 = (f32[2,128,128]{2,1,0:T(8,128)S(1)}, f32[2,128,128]{2,1,0:T(8,128)S(1)}, u32[]{:S(2)}, u32[]{:S(2)}) collective-permute-start(f32[2,128,128]{2,1,0:T(8,128)S(1)} %get-tuple-element.22), channel_id=1, source_target_pairs={{1,66},{2,65},{3,68},{4,67},{5,70},{6,69},{7,72},{8,71},{9,74},{10... | collective-permute-start | bytes 393224 | tf_op jit(solution)/shard_map/ppermute | solution.py:298
  34.6 4.7 %collective-permute-done.4.far = f32[2,128,128]{2,1,0:T(8,128)S(1)} collective-permute-done((f32[2,128,128]{2,1,0:T(8,128)S(1)}, f32[2,128,128]{2,1,0:T(8,128)S(1)}, u32[]{:S(2)}, u32[]{:S(2)}) %collective-permute-start.4) | collective-permute-done | bytes 131104 | tf_op jit(solution)/shard_map/ppermute | solution.py:298
  39.3 2.5 %prepare_b.1 = (bf16[12,256,256]{2,1,0:T(8,128)(2,1)S(1)}, f32[144]{0:T(256)S(1)}) custom-call(f32[8,128]{1,0:T(8,128)S(1)} %copy-done.5, s32[2,3]{1,0:T(2,128)S(1)} %copy-done.6, s32[4]{0:T(128)S(1)} %copy-done.7, f32[1,256,128]{2,1,0:T(8,128)S(1)} %slice.12.near, f32[4,128,128]{2,1,0:T(8,128)S(1)} %collective-permute-done.3.group, ...), custom_call_target="tpu_custom_call" | custom-call | flops 100000000 | bytes 2097152 | tf_op jit(solution)/shard_map/prepare_b/pallas_call | solution.py:320
  41.8 8.9 %sweep_b0.1 = (f32[2,512,128]{2,1,0:T(8,128)S(1)}, f32[2,512,128]{2,1,0:T(8,128)S(1)}) custom-call(f32[144]{0:T(256)S(1)} %get-tuple-element.23.refs_0_, bf16[12,256,256]{2,1,0:T(8,128)(2,1)S(1)} %get-tuple-element.24.refs_1_, f32[1024,512]{1,0:T(8,128)S(1)} %copy-done.1, f32[3,256,128]{2,1,0:T(8,128)S(1)} %collective-permute-done.5.refs_3_, ...), custom_call_target="tpu_custom_call" | custom-call | flops 2000000000 | bytes 2097152 | tf_op jit(solution)/shard_map/sweep_b0/pallas_call | solution.py:329
  50.8 9.1 %sweep_b1.1 = (f32[2,512,128]{2,1,0:T(8,128)S(1)}, f32[2,512,128]{2,1,0:T(8,128)S(1)}, f32[3,512,128]{2,1,0:T(8,128)S(1)}, f32[3,512,128]{2,1,0:T(8,128)S(1)}) custom-call(f32[144]{0:T(256)S(1)} %get-tuple-element.23.refs_0_, bf16[12,256,256]{2,1,0:T(8,128)(2,1)S(1)} %get-tuple-element.24.refs_1_, f32[1024,512]{1,0:T(8,128)S(1)} %copy-done.1, ...), custom_call_target="tpu_custom_call" | custom-call | flops 2000000000 | bytes 2097152 | tf_op jit(solution)/shard_map/sweep_b1/pallas_call | solution.py:334
  59.9 1.9 %collective-permute-start.11 = (f32[2,512,128]{2,1,0:T(8,128)S(1)}, f32[2,512,128]{2,1,0:T(8,128)S(1)}, u32[]{:S(2)}, u32[]{:S(2)}) collective-permute-start(f32[2,512,128]{2,1,0:T(8,128)S(1)} %get-tuple-element.30), channel_id=1, source_target_pairs={{0,1},{1,0},{2,3},{3,2},{4,5},{5,4},{6,7},{7,6},{8,9},{9,8},{10,11... | collective-permute-start | bytes 1572872 | tf_op jit(solution)/shard_map/ppermute | solution.py:298
  61.8 3.4 %collective-permute-start.10 = (f32[2,512,128]{2,1,0:T(8,128)S(1)}, f32[2,512,128]{2,1,0:T(8,128)S(1)}, u32[]{:S(2)}, u32[]{:S(2)}) collective-permute-start(f32[2,512,128]{2,1,0:T(8,128)S(1)} %get-tuple-element.28.refs_8_), channel_id=1, source_target_pairs={{0,1},{1,0},{2,3},{3,2},{4,5},{5,4},{6,7},{7,6},{8,9},{9,8},{10,11... | collective-permute-start | bytes 1572872 | tf_op jit(solution)/shard_map/ppermute | solution.py:298
  65.2 9.5 %collective-permute-start.12 = (f32[3,512,128]{2,1,0:T(8,128)S(1)}, f32[3,512,128]{2,1,0:T(8,128)S(1)}, u32[]{:S(2)}, u32[]{:S(2)}) collective-permute-start(f32[3,512,128]{2,1,0:T(8,128)S(1)} %get-tuple-element.31), channel_id=1, source_target_pairs={{1,33},{3,35},{5,37},{7,39},{9,41},{11,43},{13,45},{15,47},{17,49}... | collective-permute-start | bytes 2359304 | tf_op jit(solution)/shard_map/ppermute | solution.py:298
  74.7 2.5 %collective-permute-start.13 = (f32[3,512,128]{2,1,0:T(8,128)S(1)}, f32[3,512,128]{2,1,0:T(8,128)S(1)}, u32[]{:S(2)}, u32[]{:S(2)}) collective-permute-start(f32[3,512,128]{2,1,0:T(8,128)S(1)} %get-tuple-element.32), channel_id=1, source_target_pairs={{33,64},{35,66},{37,68},{39,70},{41,72},{43,74},{45,76},{47,78},{4... | collective-permute-start | bytes 2359304 | tf_op jit(solution)/shard_map/ppermute | solution.py:298
  77.2 5.2 %collective-permute-start.15 = (f32[2,512,128]{2,1,0:T(8,128)S(1)}, f32[2,512,128]{2,1,0:T(8,128)S(1)}, u32[]{:S(2)}, u32[]{:S(2)}) collective-permute-start(f32[2,512,128]{2,1,0:T(8,128)S(1)} %collective-permute-done.11.got_1), channel_id=1, source_target_pairs={{0,32},{2,34},{4,36},{6,38},{8,40},{10,42},{12,44},{14,46},{16,48}... | collective-permute-start | bytes 1572872 | tf_op jit(solution)/shard_map/ppermute | solution.py:298
  82.6 6.7 %collective-permute-start.14 = (f32[2,512,128]{2,1,0:T(8,128)S(1)}, f32[2,512,128]{2,1,0:T(8,128)S(1)}, u32[]{:S(2)}, u32[]{:S(2)}) collective-permute-start(f32[2,512,128]{2,1,0:T(8,128)S(1)} %collective-permute-done.10.got_0), channel_id=1, source_target_pairs={{0,32},{2,34},{4,36},{6,38},{8,40},{10,42},{12,44},{14,46},{16,48}... | collective-permute-start | bytes 1572872 | tf_op jit(solution)/shard_map/ppermute | solution.py:298
  89.3 9.8 %collective-permute-start = (f32[2,128,128]{2,1,0:T(8,128)S(1)}, f32[2,128,128]{2,1,0:T(8,128)S(1)}, u32[]{:S(2)}, u32[]{:S(2)}) collective-permute-start(f32[2,128,128]{2,1,0:T(8,128)S(1)} %get-tuple-element.34), channel_id=1, source_target_pairs={{0,32},{1,33},{2,34},{3,35},{4,36},{5,37},{6,38},{7,39},{8,40},{9,... | collective-permute-start | bytes 393224 | tf_op jit(solution)/shard_map/ppermute | solution.py:298
  99.1 2.3 %collective-permute-done.before = f32[2,128,128]{2,1,0:T(8,128)S(1)} collective-permute-done((f32[2,128,128]{2,1,0:T(8,128)S(1)}, f32[2,128,128]{2,1,0:T(8,128)S(1)}, u32[]{:S(2)}, u32[]{:S(2)}) %collective-permute-start) | collective-permute-done | bytes 131104 | tf_op jit(solution)/shard_map/ppermute | solution.py:298
  101.5 2.8 %collective-permute-start.1 = (f32[2,128,128]{2,1,0:T(8,128)S(1)}, f32[2,128,128]{2,1,0:T(8,128)S(1)}, u32[]{:S(2)}, u32[]{:S(2)}) collective-permute-start(f32[2,128,128]{2,1,0:T(8,128)S(1)} %get-tuple-element.33), channel_id=1, source_target_pairs={{32,0},{33,1},{34,2},{35,3},{36,4},{37,5},{38,6},{39,7},{40,8},{41... | collective-permute-start | bytes 393224 | tf_op jit(solution)/shard_map/ppermute | solution.py:298
  104.3 6.8 %collective-permute-done.1.after = f32[2,128,128]{2,1,0:T(8,128)S(1)} collective-permute-done((f32[2,128,128]{2,1,0:T(8,128)S(1)}, f32[2,128,128]{2,1,0:T(8,128)S(1)}, u32[]{:S(2)}, u32[]{:S(2)}) %collective-permute-start.1) | collective-permute-done | bytes 131104 | tf_op jit(solution)/shard_map/ppermute | solution.py:298
  111.1 2.6 %prepare_a.1 = (bf16[12,256,256]{2,1,0:T(8,128)(2,1)S(1)}, f32[144]{0:T(256)S(1)}) custom-call(f32[8,128]{1,0:T(8,128)S(1)} %copy-done.5, s32[2,3]{1,0:T(2,128)S(1)} %copy-done.6, s32[4]{0:T(128)S(1)} %copy-done.7, f32[8,128,128]{2,1,0:T(8,128)S(1)} %copy-done.2, f32[2,128,128]{2,1,0:T(8,128)S(1)} %collective-permute-done.before, ...), custom_call_target="tpu_custom_call" | custom-call | flops 100000000 | bytes 2097152 | tf_op jit(solution)/shard_map/prepare_a/pallas_call | solution.py:323
  113.7 9.5 %sweep_a.1 = f32[512,1024]{1,0:T(8,128)} custom-call(f32[144]{0:T(256)S(1)} %get-tuple-element.19.coef, bf16[12,256,256]{2,1,0:T(8,128)(2,1)S(1)} %get-tuple-element.20.weights, f32[2,512,128]{2,1,0:T(8,128)S(1)} %get-tuple-element.26.refs_7_.kept_0, f32[2,512,128]{2,1,0:T(8,128)S(1)} %get-tuple-element.29.kept_1, ...), custom_call_target="tpu_custom_call" | custom-call | flops 4000000000 | bytes 2097152 | tf_op jit(solution)/shard_map/sweep_a/pallas_call | solution.py:346
  (33 shorter events, 7.2 us)
Async XLA Ops:
  0.0 1.6 %copy-start = (f32[1024,512]{1,0:T(8,128)S(1)}, f32[1024,512]{1,0:T(8,128)}, u32[]{:S(2)}) copy-start(f32[1024,512]{1,0:T(8,128)} %refs_2_.3) | copy-start | bytes 6291460
  1.6 0.9 copy-start.3
  2.5 19.2 %copy-start.4 = (f32[4,128,128]{2,1,0:T(8,128)S(1)}, f32[4,128,128]{2,1,0:T(8,128)}, u32[]{:S(2)}) copy-start(f32[4,128,128]{2,1,0:T(8,128)} %own.3) | copy-start | bytes 786436
  2.5 36.7 %copy-start.5 = (f32[8,128]{1,0:T(8,128)S(1)}, f32[8,128]{1,0:T(8,128)}, u32[]{:S(2)}) copy-start(f32[8,128]{1,0:T(8,128)} %table.3) | copy-start | bytes 12292
  2.5 36.7 %copy-start.6 = (s32[2,3]{1,0:T(2,128)S(1)}, s32[2,3]{1,0:T(2,128)}, u32[]{:S(2)}) copy-start(s32[2,3]{1,0:T(2,128)} %winds.3) | copy-start | bytes 76
  2.5 36.7 %copy-start.7 = (s32[4]{0:T(128)S(1)}, s32[4]{0:T(128)}, u32[]{:S(2)}) copy-start(s32[4]{0:T(128)} %barriers.3) | copy-start | bytes 52
  3.3 38.5 %copy-start.1 = (f32[1024,512]{1,0:T(8,128)S(1)}, f32[1024,512]{1,0:T(8,128)}, u32[]{:S(2)}) copy-start(f32[1024,512]{1,0:T(8,128)} %refs_2_.3) | copy-start | bytes 6291460
  3.3 26.9 %collective-permute-start.2 = (f32[7,256,128]{2,1,0:T(8,128)S(1)}, f32[7,256,128]{2,1,0:T(8,128)S(1)}, u32[]{:S(2)}, u32[]{:S(2)}) collective-permute-start(f32[7,256,128]{2,1,0:T(8,128)S(1)} %get-tuple-element.21), channel_id=1, source_target_pairs={{1,3},{2,0},{3,5},{4,2},{5,7},{6,4},{7,9},{8,6},{9,11},{10,8},{11,... | collective-permute-start | bytes 2752520 | tf_op jit(solution)/shard_map/ppermute | solution.py:298
  8.3 11.6 %collective-permute-start.5 = (f32[3,256,128]{2,1,0:T(8,128)S(1)}, f32[3,256,128]{2,1,0:T(8,128)S(1)}, u32[]{:S(2)}, u32[]{:S(2)}) collective-permute-start(f32[3,256,128]{2,1,0:T(8,128)S(1)} %pack_first.1), channel_id=1, source_target_pairs={{0,1},{1,0},{2,3},{3,2},{4,5},{5,4},{6,7},{7,6},{8,9},{9,8},{10,11... | collective-permute-start | bytes 1179656 | tf_op jit(solution)/shard_map/ppermute | solution.py:298
  10.2 18.1 %collective-permute-start.8 = (f32[3,256,128]{2,1,0:T(8,128)S(1)}, f32[3,256,128]{2,1,0:T(8,128)S(1)}, u32[]{:S(2)}, u32[]{:S(2)}) collective-permute-start(f32[3,256,128]{2,1,0:T(8,128)S(1)} %get-tuple-element.27), channel_id=1, source_target_pairs={{0,1},{1,0},{2,3},{3,2},{4,5},{5,4},{6,7},{7,6},{8,9},{9,8},{10,11... | collective-permute-start | bytes 1179656 | tf_op jit(solution)/shard_map/ppermute | solution.py:298
  19.9 21.9 %collective-permute-start.7 = (f32[3,256,128]{2,1,0:T(8,128)S(1)}, f32[3,256,128]{2,1,0:T(8,128)S(1)}, u32[]{:S(2)}, u32[]{:S(2)}) collective-permute-start(f32[3,256,128]{2,1,0:T(8,128)S(1)} %collective-permute-done.5.refs_3_), channel_id=1, source_target_pairs={{0,2},{2,4},{3,1},{4,6},{5,3},{6,8},{7,5},{8,10},{9,7},{10,12},{11... | collective-permute-start | bytes 1179656 | tf_op jit(solution)/shard_map/ppermute | solution.py:298
  21.8 17.5 %collective-permute-start.3 = (f32[4,128,128]{2,1,0:T(8,128)S(1)}, f32[4,128,128]{2,1,0:T(8,128)S(1)}, u32[]{:S(2)}, u32[]{:S(2)}) collective-permute-start(f32[4,128,128]{2,1,0:T(8,128)S(1)} %copy-done.4), channel_id=1, source_target_pairs={{0,65},{1,64},{2,67},{3,66},{4,69},{5,68},{6,71},{7,70},{8,73},{9,... | collective-permute-start | bytes 786440 | tf_op jit(solution)/shard_map/ppermute | solution.py:298
  24.5 17.2 %collective-permute-start.6 = (f32[2,256,128]{2,1,0:T(8,128)S(1)}, f32[2,256,128]{2,1,0:T(8,128)S(1)}, u32[]{:S(2)}, u32[]{:S(2)}) collective-permute-start(f32[2,256,128]{2,1,0:T(8,128)S(1)} %get-tuple-element.25), channel_id=1, source_target_pairs={{0,1},{1,0},{2,3},{3,2},{4,5},{5,4},{6,7},{7,6},{8,9},{9,8},{10,11... | collective-permute-start | bytes 786440 | tf_op jit(solution)/shard_map/ppermute | solution.py:298
  28.3 22.4 %collective-permute-start.9 = (f32[3,256,128]{2,1,0:T(8,128)S(1)}, f32[3,256,128]{2,1,0:T(8,128)S(1)}, u32[]{:S(2)}, u32[]{:S(2)}) collective-permute-start(f32[3,256,128]{2,1,0:T(8,128)S(1)} %collective-permute-done.8.refs_3_), channel_id=1, source_target_pairs={{0,2},{2,4},{3,1},{4,6},{5,3},{6,8},{7,5},{8,10},{9,7},{10,12},{11... | collective-permute-start | bytes 1179656 | tf_op jit(solution)/shard_map/ppermute | solution.py:298
  30.2 9.0 %collective-permute-start.4 = (f32[2,128,128]{2,1,0:T(8,128)S(1)}, f32[2,128,128]{2,1,0:T(8,128)S(1)}, u32[]{:S(2)}, u32[]{:S(2)}) collective-permute-start(f32[2,128,128]{2,1,0:T(8,128)S(1)} %get-tuple-element.22), channel_id=1, source_target_pairs={{1,66},{2,65},{3,68},{4,67},{5,70},{6,69},{7,72},{8,71},{9,74},{10... | collective-permute-start | bytes 393224 | tf_op jit(solution)/shard_map/ppermute | solution.py:298
  50.7 38.5 %copy-start.2 = (f32[8,128,128]{2,1,0:T(8,128)S(1)}, f32[8,128,128]{2,1,0:T(8,128)}, u32[]{:S(2)}) copy-start(f32[8,128,128]{2,1,0:T(8,128)} %own.2) | copy-start | bytes 1572868
  59.9 17.3 %collective-permute-start.11 = (f32[2,512,128]{2,1,0:T(8,128)S(1)}, f32[2,512,128]{2,1,0:T(8,128)S(1)}, u32[]{:S(2)}, u32[]{:S(2)}) collective-permute-start(f32[2,512,128]{2,1,0:T(8,128)S(1)} %get-tuple-element.30), channel_id=1, source_target_pairs={{0,1},{1,0},{2,3},{3,2},{4,5},{5,4},{6,7},{7,6},{8,9},{9,8},{10,11... | collective-permute-start | bytes 1572872 | tf_op jit(solution)/shard_map/ppermute | solution.py:298
  61.8 20.8 %collective-permute-start.10 = (f32[2,512,128]{2,1,0:T(8,128)S(1)}, f32[2,512,128]{2,1,0:T(8,128)S(1)}, u32[]{:S(2)}, u32[]{:S(2)}) collective-permute-start(f32[2,512,128]{2,1,0:T(8,128)S(1)} %get-tuple-element.28.refs_8_), channel_id=1, source_target_pairs={{0,1},{1,0},{2,3},{3,2},{4,5},{5,4},{6,7},{7,6},{8,9},{9,8},{10,11... | collective-permute-start | bytes 1572872 | tf_op jit(solution)/shard_map/ppermute | solution.py:298
  65.2 48.5 %collective-permute-start.12 = (f32[3,512,128]{2,1,0:T(8,128)S(1)}, f32[3,512,128]{2,1,0:T(8,128)S(1)}, u32[]{:S(2)}, u32[]{:S(2)}) collective-permute-start(f32[3,512,128]{2,1,0:T(8,128)S(1)} %get-tuple-element.31), channel_id=1, source_target_pairs={{1,33},{3,35},{5,37},{7,39},{9,41},{11,43},{13,45},{15,47},{17,49}... | collective-permute-start | bytes 2359304 | tf_op jit(solution)/shard_map/ppermute | solution.py:298
  74.7 39.0 %collective-permute-start.13 = (f32[3,512,128]{2,1,0:T(8,128)S(1)}, f32[3,512,128]{2,1,0:T(8,128)S(1)}, u32[]{:S(2)}, u32[]{:S(2)}) collective-permute-start(f32[3,512,128]{2,1,0:T(8,128)S(1)} %get-tuple-element.32), channel_id=1, source_target_pairs={{33,64},{35,66},{37,68},{39,70},{41,72},{43,74},{45,76},{47,78},{4... | collective-permute-start | bytes 2359304 | tf_op jit(solution)/shard_map/ppermute | solution.py:298
  77.2 36.5 %collective-permute-start.15 = (f32[2,512,128]{2,1,0:T(8,128)S(1)}, f32[2,512,128]{2,1,0:T(8,128)S(1)}, u32[]{:S(2)}, u32[]{:S(2)}) collective-permute-start(f32[2,512,128]{2,1,0:T(8,128)S(1)} %collective-permute-done.11.got_1), channel_id=1, source_target_pairs={{0,32},{2,34},{4,36},{6,38},{8,40},{10,42},{12,44},{14,46},{16,48}... | collective-permute-start | bytes 1572872 | tf_op jit(solution)/shard_map/ppermute | solution.py:298
  82.6 31.1 %collective-permute-start.14 = (f32[2,512,128]{2,1,0:T(8,128)S(1)}, f32[2,512,128]{2,1,0:T(8,128)S(1)}, u32[]{:S(2)}, u32[]{:S(2)}) collective-permute-start(f32[2,512,128]{2,1,0:T(8,128)S(1)} %collective-permute-done.10.got_0), channel_id=1, source_target_pairs={{0,32},{2,34},{4,36},{6,38},{8,40},{10,42},{12,44},{14,46},{16,48}... | collective-permute-start | bytes 1572872 | tf_op jit(solution)/shard_map/ppermute | solution.py:298
  89.3 12.2 %collective-permute-start = (f32[2,128,128]{2,1,0:T(8,128)S(1)}, f32[2,128,128]{2,1,0:T(8,128)S(1)}, u32[]{:S(2)}, u32[]{:S(2)}) collective-permute-start(f32[2,128,128]{2,1,0:T(8,128)S(1)} %get-tuple-element.34), channel_id=1, source_target_pairs={{0,32},{1,33},{2,34},{3,35},{4,36},{5,37},{6,38},{7,39},{8,40},{9,... | collective-permute-start | bytes 393224 | tf_op jit(solution)/shard_map/ppermute | solution.py:298
  101.5 9.6 %collective-permute-start.1 = (f32[2,128,128]{2,1,0:T(8,128)S(1)}, f32[2,128,128]{2,1,0:T(8,128)S(1)}, u32[]{:S(2)}, u32[]{:S(2)}) collective-permute-start(f32[2,128,128]{2,1,0:T(8,128)S(1)} %get-tuple-element.33), channel_id=1, source_target_pairs={{32,0},{33,1},{34,2},{35,3},{36,4},{37,5},{38,6},{39,7},{40,8},{41... | collective-permute-start | bytes 393224 | tf_op jit(solution)/shard_map/ppermute | solution.py:298

commit v2 on v1

v2 whole, which is shorter than its diff:
```python
import functools
import itertools

import jax
import jax.numpy as jnp
from jax import lax
from jax.experimental import pallas as pl
from jax.experimental.pallas import tpu as pltpu
from jax.sharding import PartitionSpec as P

LAT = 128
LEV = 128
STEPS = 3
SPREAD = 0.15
WINDOW = 14
F32, BF16 = jnp.float32, jnp.bfloat16
COST = 4 * 10**9
AXES = ("row", "col")
ANY = pl.BlockSpec(memory_space=pl.ANY)
SMEM = pl.BlockSpec(memory_space=pltpu.SMEM)
VMEM = pl.BlockSpec(memory_space=pltpu.VMEM)


def pairs(move, x_size, z_size):
    number = lambda x, h, k, z, l: ((x * 2 + h) * 2 + k) * (2 * z_size) + z * 2 + l
    listed = []
    for x, h, k, z, l in itertools.product(range(x_size), range(2), range(2), range(z_size), range(2)):
        to = move(x, h, k, z, l)
        if to is not None and 0 <= to[0] < x_size and 0 <= to[3] < z_size:
            listed.append((number(x, h, k, z, l), number(*to)))
    return listed


def row_shift(x, h, k, by):
    at = (x * 2 + h) * 2 + k + by
    return at // 4, (at // 2) % 2, at % 2


def swap_y(x, h, k, z, l):
    return x, h, k, z, 1 - l


def near_z(x, h, k, z, l):
    return x, h, k, z + (1 if l else -1), l


def far_z(x, h, k, z, l):
    return x, h, k, z + (-1 if l else 1), l


def mats_across(size, x, h, k, z, l):
    tx, th, tk = row_shift(x, h, k, 1 if k else -1)
    return tx % size, th, tk, z, 1 - l


def mats_core(x, h, k, z, l):
    return x, h, 1 - k, z, l


def halo_same(x, h, k, z, l):
    return *row_shift(x, h, k, 1 if l else -1), z, l


def halo_cross(x, h, k, z, l):
    tx, th, tk = row_shift(x, h, k, 1 if l else -1)
    return None if (tx, th) == (x, h) else (tx, th, tk, z, 1 - l)


def halo_flip(x, h, k, z, l):
    return *row_shift(x, h, k, 1 if l else -1), z, 1 - l


def relay_core(x, h, k, z, l):
    return (x, h, 1 - k, z, l) if k == l else None


def side():
    return lax.rem(lax.axis_index("col"), 2)


def turned(l, q, count):
    return jnp.where(l == 1, q, count - 1 - q)


def rows_of(l, chunk):
    return l * 768 if chunk == 0 else 256 + l * 256


def run_copies(copies, sems):
    started = []
    for i, (src, dst) in enumerate(copies):
        copy = pltpu.make_async_copy(src, dst, sems.at[i])
        copy.start()
        started.append(copy)
    for copy in started:
        copy.wait()


def lanes(start):
    return pl.ds(pl.multiple_of(start * LEV, LEV), LEV)


def rows(start, size):
    return pl.ds(pl.multiple_of(start, LEV), size)


def pack_first(cov, out, sems):
    l = side()
    at = rows_of(1 - l, 0)
    copies = [(cov.at[rows(at, 256), lanes(l + i)], out.at[i]) for i in range(3)]
    run_copies(copies + [(cov.at[rows(at, 256), lanes(3 - 3 * l)], out.at[3])], sems)


def pack_rest(cov, mix_a, mix_b, second, near, across, core, sems):
    l = side()
    k = lax.rem(lax.axis_index("row"), 2)
    at = rows_of(1 - l, 1)
    copies = [(mix_b, across.at[pl.ds(0, 4)])]
    copies.append((mix_a.at[pl.ds(6 * k, 2)], across.at[pl.ds(4, 2)]))
    copies.append((mix_a.at[pl.ds(6 - 6 * k, 2)], core))
    copies += [(cov.at[rows(at, 256), lanes(l + i)], second.at[i]) for i in range(3)]
    copies.append((cov.at[rows(at, 256), lanes(3 - 3 * l)], second.at[3]))
    for c in range(2):
        for i in range(3):
            copies.append((cov.at[rows(rows_of(l, c), 256), lanes(l + i)], near.at[3 * c + i]))
    for m in range(2):
        copies.append((mix_b.at[2 * l + m], near.at[6, pl.ds(m * LEV, LEV)]))
    run_copies(copies, sems)


def pack_far(pair, across, out, sems):
    l = side()
    copies = [(pair.at[pl.ds(0, 3)], out.at[pl.ds(0, 3)])]
    for m in range(2):
        copies.append((across.at[2 - 2 * l + m], out.at[3, pl.ds(m * LEV, LEV)]))
    run_copies(copies, sems)


def write_coefficients(l, base, tracer, table, winds, barriers, coef, flow):
    def interface(step, n):
        g = base + n - 3
        inside = (g >= 1) & (g <= LAT - 1)
        c = table[winds[tracer, step], jnp.clip(g, 0, LAT - 1)]
        blocked = barriers[0] == g
        for b in range(1, 4):
            blocked = blocked | (barriers[b] == g)
        c = c * jnp.where(blocked, 0.25, 1.0)
        flow[0, n] = jnp.where(inside, jnp.maximum(c, 0.0) + SPREAD, 0.0)
        flow[1, n] = jnp.where(inside, jnp.maximum(-c, 0.0) + SPREAD, 0.0)

    for step in range(STEPS):
        lax.fori_loop(0, WINDOW + 1, lambda n, _: interface(step, n), None)

        def place(p, _):
            n = turned(l, p, WINDOW)
            below, above = flow[0, n], flow[1, n + 1]
            coef[step * 48 + p] = jnp.where(l == 1, below, above)
            coef[step * 48 + 16 + p] = 1.0 - flow[1, n] - flow[0, n + 1]
            coef[step * 48 + 32 + p] = jnp.where(l == 1, above, below)

        lax.fori_loop(0, WINDOW, place, None)


def write_weight(weights, at, mixer):
    turned_mixer = mixer.T
    high = turned_mixer.astype(BF16)
    low = (turned_mixer - high.astype(F32)).astype(BF16)
    for half in range(2):
        weights[at, half * LEV : (half + 1) * LEV, :LEV] = high
        weights[at, half * LEV : (half + 1) * LEV, LEV:] = low


def prepare_b(table, winds, barriers, across, own, weights, coef, flow):
    l = side()
    base = lax.axis_index("col") // 2 * 8
    write_coefficients(l, base, 1, table, winds, barriers, coef, flow)
    for q in range(4):
        b = turned(l, q, 4)
        write_weight(weights, q, across[b])
        write_weight(weights, 4 + q, own[b])


def prepare_a(table, winds, barriers, own, across, core, weights, ends, coef, flow):
    l = side()
    k = lax.rem(lax.axis_index("row"), 2)
    base = lax.axis_index("row") * 8
    write_coefficients(l, base, 0, table, winds, barriers, coef, flow)
    for q in range(8):
        write_weight(weights, q, own[turned(l, q, 8)])
    for q in range(2):
        m = turned(l, q, 2)
        write_weight(ends, q, jnp.where(k == l, core[m], across[4 + m]))
        write_weight(ends, 2 + q, jnp.where(k == l, across[4 + m], core[m]))


def step_latitude(step, p, source, weights, ends, coef):
    weight = weights[p - 3] if 3 <= p <= 10 else ends[p - 1 if p < 3 else p - 9]
    y = (
        coef[step * 48 + p] * source[p - 1]
        + coef[step * 48 + 16 + p] * source[p]
        + coef[step * 48 + 32 + p] * source[p + 1]
    )
    high = y.astype(BF16)
    low = (y - high.astype(F32)).astype(BF16)
    both = jnp.dot(
        jnp.concatenate([high, low], axis=1), weight, preferred_element_type=F32
    )
    return both[:, :LEV] + both[:, LEV:]


def first_steps(window, other, weights, ends, coef):
    for p in range(1, WINDOW - 1):
        other[p] = step_latitude(0, p, window, weights, ends, coef)
    for p in range(2, WINDOW - 2):
        window[p] = step_latitude(1, p, other, weights, ends, coef)


def sweep_b(chunk, *refs):
    if chunk == 0:
        coef, weights, cov, pair, near, far, kept, sent, ends, window, other, edge, sems = refs
    else:
        (coef, weights, cov, pair, near, far, ends, kept, sent, same, cross, window, other, sems,
         late) = refs
    l = side()
    copies = []
    for q in range(3):
        t = turned(l, q, 3)
        copies.append((near.at[3 * chunk + t], window.at[q]))
        copies.append((pair.at[t], window.at[3 + q]))
        copies.append((far.at[t], window.at[11 + q]))
    copies.append((pair.at[3], window.at[6]))
    for q in range(4):
        copies.append((cov.at[rows(rows_of(l, chunk), 256), lanes(turned(l, q, 4))], window.at[7 + q]))
    if chunk == 0:
        copies += [(near.at[6], edge.at[0]), (far.at[3], edge.at[1])]
    run_copies(copies, sems)
    if chunk == 0:
        for place in range(2):
            for q in range(2):
                m = turned(l, q, 2)
                write_weight(ends, 2 * place + q, edge[place, rows(m * LEV, LEV), :])
    first_steps(window, other, weights, ends, coef)

    def finish(p, target, q):
        z = step_latitude(2, p, window, weights, ends, coef)
        b = turned(l, q, 4)
        for i in range(2):
            u = turned(l, i, 2)
            target[u, rows(b * LEV, LEV), :] = z[i * LEV : (i + 1) * LEV].T

    for q in range(4):
        finish(3 + q, sent, q)
    for q in range(4):
        finish(7 + q, kept, q)
    if chunk == 1:
        run_copies([(kept.at[1], same.at[0]), (sent.at[1], cross.at[0])], late)


def sweep_a(coef, weights, ends, kept_0, kept_1, got_0, got_1, same_0, same_1, cross_0, cross_1, relay, out,
            window, other, sems):
    l = side()
    k = lax.rem(lax.axis_index("row"), 2)
    copies = [(same_1.at[0], window.at[0])] + [(same_0.at[u], window.at[1 + u]) for u in range(2)]
    for u in range(2):
        copies.append((kept_1.at[u], window.at[7 + u]))
        copies.append((kept_0.at[u], window.at[9 + u]))
        copies.append((got_0.at[u], window.at[4 - u]))
        copies.append((got_1.at[u], window.at[6 - u]))
    copies.append((cross_1.at[0], window.at[13]))
    across = [(cross_0.at[u], window.at[12 - u]) for u in range(2)]
    inside = [(relay.at[u], window.at[12 - u]) for u in range(2)]

    @pl.when(k == l)
    def _():
        run_copies(across, sems)

    @pl.when(k != l)
    def _():
        run_copies(inside, sems)

    run_copies(copies, sems)
    first_steps(window, other, weights, ends, coef)

    for p in range(3, WINDOW - 3):
        out[:, lanes(turned(l, p - 3, 8))] = step_latitude(2, p, window, weights, ends, coef)


def call(kernel, outs, in_specs, out_specs, scratch, flops, name):
    return pl.pallas_call(
        kernel,
        out_shape=outs,
        in_specs=in_specs,
        out_specs=out_specs,
        scratch_shapes=scratch,
        compiler_params=pltpu.CompilerParams(vmem_limit_bytes=40 * 1024 * 1024),
        cost_estimate=pl.CostEstimate(flops=flops, bytes_accessed=2**10, transcendentals=0),
        name=name,
    )


def shaped(*dims, dtype=F32):
    return jax.ShapeDtypeStruct(dims, dtype)


def per_device(x_size, z_size, covariance, table, winds, barriers, mix_a, mix_b):
    send = lambda value, move: lax.ppermute(value, AXES, pairs(move, x_size, z_size))
    dma = lambda n: pltpu.SemaphoreType.DMA((n,))

    out_0 = call(pack_first, shaped(4, 256, LEV), [ANY], ANY, [dma(4)], 0, "pack_first")(covariance)
    pair_0 = send(out_0, swap_y)
    covariance, out_0 = lax.optimization_barrier((covariance, out_0))
    pair_0 = send(out_0, swap_y)
    out_1, out_near, out_across, out_core = call(
        pack_rest,
        (shaped(4, 256, LEV), shaped(7, 256, LEV), shaped(6, LEV, LEV), shaped(2, LEV, LEV)),
        [ANY] * 3, (ANY,) * 4, [dma(15)], 0, "pack_rest",
    )(covariance, mix_a, mix_b)
    across = send(out_across, functools.partial(mats_across, x_size))
    near = send(out_near, near_z)
    core = send(out_core, mats_core)
    pair_1 = send(out_1, swap_y)
    across, core = lax.optimization_barrier((across, core))
    out_far = call(pack_far, shaped(4, 256, LEV), [ANY] * 2, ANY, [dma(3)], 0, "pack_far")(pair_0, across)
    far_0 = send(out_far, far_z)
    far_1 = send(pair_1[:3], far_z)

    weight = shaped(8, 256, 256, dtype=BF16)
    ends = shaped(4, 256, 256, dtype=BF16)
    prep_scratch = [pltpu.SMEM((2, 16), F32)]
    weights_b, coef_b = call(
        prepare_b, (weight, shaped(144)), [SMEM] * 3 + [VMEM] * 2, (VMEM, SMEM), prep_scratch, 10**3,
        "prepare_b",
    )(table, winds, barriers, across, mix_b)
    block = shaped(2, 512, LEV)
    field = pltpu.VMEM((WINDOW, 256, LEV), F32)
    kept_0, sent_0, ends_b = call(
        functools.partial(sweep_b, 0), (block, block, ends), [SMEM, VMEM] + [ANY] * 4, (VMEM,) * 3,
        [field, field, pltpu.VMEM((2, 256, LEV), F32), dma(16)], COST, "sweep_b0",
    )(coef_b, weights_b, covariance, pair_0, near, far_0)
    got_0 = send(sent_0, swap_y)
    kept_1, sent_1, same_1, cross_1 = call(
        functools.partial(sweep_b, 1), (block,) * 2 + (shaped(1, 512, LEV),) * 2,
        [SMEM, VMEM] + [ANY] * 4 + [VMEM], (VMEM, VMEM, ANY, ANY),
        [field, field, dma(14), dma(2)], COST, "sweep_b1",
    )(coef_b, weights_b, covariance, pair_1, near, far_1, ends_b)
    kept_0, sent_0, same_1, cross_1, core = lax.optimization_barrier(
        (kept_0, sent_0, same_1, cross_1, core)
    )
    same_0 = send(kept_0, halo_same)
    cross_0 = send(sent_0, halo_cross)
    weights_a, ends_a, coef_a = call(
        prepare_a, (weight, ends, shaped(144)), [SMEM] * 3 + [VMEM] * 3, (VMEM, VMEM, SMEM),
        prep_scratch, 10**3, "prepare_a",
    )(table, winds, barriers, mix_a, across, core)
    sent_1, same_1, cross_1, got_0, weights_a = lax.optimization_barrier(
        (sent_1, same_1, cross_1, got_0, weights_a)
    )
    got_1 = send(sent_1, swap_y)
    same_1 = send(same_1, halo_same)
    cross_1 = send(cross_1, halo_flip)
    relay = send(got_0, relay_core)

    field = pltpu.VMEM((WINDOW, 512, LEV), F32)
    return call(
        sweep_a, shaped(512, 1024), [SMEM, VMEM, VMEM] + [ANY] * 9, VMEM, [field, field, dma(12)],
        4 * 10**3, "sweep_a",
    )(coef_a, weights_a, ends_a, kept_0, kept_1, got_0, got_1, same_0, same_1, cross_0, cross_1, relay)


def solution(mesh):
    placed = (P("row", "col"), P(), P(), P(), P("row", None, None), P("col", None, None))
    return jax.shard_map(
        functools.partial(per_device, mesh.shape["row"] // 4, mesh.shape["col"] // 2),
        mesh=mesh, in_specs=placed, out_specs=P("col", "row"), check_vma=False,
    )
```

time: 124 us -> 90.5 us (0.73)
  the two profiles are of different devices: /device:TPU:249 before, /device:TPU:72 now
where the time goes in v2:
time: 90.5 us; the launch traced here: 90 us
  starting transfers between devices  39.1 us (43%)
  waiting for transfers between devices  28.4 us (31%)
  Pallas kernels  20.5 us (23%)
  local copies, waits for them, and re-layouts  1.65 us (2%)
    ppermute x14, starting transfers between devices, per_device(): lax.ppermute(value, AXES, pairs(move, x_size, z_size))  39.1 us
    ppermute x14, waiting for transfers between devices, per_device(): lax.ppermute(value, AXES, pairs(move, x_size, z_size))  28.4 us
    pallas_call x1, Pallas kernels, per_device(): call(sweep_a, shaped(512, 1024), [SMEM, VMEM, VMEM] + [ANY] * 9, VMEM, [f...  5.18 us
    pallas_call x1, Pallas kernels, per_device(): call(functools.partial(sweep_b, 0), (block, block, ends), [SMEM, VMEM] +...  4.64 us
    pallas_call x1, Pallas kernels, per_device(): call(functools.partial(sweep_b, 1), (block,) * 2 + (shaped(1, 512, LEV),)...  4.22 us
    pallas_call x1, Pallas kernels, per_device(): call(prepare_a, (weight, ends, shaped(144)), [SMEM] * 3 + [VMEM] * 3, (VM...  2.61 us
    pallas_call x1, Pallas kernels, per_device(): call(prepare_b, (weight, shaped(144)), [SMEM] * 3 + [VMEM] * 2, (VMEM, SM...  2.46 us
  transfers between devices with their start and end apart: 14, of which 3 were waited for; matrix products, arithmetic and copies ran while one was open for 0% of the time, Pallas kernels for 17%

profile of v2, /device:TPU:72, one launch (start us, length us, event | category | flops | bytes accessed | tf_op | source)
XLA Modules:
  0.0 90.0 jit_solution(15059535587808621070)
XLA Ops:
  0.0 1.6 %copy-done = f32[1024,512]{1,0:T(8,128)S(1)} copy-done((f32[1024,512]{1,0:T(8,128)S(1)}, f32[1024,512]{1,0:T(8,128)}, u32[]{:S(2)}) %copy-start) | copy-done | bytes 2097176
  1.8 2.5 %collective-permute-start.2 = (f32[4,256,128]{2,1,0:T(8,128)S(1)}, f32[4,256,128]{2,1,0:T(8,128)S(1)}, u32[]{:S(2)}, u32[]{:S(2)}) collective-permute-start(f32[4,256,128]{2,1,0:T(8,128)S(1)} %pack_first.1), channel_id=1, source_target_pairs={{0,1},{1,0},{2,3},{3,2},{4,5},{5,4},{6,7},{7,6},{8,9},{9,8},{10,11... | collective-permute-start | bytes 1572872 | tf_op jit(solution)/shard_map/ppermute | solution.py:306
  4.3 0.9 %pack_rest.1 = (f32[4,256,128]{2,1,0:T(8,128)S(1)}, f32[7,256,128]{2,1,0:T(8,128)S(1)}, f32[6,128,128]{2,1,0:T(8,128)S(1)}, f32[2,128,128]{2,1,0:T(8,128)S(1)}) custom-call(f32[1024,512]{1,0:T(8,128)S(1)} %copy-done, f32[8,128,128]{2,1,0:T(8,128)S(1)} %copy-done.2, f32[4,128,128]{2,1,0:T(8,128)S(1)} %copy-done.3), custom_call_target="tpu_custom_call" | custom-call | bytes 1024 | tf_op jit(solution)/shard_map/pack_rest/pallas_call | solution.py:313
  5.2 5.8 %collective-permute-start = (f32[6,128,128]{2,1,0:T(8,128)S(1)}, f32[6,128,128]{2,1,0:T(8,128)S(1)}, u32[]{:S(2)}, u32[]{:S(2)}) collective-permute-start(f32[6,128,128]{2,1,0:T(8,128)S(1)} %get-tuple-element.36), channel_id=1, source_target_pairs={{0,481},{1,480},{2,483},{3,482},{4,485},{5,484},{6,487},{7,486},{8... | collective-permute-start | bytes 1179656 | tf_op jit(solution)/shard_map/ppermute | solution.py:306
  11.0 3.8 %collective-permute-start.3 = (f32[7,256,128]{2,1,0:T(8,128)S(1)}, f32[7,256,128]{2,1,0:T(8,128)S(1)}, u32[]{:S(2)}, u32[]{:S(2)}) collective-permute-start(f32[7,256,128]{2,1,0:T(8,128)S(1)} %get-tuple-element.42), channel_id=1, source_target_pairs={{1,3},{2,0},{3,5},{4,2},{5,7},{6,4},{7,9},{8,6},{9,11},{10,8},{11,... | collective-permute-start | bytes 2752520 | tf_op jit(solution)/shard_map/ppermute | solution.py:306
  14.8 1.9 %collective-permute-start.1 = (f32[2,128,128]{2,1,0:T(8,128)S(1)}, f32[2,128,128]{2,1,0:T(8,128)S(1)}, u32[]{:S(2)}, u32[]{:S(2)}) collective-permute-start(f32[2,128,128]{2,1,0:T(8,128)S(1)} %get-tuple-element.37), channel_id=1, source_target_pairs={{0,32},{1,33},{2,34},{3,35},{4,36},{5,37},{6,38},{7,39},{8,40},{9,... | collective-permute-start | bytes 393224 | tf_op jit(solution)/shard_map/ppermute | solution.py:306
  16.8 1.9 %collective-permute-start.5 = (f32[4,256,128]{2,1,0:T(8,128)S(1)}, f32[4,256,128]{2,1,0:T(8,128)S(1)}, u32[]{:S(2)}, u32[]{:S(2)}) collective-permute-start(f32[4,256,128]{2,1,0:T(8,128)S(1)} %get-tuple-element.45), channel_id=1, source_target_pairs={{0,1},{1,0},{2,3},{3,2},{4,5},{5,4},{6,7},{7,6},{8,9},{9,8},{10,11... | collective-permute-start | bytes 1572872 | tf_op jit(solution)/shard_map/ppermute | solution.py:306
  19.1 2.0 %collective-permute-start.4 = (f32[4,256,128]{2,1,0:T(8,128)S(1)}, f32[4,256,128]{2,1,0:T(8,128)S(1)}, u32[]{:S(2)}, u32[]{:S(2)}) collective-permute-start(f32[4,256,128]{2,1,0:T(8,128)S(1)} %pack_far.1), channel_id=1, source_target_pairs={{0,2},{2,4},{3,1},{4,6},{5,3},{6,8},{7,5},{8,10},{9,7},{10,12},{11... | collective-permute-start | bytes 1572872 | tf_op jit(solution)/shard_map/ppermute | solution.py:306
  21.2 11.8 %collective-permute-done.5.refs_3_ = f32[4,256,128]{2,1,0:T(8,128)S(1)} collective-permute-done((f32[4,256,128]{2,1,0:T(8,128)S(1)}, f32[4,256,128]{2,1,0:T(8,128)S(1)}, u32[]{:S(2)}, u32[]{:S(2)}) %collective-permute-start.5) | collective-permute-done | bytes 524320 | tf_op jit(solution)/shard_map/ppermute | solution.py:306
  33.0 2.0 %collective-permute-start.6 = (f32[3,256,128]{2,1,0:T(8,128)S(1)}, f32[3,256,128]{2,1,0:T(8,128)S(1)}, u32[]{:S(2)}, u32[]{:S(2)}) collective-permute-start(f32[3,256,128]{2,1,0:T(8,128)S(1)} %slice.4), channel_id=1, source_target_pairs={{0,2},{2,4},{3,1},{4,6},{5,3},{6,8},{7,5},{8,10},{9,7},{10,12},{11... | collective-permute-start | bytes 1179656 | tf_op jit(solution)/shard_map/ppermute | solution.py:306
  35.1 2.5 %prepare_b.1 = (bf16[8,256,256]{2,1,0:T(8,128)(2,1)S(1)}, f32[144]{0:T(256)S(1)}) custom-call(f32[8,128]{1,0:T(8,128)S(1)} %copy-done.4, s32[2,3]{1,0:T(2,128)S(1)} %copy-done.5, s32[4]{0:T(128)S(1)} %copy-done.6, f32[6,128,128]{2,1,0:T(8,128)S(1)} %collective-permute-done.across, f32[4,128,128]{2,1,0:T(8,128)S(1)} %copy-done.3), custom_call_target="tpu_custom_call" | custom-call | flops 1000 | bytes 1024 | tf_op jit(solution)/shard_map/prepare_b/pallas_call | solution.py:330
  37.6 4.6 %sweep_b0.1 = (f32[2,512,128]{2,1,0:T(8,128)S(1)}, f32[2,512,128]{2,1,0:T(8,128)S(1)}, bf16[4,256,256]{2,1,0:T(8,128)(2,1)S(1)}) custom-call(f32[144]{0:T(256)S(1)} %get-tuple-element.39.refs_0_, bf16[8,256,256]{2,1,0:T(8,128)(2,1)S(1)} %get-tuple-element.40.refs_1_, f32[1024,512]{1,0:T(8,128)S(1)} %copy-done.1, ...), custom_call_target="tpu_custom_call" | custom-call | flops 4000000000 | bytes 1024 | tf_op jit(solution)/shard_map/sweep_b0/pallas_call | solution.py:336
  42.2 5.2 %collective-permute-start.7 = (f32[2,512,128]{2,1,0:T(8,128)S(1)}, f32[2,512,128]{2,1,0:T(8,128)S(1)}, u32[]{:S(2)}, u32[]{:S(2)}) collective-permute-start(f32[2,512,128]{2,1,0:T(8,128)S(1)} %get-tuple-element.63), channel_id=1, source_target_pairs={{0,1},{1,0},{2,3},{3,2},{4,5},{5,4},{6,7},{7,6},{8,9},{9,8},{10,11... | collective-permute-start | bytes 1572872 | tf_op jit(solution)/shard_map/ppermute | solution.py:306
  47.5 4.2 %sweep_b1.1 = (f32[2,512,128]{2,1,0:T(8,128)S(1)}, f32[2,512,128]{2,1,0:T(8,128)S(1)}, f32[1,512,128]{2,1,0:T(8,128)S(1)}, f32[1,512,128]{2,1,0:T(8,128)S(1)}) custom-call(f32[144]{0:T(256)S(1)} %get-tuple-element.39.refs_0_, bf16[8,256,256]{2,1,0:T(8,128)(2,1)S(1)} %get-tuple-element.40.refs_1_, f32[1024,512]{1,0:T(8,128)S(1)} %copy-done.1, ...), custom_call_target="tpu_custom_call" | custom-call | flops 4000000000 | bytes 1024 | tf_op jit(solution)/shard_map/sweep_b1/pallas_call | solution.py:341
  51.7 0.7 collective-permute-start.11
  52.4 2.5 %collective-permute-start.9 = (f32[2,512,128]{2,1,0:T(8,128)S(1)}, f32[2,512,128]{2,1,0:T(8,128)S(1)}, u32[]{:S(2)}, u32[]{:S(2)}) collective-permute-start(f32[2,512,128]{2,1,0:T(8,128)S(1)} %get-tuple-element.58.kept_0), channel_id=1, source_target_pairs={{1,33},{3,35},{5,37},{7,39},{9,41},{11,43},{13,45},{15,47},{17,49}... | collective-permute-start | bytes 1572872 | tf_op jit(solution)/shard_map/ppermute | solution.py:306
  54.9 2.6 %prepare_a.1 = (bf16[8,256,256]{2,1,0:T(8,128)(2,1)S(1)}, bf16[4,256,256]{2,1,0:T(8,128)(2,1)S(1)}, f32[144]{0:T(256)S(1)}) custom-call(f32[8,128]{1,0:T(8,128)S(1)} %copy-done.4, s32[2,3]{1,0:T(2,128)S(1)} %copy-done.5, s32[4]{0:T(128)S(1)} %copy-done.6, f32[8,128,128]{2,1,0:T(8,128)S(1)} %copy-done.2, f32[6,128,128]{2,1,0:T(8,128)S(1)} %collective-permute-done.across, ...), custom_call_target="tpu_custom_call" | custom-call | flops 1000 | bytes 1024 | tf_op jit(solution)/shard_map/prepare_a/pallas_call | solution.py:351
  57.5 2.2 %collective-permute-done.7.got_0 = f32[2,512,128]{2,1,0:T(8,128)S(1)} collective-permute-done((f32[2,512,128]{2,1,0:T(8,128)S(1)}, f32[2,512,128]{2,1,0:T(8,128)S(1)}, u32[]{:S(2)}, u32[]{:S(2)}) %collective-permute-start.7) | collective-permute-done | bytes 524320 | tf_op jit(solution)/shard_map/ppermute | solution.py:306
  59.8 4.4 %collective-permute-start.8 = (f32[2,512,128]{2,1,0:T(8,128)S(1)}, f32[2,512,128]{2,1,0:T(8,128)S(1)}, u32[]{:S(2)}, u32[]{:S(2)}) collective-permute-start(f32[2,512,128]{2,1,0:T(8,128)S(1)} %get-tuple-element.61), channel_id=1, source_target_pairs={{0,1},{1,0},{2,3},{3,2},{4,5},{5,4},{6,7},{7,6},{8,9},{9,8},{10,11... | collective-permute-start | bytes 1572872 | tf_op jit(solution)/shard_map/ppermute | solution.py:306
  64.2 1.3 %collective-permute-start.13 = (f32[2,512,128]{2,1,0:T(8,128)S(1)}, f32[2,512,128]{2,1,0:T(8,128)S(1)}, u32[]{:S(2)}, u32[]{:S(2)}) collective-permute-start(f32[2,512,128]{2,1,0:T(8,128)S(1)} %collective-permute-done.7.got_0), channel_id=1, source_target_pairs={{0,32},{2,34},{4,36},{6,38},{8,40},{10,42},{12,44},{14,46},{16,48}... | collective-permute-start | bytes 1572872 | tf_op jit(solution)/shard_map/ppermute | solution.py:306
  65.5 3.1 %collective-permute-start.10 = (f32[1,512,128]{2,1,0:T(8,128)S(1)}, f32[1,512,128]{2,1,0:T(8,128)S(1)}, u32[]{:S(2)}, u32[]{:S(2)}) collective-permute-start(f32[1,512,128]{2,1,0:T(8,128)S(1)} %get-tuple-element.62), channel_id=1, source_target_pairs={{1,33},{3,35},{5,37},{7,39},{9,41},{11,43},{13,45},{15,47},{17,49}... | collective-permute-start | bytes 786440 | tf_op jit(solution)/shard_map/ppermute | solution.py:306
  68.6 1.9 %collective-permute-start.12 = (f32[1,512,128]{2,1,0:T(8,128)S(1)}, f32[1,512,128]{2,1,0:T(8,128)S(1)}, u32[]{:S(2)}, u32[]{:S(2)}) collective-permute-start(f32[1,512,128]{2,1,0:T(8,128)S(1)} %get-tuple-element.64), channel_id=1, source_target_pairs={{1,32},{3,34},{5,36},{7,38},{9,40},{11,42},{13,44},{15,46},{17,48}... | collective-permute-start | bytes 786440 | tf_op jit(solution)/shard_map/ppermute | solution.py:306
  70.5 14.3 %collective-permute-done.12.cross_1 = f32[1,512,128]{2,1,0:T(8,128)S(1)} collective-permute-done((f32[1,512,128]{2,1,0:T(8,128)S(1)}, f32[1,512,128]{2,1,0:T(8,128)S(1)}, u32[]{:S(2)}, u32[]{:S(2)}) %collective-permute-start.12) | collective-permute-done | bytes 262176 | tf_op jit(solution)/shard_map/ppermute | solution.py:306
  84.8 5.2 %sweep_a.1 = f32[512,1024]{1,0:T(8,128)} custom-call(f32[144]{0:T(256)S(1)} %get-tuple-element.51.coef, bf16[8,256,256]{2,1,0:T(8,128)(2,1)S(1)} %get-tuple-element.56.weights, bf16[4,256,256]{2,1,0:T(8,128)(2,1)S(1)} %get-tuple-element.57.ends, f32[2,512,128]{2,1,0:T(8,128)S(1)} %get-tuple-element.58.kept_0, f32[2,512,128]{2,1,0:T(8,128)S(1)} %get-tuple-element.59.kept_1, ...), custom_call_target="tpu_custom_call" | custom-call | flops 4000 | bytes 1024 | tf_op jit(solution)/shard_map/sweep_a/pallas_call | solution.py:364
  (27 shorter events, 0.6 us)
Async XLA Ops:
  0.0 1.6 %copy-start = (f32[1024,512]{1,0:T(8,128)S(1)}, f32[1024,512]{1,0:T(8,128)}, u32[]{:S(2)}) copy-start(f32[1024,512]{1,0:T(8,128)} %refs_2_.1) | copy-start | bytes 6291460
  1.6 2.7 %copy-start.2 = (f32[8,128,128]{2,1,0:T(8,128)S(1)}, f32[8,128,128]{2,1,0:T(8,128)}, u32[]{:S(2)}) copy-start(f32[8,128,128]{2,1,0:T(8,128)} %own.3) | copy-start | bytes 1572868
  1.6 2.7 %copy-start.3 = (f32[4,128,128]{2,1,0:T(8,128)S(1)}, f32[4,128,128]{2,1,0:T(8,128)}, u32[]{:S(2)}) copy-start(f32[4,128,128]{2,1,0:T(8,128)} %own.2) | copy-start | bytes 786436
  1.7 33.3 %copy-start.4 = (f32[8,128]{1,0:T(8,128)S(1)}, f32[8,128]{1,0:T(8,128)}, u32[]{:S(2)}) copy-start(f32[8,128]{1,0:T(8,128)} %table.3) | copy-start | bytes 12292
  1.7 33.3 %copy-start.5 = (s32[2,3]{1,0:T(2,128)S(1)}, s32[2,3]{1,0:T(2,128)}, u32[]{:S(2)}) copy-start(s32[2,3]{1,0:T(2,128)} %winds.3) | copy-start | bytes 76
  1.7 33.3 %copy-start.6 = (s32[4]{0:T(128)S(1)}, s32[4]{0:T(128)}, u32[]{:S(2)}) copy-start(s32[4]{0:T(128)} %barriers.3) | copy-start | bytes 52
  1.8 17.0 %collective-permute-start.2 = (f32[4,256,128]{2,1,0:T(8,128)S(1)}, f32[4,256,128]{2,1,0:T(8,128)S(1)}, u32[]{:S(2)}, u32[]{:S(2)}) collective-permute-start(f32[4,256,128]{2,1,0:T(8,128)S(1)} %pack_first.1), channel_id=1, source_target_pairs={{0,1},{1,0},{2,3},{3,2},{4,5},{5,4},{6,7},{7,6},{8,9},{9,8},{10,11... | collective-permute-start | bytes 1572872 | tf_op jit(solution)/shard_map/ppermute | solution.py:306
  5.2 32.4 %copy-start.1 = (f32[1024,512]{1,0:T(8,128)S(1)}, f32[1024,512]{1,0:T(8,128)}, u32[]{:S(2)}) copy-start(f32[1024,512]{1,0:T(8,128)} %refs_2_.1) | copy-start | bytes 6291460
  5.2 13.5 %collective-permute-start = (f32[6,128,128]{2,1,0:T(8,128)S(1)}, f32[6,128,128]{2,1,0:T(8,128)S(1)}, u32[]{:S(2)}, u32[]{:S(2)}) collective-permute-start(f32[6,128,128]{2,1,0:T(8,128)S(1)} %get-tuple-element.36), channel_id=1, source_target_pairs={{0,481},{1,480},{2,483},{3,482},{4,485},{5,484},{6,487},{7,486},{8... | collective-permute-start | bytes 1179656 | tf_op jit(solution)/shard_map/ppermute | solution.py:306
  11.0 26.5 %collective-permute-start.3 = (f32[7,256,128]{2,1,0:T(8,128)S(1)}, f32[7,256,128]{2,1,0:T(8,128)S(1)}, u32[]{:S(2)}, u32[]{:S(2)}) collective-permute-start(f32[7,256,128]{2,1,0:T(8,128)S(1)} %get-tuple-element.42), channel_id=1, source_target_pairs={{1,3},{2,0},{3,5},{4,2},{5,7},{6,4},{7,9},{8,6},{9,11},{10,8},{11,... | collective-permute-start | bytes 2752520 | tf_op jit(solution)/shard_map/ppermute | solution.py:306
  14.8 3.9 %collective-permute-start.1 = (f32[2,128,128]{2,1,0:T(8,128)S(1)}, f32[2,128,128]{2,1,0:T(8,128)S(1)}, u32[]{:S(2)}, u32[]{:S(2)}) collective-permute-start(f32[2,128,128]{2,1,0:T(8,128)S(1)} %get-tuple-element.37), channel_id=1, source_target_pairs={{0,32},{1,33},{2,34},{3,35},{4,36},{5,37},{6,38},{7,39},{8,40},{9,... | collective-permute-start | bytes 393224 | tf_op jit(solution)/shard_map/ppermute | solution.py:306
  16.8 16.2 %collective-permute-start.5 = (f32[4,256,128]{2,1,0:T(8,128)S(1)}, f32[4,256,128]{2,1,0:T(8,128)S(1)}, u32[]{:S(2)}, u32[]{:S(2)}) collective-permute-start(f32[4,256,128]{2,1,0:T(8,128)S(1)} %get-tuple-element.45), channel_id=1, source_target_pairs={{0,1},{1,0},{2,3},{3,2},{4,5},{5,4},{6,7},{7,6},{8,9},{9,8},{10,11... | collective-permute-start | bytes 1572872 | tf_op jit(solution)/shard_map/ppermute | solution.py:306
  19.1 18.4 %collective-permute-start.4 = (f32[4,256,128]{2,1,0:T(8,128)S(1)}, f32[4,256,128]{2,1,0:T(8,128)S(1)}, u32[]{:S(2)}, u32[]{:S(2)}) collective-permute-start(f32[4,256,128]{2,1,0:T(8,128)S(1)} %pack_far.1), channel_id=1, source_target_pairs={{0,2},{2,4},{3,1},{4,6},{5,3},{6,8},{7,5},{8,10},{9,7},{10,12},{11... | collective-permute-start | bytes 1572872 | tf_op jit(solution)/shard_map/ppermute | solution.py:306
  33.0 14.4 %collective-permute-start.6 = (f32[3,256,128]{2,1,0:T(8,128)S(1)}, f32[3,256,128]{2,1,0:T(8,128)S(1)}, u32[]{:S(2)}, u32[]{:S(2)}) collective-permute-start(f32[3,256,128]{2,1,0:T(8,128)S(1)} %slice.4), channel_id=1, source_target_pairs={{0,2},{2,4},{3,1},{4,6},{5,3},{6,8},{7,5},{8,10},{9,7},{10,12},{11... | collective-permute-start | bytes 1179656 | tf_op jit(solution)/shard_map/ppermute | solution.py:306
  42.2 17.6 %collective-permute-start.7 = (f32[2,512,128]{2,1,0:T(8,128)S(1)}, f32[2,512,128]{2,1,0:T(8,128)S(1)}, u32[]{:S(2)}, u32[]{:S(2)}) collective-permute-start(f32[2,512,128]{2,1,0:T(8,128)S(1)} %get-tuple-element.63), channel_id=1, source_target_pairs={{0,1},{1,0},{2,3},{3,2},{4,5},{5,4},{6,7},{7,6},{8,9},{9,8},{10,11... | collective-permute-start | bytes 1572872 | tf_op jit(solution)/shard_map/ppermute | solution.py:306
  51.7 16.9 %collective-permute-start.11 = (f32[2,512,128]{2,1,0:T(8,128)S(1)}, f32[2,512,128]{2,1,0:T(8,128)S(1)}, u32[]{:S(2)}, u32[]{:S(2)}) collective-permute-start(f32[2,512,128]{2,1,0:T(8,128)S(1)} %get-tuple-element.63), channel_id=1, source_target_pairs={{33,64},{35,66},{37,68},{39,70},{41,72},{43,74},{45,76},{47,78},{4... | collective-permute-start | bytes 1572872 | tf_op jit(solution)/shard_map/ppermute | solution.py:306
  52.4 18.1 %collective-permute-start.9 = (f32[2,512,128]{2,1,0:T(8,128)S(1)}, f32[2,512,128]{2,1,0:T(8,128)S(1)}, u32[]{:S(2)}, u32[]{:S(2)}) collective-permute-start(f32[2,512,128]{2,1,0:T(8,128)S(1)} %get-tuple-element.58.kept_0), channel_id=1, source_target_pairs={{1,33},{3,35},{5,37},{7,39},{9,41},{11,43},{13,45},{15,47},{17,49}... | collective-permute-start | bytes 1572872 | tf_op jit(solution)/shard_map/ppermute | solution.py:306
  59.8 25.0 %collective-permute-start.8 = (f32[2,512,128]{2,1,0:T(8,128)S(1)}, f32[2,512,128]{2,1,0:T(8,128)S(1)}, u32[]{:S(2)}, u32[]{:S(2)}) collective-permute-start(f32[2,512,128]{2,1,0:T(8,128)S(1)} %get-tuple-element.61), channel_id=1, source_target_pairs={{0,1},{1,0},{2,3},{3,2},{4,5},{5,4},{6,7},{7,6},{8,9},{9,8},{10,11... | collective-permute-start | bytes 1572872 | tf_op jit(solution)/shard_map/ppermute | solution.py:306
  64.2 20.6 %collective-permute-start.13 = (f32[2,512,128]{2,1,0:T(8,128)S(1)}, f32[2,512,128]{2,1,0:T(8,128)S(1)}, u32[]{:S(2)}, u32[]{:S(2)}) collective-permute-start(f32[2,512,128]{2,1,0:T(8,128)S(1)} %collective-permute-done.7.got_0), channel_id=1, source_target_pairs={{0,32},{2,34},{4,36},{6,38},{8,40},{10,42},{12,44},{14,46},{16,48}... | collective-permute-start | bytes 1572872 | tf_op jit(solution)/shard_map/ppermute | solution.py:306
  65.5 5.0 %collective-permute-start.10 = (f32[1,512,128]{2,1,0:T(8,128)S(1)}, f32[1,512,128]{2,1,0:T(8,128)S(1)}, u32[]{:S(2)}, u32[]{:S(2)}) collective-permute-start(f32[1,512,128]{2,1,0:T(8,128)S(1)} %get-tuple-element.62), channel_id=1, source_target_pairs={{1,33},{3,35},{5,37},{7,39},{9,41},{11,43},{13,45},{15,47},{17,49}... | collective-permute-start | bytes 786440 | tf_op jit(solution)/shard_map/ppermute | solution.py:306
  68.6 16.2 %collective-permute-start.12 = (f32[1,512,128]{2,1,0:T(8,128)S(1)}, f32[1,512,128]{2,1,0:T(8,128)S(1)}, u32[]{:S(2)}, u32[]{:S(2)}) collective-permute-start(f32[1,512,128]{2,1,0:T(8,128)S(1)} %get-tuple-element.64), channel_id=1, source_target_pairs={{1,32},{3,34},{5,36},{7,38},{9,40},{11,42},{13,44},{15,46},{17,48}... | collective-permute-start | bytes 786440 | tf_op jit(solution)/shard_map/ppermute | solution.py:306

commit v3 on v2

--- a/solution.py
+++ b/solution.py
@@ -48,6 +48,10 @@
     return x, h, k, z + (-1 if l else 1), l
 
 
+def far_direct(x, h, k, z, l):
+    return x, h, k, z + (1 if l else -1), 1 - l
+
+
 def mats_across(size, x, h, k, z, l):
     tx, th, tk = row_shift(x, h, k, 1 if k else -1)
     return tx % size, th, tk, z, 1 - l
@@ -64,10 +68,6 @@
 def halo_cross(x, h, k, z, l):
     tx, th, tk = row_shift(x, h, k, 1 if l else -1)
     return None if (tx, th) == (x, h) else (tx, th, tk, z, 1 - l)
-
-
-def halo_flip(x, h, k, z, l):
-    return *row_shift(x, h, k, 1 if l else -1), z, 1 - l
 
 
 def relay_core(x, h, k, z, l):
@@ -104,22 +104,28 @@
     return pl.ds(pl.multiple_of(start, LEV), size)
 
 
-def pack_first(cov, out, sems):
+def pack_mats(mix_a, mix_b, across, core, sems):
+    k = lax.rem(lax.axis_index("row"), 2)
+    run_copies(
+        [
+            (mix_b, across.at[pl.ds(0, 4)]),
+            (mix_a.at[pl.ds(6 * k, 2)], across.at[pl.ds(4, 2)]),
+            (mix_a.at[pl.ds(6 - 6 * k, 2)], core),
+        ],
+        sems,
+    )
+
+
+def pack_first(cov, first, sems):
     l = side()
     at = rows_of(1 - l, 0)
-    copies = [(cov.at[rows(at, 256), lanes(l + i)], out.at[i]) for i in range(3)]
-    run_copies(copies + [(cov.at[rows(at, 256), lanes(3 - 3 * l)], out.at[3])], sems)
-
-
-def pack_rest(cov, mix_a, mix_b, second, near, across, core, sems):
-    l = side()
-    k = lax.rem(lax.axis_index("row"), 2)
-    at = rows_of(1 - l, 1)
-    copies = [(mix_b, across.at[pl.ds(0, 4)])]
-    copies.append((mix_a.at[pl.ds(6 * k, 2)], across.at[pl.ds(4, 2)]))
-    copies.append((mix_a.at[pl.ds(6 - 6 * k, 2)], core))
-    copies += [(cov.at[rows(at, 256), lanes(l + i)], second.at[i]) for i in range(3)]
-    copies.append((cov.at[rows(at, 256), lanes(3 - 3 * l)], second.at[3]))
+    copies = [(cov.at[rows(at, 256), lanes(l + i)], first.at[i]) for i in range(3)]
+    run_copies(copies + [(cov.at[rows(at, 256), lanes(3 - 3 * l)], first.at[3])], sems)
+
+
+def pack_near(cov, mix_b, near, sems):
+    l = side()
+    copies = []
     for c in range(2):
         for i in range(3):
             copies.append((cov.at[rows(rows_of(l, c), 256), lanes(l + i)], near.at[3 * c + i]))
@@ -128,12 +134,19 @@
     run_copies(copies, sems)
 
 
-def pack_far(pair, across, out, sems):
-    l = side()
-    copies = [(pair.at[pl.ds(0, 3)], out.at[pl.ds(0, 3)])]
-    for m in range(2):
-        copies.append((across.at[2 - 2 * l + m], out.at[3, pl.ds(m * LEV, LEV)]))
-    run_copies(copies, sems)
+def pack_rest(cov, second, third, sems):
+    l = side()
+    at = rows_of(1 - l, 1)
+    copies = []
+    for i in range(3):
+        copies.append((cov.at[rows(at, 256), lanes(l + i)], second.at[i]))
+        copies.append((cov.at[rows(at, 256), lanes(l + i)], third.at[i]))
+    run_copies(copies + [(cov.at[rows(at, 256), lanes(3 - 3 * l)], second.at[3])], sems)
+
+
+def pack_edge(across, out, sems):
+    l = side()
+    run_copies([(across.at[pl.ds(2 - 2 * l, 2)], out)], sems)
 
 
 def write_coefficients(l, base, tracer, table, winds, barriers, coef, flow):
@@ -217,10 +230,10 @@
 
 def sweep_b(chunk, *refs):
     if chunk == 0:
-        coef, weights, cov, pair, near, far, kept, sent, ends, window, other, edge, sems = refs
+        coef, weights, cov, pair, near, far, edge_far, kept, sent, ends, window, other, edge, sems = refs
     else:
-        (coef, weights, cov, pair, near, far, ends, kept, sent, same, cross, window, other, sems,
-         late) = refs
+        (coef, weights, cov, pair, near, far, ends, kept_before, sent_before,
+         kept, sent, same, cross, window, other, sems, late) = refs
     l = side()
     copies = []
     for q in range(3):
@@ -232,13 +245,15 @@
     for q in range(4):
         copies.append((cov.at[rows(rows_of(l, chunk), 256), lanes(turned(l, q, 4))], window.at[7 + q]))
     if chunk == 0:
-        copies += [(near.at[6], edge.at[0]), (far.at[3], edge.at[1])]
+        for m in range(2):
+            copies.append((near.at[6, pl.ds(m * LEV, LEV)], edge.at[m]))
+            copies.append((edge_far.at[m], edge.at[2 + m]))
     run_copies(copies, sems)
     if chunk == 0:
         for place in range(2):
             for q in range(2):
                 m = turned(l, q, 2)
-                write_weight(ends, 2 * place + q, edge[place, rows(m * LEV, LEV), :])
+                write_weight(ends, 2 * place + q, edge[2 * place + m])
     first_steps(window, other, weights, ends, coef)
 
     def finish(p, target, q):
@@ -253,22 +268,29 @@
     for q in range(4):
         finish(7 + q, kept, q)
     if chunk == 1:
-        run_copies([(kept.at[1], same.at[0]), (sent.at[1], cross.at[0])], late)
-
-
-def sweep_a(coef, weights, ends, kept_0, kept_1, got_0, got_1, same_0, same_1, cross_0, cross_1, relay, out,
+        run_copies(
+            [
+                (kept_before, same.at[pl.ds(1, 2)]),
+                (sent_before, cross.at[pl.ds(1, 2)]),
+                (kept.at[1], same.at[0]),
+                (sent.at[1], cross.at[0]),
+            ],
+            late,
+        )
+
+
+def sweep_a(coef, weights, ends, kept_0, kept_1, got_0, got_1, same, cross, relay_0, relay_1, out,
             window, other, sems):
     l = side()
     k = lax.rem(lax.axis_index("row"), 2)
-    copies = [(same_1.at[0], window.at[0])] + [(same_0.at[u], window.at[1 + u]) for u in range(2)]
+    copies = [(same.at[q], window.at[q]) for q in range(3)]
     for u in range(2):
         copies.append((kept_1.at[u], window.at[7 + u]))
         copies.append((kept_0.at[u], window.at[9 + u]))
         copies.append((got_0.at[u], window.at[4 - u]))
         copies.append((got_1.at[u], window.at[6 - u]))
-    copies.append((cross_1.at[0], window.at[13]))
-    across = [(cross_0.at[u], window.at[12 - u]) for u in range(2)]
-    inside = [(relay.at[u], window.at[12 - u]) for u in range(2)]
+    across = [(cross.at[q], window.at[13 - q]) for q in range(3)]
+    inside = [(relay_1.at[0], window.at[13])] + [(relay_0.at[u], window.at[12 - u]) for u in range(2)]
 
     @pl.when(k == l)
     def _():
@@ -283,6 +305,19 @@
 
     for p in range(3, WINDOW - 3):
         out[:, lanes(turned(l, p - 3, 8))] = step_latitude(2, p, window, weights, ends, coef)
+
+
+def pack(kernel, outs, operands, copies, name):
+    return pl.pallas_call(
+        kernel,
+        out_shape=outs,
+        in_specs=[ANY] * operands,
+        out_specs=ANY if isinstance(outs, jax.ShapeDtypeStruct) else (ANY,) * len(outs),
+        scratch_shapes=[pltpu.SemaphoreType.DMA((copies,))],
+        compiler_params=pltpu.CompilerParams(vmem_limit_bytes=40 * 1024 * 1024),
+        cost_estimate=pl.CostEstimate(flops=0, bytes_accessed=2**10, transcendentals=0),
+        name=name,
+    )
 
 
 def call(kernel, outs, in_specs, out_specs, scratch, flops, name):
@@ -306,23 +341,26 @@
     send = lambda value, move: lax.ppermute(value, AXES, pairs(move, x_size, z_size))
     dma = lambda n: pltpu.SemaphoreType.DMA((n,))
 
-    out_0 = call(pack_first, shaped(4, 256, LEV), [ANY], ANY, [dma(4)], 0, "pack_first")(covariance)
+    piece = lambda n: shaped(n, 256, LEV)
+    out_0 = pack(pack_first, piece(4), 1, 4, "pack_first")(covariance)
     pair_0 = send(out_0, swap_y)
-    covariance, out_0 = lax.optimization_barrier((covariance, out_0))
-    pair_0 = send(out_0, swap_y)
-    out_1, out_near, out_across, out_core = call(
-        pack_rest,
-        (shaped(4, 256, LEV), shaped(7, 256, LEV), shaped(6, LEV, LEV), shaped(2, LEV, LEV)),
-        [ANY] * 3, (ANY,) * 4, [dma(15)], 0, "pack_rest",
-    )(covariance, mix_a, mix_b)
+    mix_a, mix_b, out_0 = lax.optimization_barrier((mix_a, mix_b, out_0))
+    out_across, out_core = pack(
+        pack_mats, (shaped(6, LEV, LEV), shaped(2, LEV, LEV)), 2, 3, "pack_mats"
+    )(mix_a, mix_b)
     across = send(out_across, functools.partial(mats_across, x_size))
+    core = send(out_core, mats_core)
+    covariance, out_across = lax.optimization_barrier((covariance, out_across))
+    out_near = pack(pack_near, piece(7), 2, 8, "pack_near")(covariance, mix_b)
     near = send(out_near, near_z)
-    core = send(out_core, mats_core)
+    out_1, out_far_1 = pack(pack_rest, (piece(4), piece(3)), 1, 7, "pack_rest")(covariance)
+    out_1, core = lax.optimization_barrier((out_1, core))
     pair_1 = send(out_1, swap_y)
-    across, core = lax.optimization_barrier((across, core))
-    out_far = call(pack_far, shaped(4, 256, LEV), [ANY] * 2, ANY, [dma(3)], 0, "pack_far")(pair_0, across)
-    far_0 = send(out_far, far_z)
-    far_1 = send(pair_1[:3], far_z)
+    pair_0, across = lax.optimization_barrier((pair_0, across))
+    far_0 = send(pair_0[:3], far_z)
+    edge_far = send(pack(pack_edge, shaped(2, LEV, LEV), 1, 1, "pack_edge")(across), far_z)
+    out_far_1, pair_1 = lax.optimization_barrier((out_far_1, pair_1))
+    far_1 = send(out_far_1, far_direct)
 
     weight = shaped(8, 256, 256, dtype=BF16)
     ends = shaped(4, 256, 256, dtype=BF16)
@@ -331,40 +369,35 @@
         prepare_b, (weight, shaped(144)), [SMEM] * 3 + [VMEM] * 2, (VMEM, SMEM), prep_scratch, 10**3,
         "prepare_b",
     )(table, winds, barriers, across, mix_b)
-    block = shaped(2, 512, LEV)
-    field = pltpu.VMEM((WINDOW, 256, LEV), F32)
-    kept_0, sent_0, ends_b = call(
-        functools.partial(sweep_b, 0), (block, block, ends), [SMEM, VMEM] + [ANY] * 4, (VMEM,) * 3,
-        [field, field, pltpu.VMEM((2, 256, LEV), F32), dma(16)], COST, "sweep_b0",
-    )(coef_b, weights_b, covariance, pair_0, near, far_0)
-    got_0 = send(sent_0, swap_y)
-    kept_1, sent_1, same_1, cross_1 = call(
-        functools.partial(sweep_b, 1), (block,) * 2 + (shaped(1, 512, LEV),) * 2,
-        [SMEM, VMEM] + [ANY] * 4 + [VMEM], (VMEM, VMEM, ANY, ANY),
-        [field, field, dma(14), dma(2)], COST, "sweep_b1",
-    )(coef_b, weights_b, covariance, pair_1, near, far_1, ends_b)
-    kept_0, sent_0, same_1, cross_1, core = lax.optimization_barrier(
-        (kept_0, sent_0, same_1, cross_1, core)
-    )
-    same_0 = send(kept_0, halo_same)
-    cross_0 = send(sent_0, halo_cross)
     weights_a, ends_a, coef_a = call(
         prepare_a, (weight, ends, shaped(144)), [SMEM] * 3 + [VMEM] * 3, (VMEM, VMEM, SMEM),
         prep_scratch, 10**3, "prepare_a",
     )(table, winds, barriers, mix_a, across, core)
-    sent_1, same_1, cross_1, got_0, weights_a = lax.optimization_barrier(
-        (sent_1, same_1, cross_1, got_0, weights_a)
-    )
+    weights_b, weights_a, far_0, pair_1 = lax.optimization_barrier((weights_b, weights_a, far_0, pair_1))
+    block = shaped(2, 512, LEV)
+    field = pltpu.VMEM((WINDOW, 256, LEV), F32)
+    kept_0, sent_0, ends_b = call(
+        functools.partial(sweep_b, 0), (block, block, ends), [SMEM, VMEM] + [ANY] * 5, (VMEM,) * 3,
+        [field, field, pltpu.VMEM((4, LEV, LEV), F32), dma(18)], COST, "sweep_b0",
+    )(coef_b, weights_b, covariance, pair_0, near, far_0, edge_far)
+    got_0 = send(sent_0, swap_y)
+    kept_1, sent_1, out_same, out_cross = call(
+        functools.partial(sweep_b, 1), (block,) * 2 + (shaped(3, 512, LEV),) * 2,
+        [SMEM, VMEM] + [ANY] * 4 + [VMEM] + [ANY] * 2, (VMEM, VMEM, ANY, ANY),
+        [field, field, dma(14), dma(4)], COST, "sweep_b1",
+    )(coef_b, weights_b, covariance, pair_1, near, far_1, ends_b, kept_0, sent_0)
     got_1 = send(sent_1, swap_y)
-    same_1 = send(same_1, halo_same)
-    cross_1 = send(cross_1, halo_flip)
-    relay = send(got_0, relay_core)
+    out_same, got_0 = lax.optimization_barrier((out_same, got_0))
+    same = send(out_same, halo_same)
+    cross = send(out_cross, halo_cross)
+    relay_0 = send(got_0, relay_core)
+    relay_1 = send(got_1[1:], relay_core)
 
     field = pltpu.VMEM((WINDOW, 512, LEV), F32)
     return call(
-        sweep_a, shaped(512, 1024), [SMEM, VMEM, VMEM] + [ANY] * 9, VMEM, [field, field, dma(12)],
+        sweep_a, shaped(512, 1024), [SMEM, VMEM, VMEM] + [ANY] * 8, VMEM, [field, field, dma(11)],
         4 * 10**3, "sweep_a",
-    )(coef_a, weights_a, ends_a, kept_0, kept_1, got_0, got_1, same_0, same_1, cross_0, cross_1, relay)
+    )(coef_a, weights_a, ends_a, kept_0, kept_1, got_0, got_1, same, cross, relay_0, relay_1)
 
 
 def solution(mesh):

time: 90.5 us -> 91.7 us (1.013)
  the two profiles are of different devices: /device:TPU:72 before, /device:TPU:105 now
where the time goes in v3:
time: 91.7 us; the launch traced here: 91.2 us
  starting transfers between devices  43 us (47%)
  waiting for transfers between devices  24.7 us (27%)
  Pallas kernels  20.5 us (22%)
  local copies, waits for them, and re-layouts  2.7 us (3%)
    ppermute x14, starting transfers between devices, per_device(): lax.ppermute(value, AXES, pairs(move, x_size, z_size))  43 us
    ppermute x14, waiting for transfers between devices, per_device(): lax.ppermute(value, AXES, pairs(move, x_size, z_size))  24.7 us
    pallas_call x1, Pallas kernels, per_device(): call(sweep_a, shaped(512, 1024), [SMEM, VMEM, VMEM] + [ANY] * 8, VMEM, [f...  5.17 us
    pallas_call x1, Pallas kernels, per_device(): call(functools.partial(sweep_b, 0), (block, block, ends), [SMEM, VMEM] +...  4.66 us
    pallas_call x1, Pallas kernels, per_device(): call(functools.partial(sweep_b, 1), (block,) * 2 + (shaped(3, 512, LEV),)...  4.31 us
    unnamed x16, local copies, waits for them, and re-layouts  2.66 us
    pallas_call x1, Pallas kernels, per_device(): call(prepare_a, (weight, ends, shaped(144)), [SMEM] * 3 + [VMEM] * 3, (VM...  2.61 us
    pallas_call x1, Pallas kernels, per_device(): call(prepare_b, (weight, shaped(144)), [SMEM] * 3 + [VMEM] * 2, (VMEM, SM...  2.46 us
  transfers between devices with their start and end apart: 14, of which 7 were waited for; matrix products, arithmetic and copies ran while one was open for 0% of the time, Pallas kernels for 17%

profile of v3, /device:TPU:105, one launch (start us, length us, event | category | flops | bytes accessed | tf_op | source)
XLA Modules:
  0.0 91.2 jit_solution(561108873884866573)
XLA Ops:
  0.0 1.6 %copy-done = f32[1024,512]{1,0:T(8,128)S(1)} copy-done((f32[1024,512]{1,0:T(8,128)S(1)}, f32[1024,512]{1,0:T(8,128)}, u32[]{:S(2)}) %copy-start) | copy-done | bytes 2097176
  1.7 2.2 %collective-permute-start = (f32[4,256,128]{2,1,0:T(8,128)S(1)}, f32[4,256,128]{2,1,0:T(8,128)S(1)}, u32[]{:S(2)}, u32[]{:S(2)}) collective-permute-start(f32[4,256,128]{2,1,0:T(8,128)S(1)} %pack_first.1), channel_id=1, source_target_pairs={{0,1},{1,0},{2,3},{3,2},{4,5},{5,4},{6,7},{7,6},{8,9},{9,8},{10,11... | collective-permute-start | bytes 1572872 | tf_op jit(solution)/shard_map/ppermute | solution.py:341
  5.8 4.9 %collective-permute-start.5 = (f32[7,256,128]{2,1,0:T(8,128)S(1)}, f32[7,256,128]{2,1,0:T(8,128)S(1)}, u32[]{:S(2)}, u32[]{:S(2)}) collective-permute-start(f32[7,256,128]{2,1,0:T(8,128)S(1)} %pack_near.1), channel_id=1, source_target_pairs={{1,3},{2,0},{3,5},{4,2},{5,7},{6,4},{7,9},{8,6},{9,11},{10,8},{11,... | collective-permute-start | bytes 2752520 | tf_op jit(solution)/shard_map/ppermute | solution.py:341
  10.7 2.1 %collective-permute-start.1 = (f32[6,128,128]{2,1,0:T(8,128)S(1)}, f32[6,128,128]{2,1,0:T(8,128)S(1)}, u32[]{:S(2)}, u32[]{:S(2)}) collective-permute-start(f32[6,128,128]{2,1,0:T(8,128)S(1)} %get-tuple-element.38), channel_id=1, source_target_pairs={{0,481},{1,480},{2,483},{3,482},{4,485},{5,484},{6,487},{7,486},{8... | collective-permute-start | bytes 1179656 | tf_op jit(solution)/shard_map/ppermute | solution.py:341
  12.9 3.6 %collective-permute-start.2 = (f32[2,128,128]{2,1,0:T(8,128)S(1)}, f32[2,128,128]{2,1,0:T(8,128)S(1)}, u32[]{:S(2)}, u32[]{:S(2)}) collective-permute-start(f32[2,128,128]{2,1,0:T(8,128)S(1)} %get-tuple-element.42), channel_id=1, source_target_pairs={{0,32},{1,33},{2,34},{3,35},{4,36},{5,37},{6,38},{7,39},{8,40},{9,... | collective-permute-start | bytes 393224 | tf_op jit(solution)/shard_map/ppermute | solution.py:341
  17.4 5.8 %collective-permute-start.4 = (f32[4,256,128]{2,1,0:T(8,128)S(1)}, f32[4,256,128]{2,1,0:T(8,128)S(1)}, u32[]{:S(2)}, u32[]{:S(2)}) collective-permute-start(f32[4,256,128]{2,1,0:T(8,128)S(1)} %get-tuple-element.49), channel_id=1, source_target_pairs={{0,1},{1,0},{2,3},{3,2},{4,5},{5,4},{6,7},{7,6},{8,9},{9,8},{10,11... | collective-permute-start | bytes 1572872 | tf_op jit(solution)/shard_map/ppermute | solution.py:341
  24.4 1.9 %collective-permute-start.3 = (f32[3,256,128]{2,1,0:T(8,128)S(1)}, f32[3,256,128]{2,1,0:T(8,128)S(1)}, u32[]{:S(2)}, u32[]{:S(2)}) collective-permute-start(f32[3,256,128]{2,1,0:T(8,128)S(1)} %slice.6), channel_id=1, source_target_pairs={{0,2},{2,4},{3,1},{4,6},{5,3},{6,8},{7,5},{8,10},{9,7},{10,12},{11... | collective-permute-start | bytes 1179656 | tf_op jit(solution)/shard_map/ppermute | solution.py:341
  26.5 1.9 %collective-permute-start.6 = (f32[2,128,128]{2,1,0:T(8,128)S(1)}, f32[2,128,128]{2,1,0:T(8,128)S(1)}, u32[]{:S(2)}, u32[]{:S(2)}) collective-permute-start(f32[2,128,128]{2,1,0:T(8,128)S(1)} %pack_edge.1), channel_id=1, source_target_pairs={{0,2},{2,4},{3,1},{4,6},{5,3},{6,8},{7,5},{8,10},{9,7},{10,12},{11... | collective-permute-start | bytes 393224 | tf_op jit(solution)/shard_map/ppermute | solution.py:341
  28.5 2.5 %prepare_b.1 = (bf16[8,256,256]{2,1,0:T(8,128)(2,1)S(1)}, f32[144]{0:T(256)S(1)}) custom-call(f32[8,128]{1,0:T(8,128)S(1)} %copy-done.5, s32[2,3]{1,0:T(2,128)S(1)} %copy-done.6, s32[4]{0:T(128)S(1)} %copy-done.7, f32[6,128,128]{2,1,0:T(8,128)S(1)} %collective-permute-done.1.across, f32[4,128,128]{2,1,0:T(8,128)S(1)} %copy-done.2), custom_call_target="tpu_custom_call" | custom-call | flops 1000 | bytes 1024 | tf_op jit(solution)/shard_map/prepare_b/pallas_call | solution.py:368
  30.9 2.6 %prepare_a.1 = (bf16[8,256,256]{2,1,0:T(8,128)(2,1)S(1)}, bf16[4,256,256]{2,1,0:T(8,128)(2,1)S(1)}, f32[144]{0:T(256)S(1)}) custom-call(f32[8,128]{1,0:T(8,128)S(1)} %copy-done.5, s32[2,3]{1,0:T(2,128)S(1)} %copy-done.6, s32[4]{0:T(128)S(1)} %copy-done.7, f32[8,128,128]{2,1,0:T(8,128)S(1)} %copy-done.4, f32[6,128,128]{2,1,0:T(8,128)S(1)} %collective-permute-done.1.across, ...), custom_call_target="tpu_custom_call" | custom-call | flops 1000 | bytes 1024 | tf_op jit(solution)/shard_map/prepare_a/pallas_call | solution.py:372
  33.6 1.7 %collective-permute-done.4.refs_3_ = f32[4,256,128]{2,1,0:T(8,128)S(1)} collective-permute-done((f32[4,256,128]{2,1,0:T(8,128)S(1)}, f32[4,256,128]{2,1,0:T(8,128)S(1)}, u32[]{:S(2)}, u32[]{:S(2)}) %collective-permute-start.4) | collective-permute-done | bytes 524320 | tf_op jit(solution)/shard_map/ppermute | solution.py:341
  35.2 7.2 %collective-permute-start.7 = (f32[3,256,128]{2,1,0:T(8,128)S(1)}, f32[3,256,128]{2,1,0:T(8,128)S(1)}, u32[]{:S(2)}, u32[]{:S(2)}) collective-permute-start(f32[3,256,128]{2,1,0:T(8,128)S(1)} %get-tuple-element.58), channel_id=1, source_target_pairs={{1,2},{2,1},{3,4},{4,3},{5,6},{6,5},{7,8},{8,7},{9,10},{10,9},{11,... | collective-permute-start | bytes 1179656 | tf_op jit(solution)/shard_map/ppermute | solution.py:341
  42.4 4.7 %sweep_b0.1 = (f32[2,512,128]{2,1,0:T(8,128)S(1)}, f32[2,512,128]{2,1,0:T(8,128)S(1)}, bf16[4,256,256]{2,1,0:T(8,128)(2,1)S(1)}) custom-call(f32[144]{0:T(256)S(1)} %get-tuple-element.53.refs_0_, bf16[8,256,256]{2,1,0:T(8,128)(2,1)S(1)} %get-tuple-element.54.refs_1_, f32[1024,512]{1,0:T(8,128)S(1)} %copy-done.1, ...), custom_call_target="tpu_custom_call" | custom-call | flops 4000000000 | bytes 1024 | tf_op jit(solution)/shard_map/sweep_b0/pallas_call | solution.py:379
  47.1 1.9 %collective-permute-start.8 = (f32[2,512,128]{2,1,0:T(8,128)S(1)}, f32[2,512,128]{2,1,0:T(8,128)S(1)}, u32[]{:S(2)}, u32[]{:S(2)}) collective-permute-start(f32[2,512,128]{2,1,0:T(8,128)S(1)} %get-tuple-element.60.refs_8_), channel_id=1, source_target_pairs={{0,1},{1,0},{2,3},{3,2},{4,5},{5,4},{6,7},{7,6},{8,9},{9,8},{10,11... | collective-permute-start | bytes 1572872 | tf_op jit(solution)/shard_map/ppermute | solution.py:341
  49.0 2.4 %collective-permute-done.7.refs_5_ = f32[3,256,128]{2,1,0:T(8,128)S(1)} collective-permute-done((f32[3,256,128]{2,1,0:T(8,128)S(1)}, f32[3,256,128]{2,1,0:T(8,128)S(1)}, u32[]{:S(2)}, u32[]{:S(2)}) %collective-permute-start.7) | collective-permute-done | bytes 393248 | tf_op jit(solution)/shard_map/ppermute | solution.py:341
  51.4 4.3 %sweep_b1.1 = (f32[2,512,128]{2,1,0:T(8,128)S(1)}, f32[2,512,128]{2,1,0:T(8,128)S(1)}, f32[3,512,128]{2,1,0:T(8,128)S(1)}, f32[3,512,128]{2,1,0:T(8,128)S(1)}) custom-call(f32[144]{0:T(256)S(1)} %get-tuple-element.53.refs_0_, bf16[8,256,256]{2,1,0:T(8,128)(2,1)S(1)} %get-tuple-element.54.refs_1_, f32[1024,512]{1,0:T(8,128)S(1)} %copy-done.1, ...), custom_call_target="tpu_custom_call" | custom-call | flops 4000000000 | bytes 1024 | tf_op jit(solution)/shard_map/sweep_b1/pallas_call | solution.py:384
  55.7 2.2 %collective-permute-start.9 = (f32[2,512,128]{2,1,0:T(8,128)S(1)}, f32[2,512,128]{2,1,0:T(8,128)S(1)}, u32[]{:S(2)}, u32[]{:S(2)}) collective-permute-start(f32[2,512,128]{2,1,0:T(8,128)S(1)} %get-tuple-element.64), channel_id=1, source_target_pairs={{0,1},{1,0},{2,3},{3,2},{4,5},{5,4},{6,7},{7,6},{8,9},{9,8},{10,11... | collective-permute-start | bytes 1572872 | tf_op jit(solution)/shard_map/ppermute | solution.py:341
  57.9 1.9 %collective-permute-start.11 = (f32[3,512,128]{2,1,0:T(8,128)S(1)}, f32[3,512,128]{2,1,0:T(8,128)S(1)}, u32[]{:S(2)}, u32[]{:S(2)}) collective-permute-start(f32[3,512,128]{2,1,0:T(8,128)S(1)} %get-tuple-element.66), channel_id=1, source_target_pairs={{33,64},{35,66},{37,68},{39,70},{41,72},{43,74},{45,76},{47,78},{4... | collective-permute-start | bytes 2359304 | tf_op jit(solution)/shard_map/ppermute | solution.py:341
  59.8 3.1 %collective-permute-done.8.got_0 = f32[2,512,128]{2,1,0:T(8,128)S(1)} collective-permute-done((f32[2,512,128]{2,1,0:T(8,128)S(1)}, f32[2,512,128]{2,1,0:T(8,128)S(1)}, u32[]{:S(2)}, u32[]{:S(2)}) %collective-permute-start.8) | collective-permute-done | bytes 524320 | tf_op jit(solution)/shard_map/ppermute | solution.py:341
  62.9 3.7 %collective-permute-start.10 = (f32[3,512,128]{2,1,0:T(8,128)S(1)}, f32[3,512,128]{2,1,0:T(8,128)S(1)}, u32[]{:S(2)}, u32[]{:S(2)}) collective-permute-start(f32[3,512,128]{2,1,0:T(8,128)S(1)} %get-tuple-element.65), channel_id=1, source_target_pairs={{1,33},{3,35},{5,37},{7,39},{9,41},{11,43},{13,45},{15,47},{17,49}... | collective-permute-start | bytes 2359304 | tf_op jit(solution)/shard_map/ppermute | solution.py:341
  66.6 1.3 %collective-permute-start.12 = (f32[2,512,128]{2,1,0:T(8,128)S(1)}, f32[2,512,128]{2,1,0:T(8,128)S(1)}, u32[]{:S(2)}, u32[]{:S(2)}) collective-permute-start(f32[2,512,128]{2,1,0:T(8,128)S(1)} %collective-permute-done.8.got_0), channel_id=1, source_target_pairs={{0,32},{2,34},{4,36},{6,38},{8,40},{10,42},{12,44},{14,46},{16,48}... | collective-permute-start | bytes 1572872 | tf_op jit(solution)/shard_map/ppermute | solution.py:341
  68.0 14.6 %collective-permute-done.9.got_1 = f32[2,512,128]{2,1,0:T(8,128)S(1)} collective-permute-done((f32[2,512,128]{2,1,0:T(8,128)S(1)}, f32[2,512,128]{2,1,0:T(8,128)S(1)}, u32[]{:S(2)}, u32[]{:S(2)}) %collective-permute-start.9) | collective-permute-done | bytes 524320 | tf_op jit(solution)/shard_map/ppermute | solution.py:341
  82.6 2.3 %collective-permute-start.13 = (f32[1,512,128]{2,1,0:T(8,128)S(1)}, f32[1,512,128]{2,1,0:T(8,128)S(1)}, u32[]{:S(2)}, u32[]{:S(2)}) collective-permute-start(f32[1,512,128]{2,1,0:T(8,128)S(1)} %slice.8), channel_id=1, source_target_pairs={{0,32},{2,34},{4,36},{6,38},{8,40},{10,42},{12,44},{14,46},{16,48}... | collective-permute-start | bytes 786440 | tf_op jit(solution)/shard_map/ppermute | solution.py:341
  86.0 5.2 %sweep_a.1 = f32[512,1024]{1,0:T(8,128)} custom-call(f32[144]{0:T(256)S(1)} %get-tuple-element.44.coef, bf16[8,256,256]{2,1,0:T(8,128)(2,1)S(1)} %get-tuple-element.51.weights, bf16[4,256,256]{2,1,0:T(8,128)(2,1)S(1)} %get-tuple-element.52.ends, f32[2,512,128]{2,1,0:T(8,128)S(1)} %get-tuple-element.56.refs_7_.kept_0, ...), custom_call_target="tpu_custom_call" | custom-call | flops 4000 | bytes 1024 | tf_op jit(solution)/shard_map/sweep_a/pallas_call | solution.py:397
  (32 shorter events, 5.4 us)
Async XLA Ops:
  0.0 1.6 %copy-start = (f32[1024,512]{1,0:T(8,128)S(1)}, f32[1024,512]{1,0:T(8,128)}, u32[]{:S(2)}) copy-start(f32[1024,512]{1,0:T(8,128)} %refs_2_.1) | copy-start | bytes 6291460
  1.6 2.3 %copy-start.2 = (f32[4,128,128]{2,1,0:T(8,128)S(1)}, f32[4,128,128]{2,1,0:T(8,128)}, u32[]{:S(2)}) copy-start(f32[4,128,128]{2,1,0:T(8,128)} %mix_b.1) | copy-start | bytes 786436
  1.6 3.8 %copy-start.1 = (f32[1024,512]{1,0:T(8,128)S(1)}, f32[1024,512]{1,0:T(8,128)}, u32[]{:S(2)}) copy-start(f32[1024,512]{1,0:T(8,128)} %refs_2_.1) | copy-start | bytes 6291460
  1.7 22.6 %collective-permute-start = (f32[4,256,128]{2,1,0:T(8,128)S(1)}, f32[4,256,128]{2,1,0:T(8,128)S(1)}, u32[]{:S(2)}, u32[]{:S(2)}) collective-permute-start(f32[4,256,128]{2,1,0:T(8,128)S(1)} %pack_first.1), channel_id=1, source_target_pairs={{0,1},{1,0},{2,3},{3,2},{4,5},{5,4},{6,7},{7,6},{8,9},{9,8},{10,11... | collective-permute-start | bytes 1572872 | tf_op jit(solution)/shard_map/ppermute | solution.py:341
  3.9 1.0 %copy-start.3 = (f32[8,128,128]{2,1,0:T(8,128)S(1)}, f32[8,128,128]{2,1,0:T(8,128)}, u32[]{:S(2)}) copy-start(f32[8,128,128]{2,1,0:T(8,128)} %own) | copy-start | bytes 1572868
  5.8 22.6 %copy-start.5 = (f32[8,128]{1,0:T(8,128)S(1)}, f32[8,128]{1,0:T(8,128)}, u32[]{:S(2)}) copy-start(f32[8,128]{1,0:T(8,128)} %table.3) | copy-start | bytes 12292
  5.8 22.6 %copy-start.6 = (s32[2,3]{1,0:T(2,128)S(1)}, s32[2,3]{1,0:T(2,128)}, u32[]{:S(2)}) copy-start(s32[2,3]{1,0:T(2,128)} %winds.3) | copy-start | bytes 76
  5.8 22.6 %copy-start.7 = (s32[4]{0:T(128)S(1)}, s32[4]{0:T(128)}, u32[]{:S(2)}) copy-start(s32[4]{0:T(128)} %barriers.3) | copy-start | bytes 52
  5.8 25.1 %copy-start.4 = (f32[8,128,128]{2,1,0:T(8,128)S(1)}, f32[8,128,128]{2,1,0:T(8,128)}, u32[]{:S(2)}) copy-start(f32[8,128,128]{2,1,0:T(8,128)} %own) | copy-start | bytes 1572868
  5.8 36.6 %collective-permute-start.5 = (f32[7,256,128]{2,1,0:T(8,128)S(1)}, f32[7,256,128]{2,1,0:T(8,128)S(1)}, u32[]{:S(2)}, u32[]{:S(2)}) collective-permute-start(f32[7,256,128]{2,1,0:T(8,128)S(1)} %pack_near.1), channel_id=1, source_target_pairs={{1,3},{2,0},{3,5},{4,2},{5,7},{6,4},{7,9},{8,6},{9,11},{10,8},{11,... | collective-permute-start | bytes 2752520 | tf_op jit(solution)/shard_map/ppermute | solution.py:341
  10.7 13.6 %collective-permute-start.1 = (f32[6,128,128]{2,1,0:T(8,128)S(1)}, f32[6,128,128]{2,1,0:T(8,128)S(1)}, u32[]{:S(2)}, u32[]{:S(2)}) collective-permute-start(f32[6,128,128]{2,1,0:T(8,128)S(1)} %get-tuple-element.38), channel_id=1, source_target_pairs={{0,481},{1,480},{2,483},{3,482},{4,485},{5,484},{6,487},{7,486},{8... | collective-permute-start | bytes 1179656 | tf_op jit(solution)/shard_map/ppermute | solution.py:341
  12.9 4.5 %collective-permute-start.2 = (f32[2,128,128]{2,1,0:T(8,128)S(1)}, f32[2,128,128]{2,1,0:T(8,128)S(1)}, u32[]{:S(2)}, u32[]{:S(2)}) collective-permute-start(f32[2,128,128]{2,1,0:T(8,128)S(1)} %get-tuple-element.42), channel_id=1, source_target_pairs={{0,32},{1,33},{2,34},{3,35},{4,36},{5,37},{6,38},{7,39},{8,40},{9,... | collective-permute-start | bytes 393224 | tf_op jit(solution)/shard_map/ppermute | solution.py:341
  17.4 17.8 %collective-permute-start.4 = (f32[4,256,128]{2,1,0:T(8,128)S(1)}, f32[4,256,128]{2,1,0:T(8,128)S(1)}, u32[]{:S(2)}, u32[]{:S(2)}) collective-permute-start(f32[4,256,128]{2,1,0:T(8,128)S(1)} %get-tuple-element.49), channel_id=1, source_target_pairs={{0,1},{1,0},{2,3},{3,2},{4,5},{5,4},{6,7},{7,6},{8,9},{9,8},{10,11... | collective-permute-start | bytes 1572872 | tf_op jit(solution)/shard_map/ppermute | solution.py:341
  24.4 18.0 %collective-permute-start.3 = (f32[3,256,128]{2,1,0:T(8,128)S(1)}, f32[3,256,128]{2,1,0:T(8,128)S(1)}, u32[]{:S(2)}, u32[]{:S(2)}) collective-permute-start(f32[3,256,128]{2,1,0:T(8,128)S(1)} %slice.6), channel_id=1, source_target_pairs={{0,2},{2,4},{3,1},{4,6},{5,3},{6,8},{7,5},{8,10},{9,7},{10,12},{11... | collective-permute-start | bytes 1179656 | tf_op jit(solution)/shard_map/ppermute | solution.py:341
  26.5 15.9 %collective-permute-start.6 = (f32[2,128,128]{2,1,0:T(8,128)S(1)}, f32[2,128,128]{2,1,0:T(8,128)S(1)}, u32[]{:S(2)}, u32[]{:S(2)}) collective-permute-start(f32[2,128,128]{2,1,0:T(8,128)S(1)} %pack_edge.1), channel_id=1, source_target_pairs={{0,2},{2,4},{3,1},{4,6},{5,3},{6,8},{7,5},{8,10},{9,7},{10,12},{11... | collective-permute-start | bytes 393224 | tf_op jit(solution)/shard_map/ppermute | solution.py:341
  35.2 16.2 %collective-permute-start.7 = (f32[3,256,128]{2,1,0:T(8,128)S(1)}, f32[3,256,128]{2,1,0:T(8,128)S(1)}, u32[]{:S(2)}, u32[]{:S(2)}) collective-permute-start(f32[3,256,128]{2,1,0:T(8,128)S(1)} %get-tuple-element.58), channel_id=1, source_target_pairs={{1,2},{2,1},{3,4},{4,3},{5,6},{6,5},{7,8},{8,7},{9,10},{10,9},{11,... | collective-permute-start | bytes 1179656 | tf_op jit(solution)/shard_map/ppermute | solution.py:341
  47.1 15.8 %collective-permute-start.8 = (f32[2,512,128]{2,1,0:T(8,128)S(1)}, f32[2,512,128]{2,1,0:T(8,128)S(1)}, u32[]{:S(2)}, u32[]{:S(2)}) collective-permute-start(f32[2,512,128]{2,1,0:T(8,128)S(1)} %get-tuple-element.60.refs_8_), channel_id=1, source_target_pairs={{0,1},{1,0},{2,3},{3,2},{4,5},{5,4},{6,7},{7,6},{8,9},{9,8},{10,11... | collective-permute-start | bytes 1572872 | tf_op jit(solution)/shard_map/ppermute | solution.py:341
  55.7 26.8 %collective-permute-start.9 = (f32[2,512,128]{2,1,0:T(8,128)S(1)}, f32[2,512,128]{2,1,0:T(8,128)S(1)}, u32[]{:S(2)}, u32[]{:S(2)}) collective-permute-start(f32[2,512,128]{2,1,0:T(8,128)S(1)} %get-tuple-element.64), channel_id=1, source_target_pairs={{0,1},{1,0},{2,3},{3,2},{4,5},{5,4},{6,7},{7,6},{8,9},{9,8},{10,11... | collective-permute-start | bytes 1572872 | tf_op jit(solution)/shard_map/ppermute | solution.py:341
  57.9 28.1 %collective-permute-start.11 = (f32[3,512,128]{2,1,0:T(8,128)S(1)}, f32[3,512,128]{2,1,0:T(8,128)S(1)}, u32[]{:S(2)}, u32[]{:S(2)}) collective-permute-start(f32[3,512,128]{2,1,0:T(8,128)S(1)} %get-tuple-element.66), channel_id=1, source_target_pairs={{33,64},{35,66},{37,68},{39,70},{41,72},{43,74},{45,76},{47,78},{4... | collective-permute-start | bytes 2359304 | tf_op jit(solution)/shard_map/ppermute | solution.py:341
  62.9 23.1 %collective-permute-start.10 = (f32[3,512,128]{2,1,0:T(8,128)S(1)}, f32[3,512,128]{2,1,0:T(8,128)S(1)}, u32[]{:S(2)}, u32[]{:S(2)}) collective-permute-start(f32[3,512,128]{2,1,0:T(8,128)S(1)} %get-tuple-element.65), channel_id=1, source_target_pairs={{1,33},{3,35},{5,37},{7,39},{9,41},{11,43},{13,45},{15,47},{17,49}... | collective-permute-start | bytes 2359304 | tf_op jit(solution)/shard_map/ppermute | solution.py:341
  66.6 19.4 %collective-permute-start.12 = (f32[2,512,128]{2,1,0:T(8,128)S(1)}, f32[2,512,128]{2,1,0:T(8,128)S(1)}, u32[]{:S(2)}, u32[]{:S(2)}) collective-permute-start(f32[2,512,128]{2,1,0:T(8,128)S(1)} %collective-permute-done.8.got_0), channel_id=1, source_target_pairs={{0,32},{2,34},{4,36},{6,38},{8,40},{10,42},{12,44},{14,46},{16,48}... | collective-permute-start | bytes 1572872 | tf_op jit(solution)/shard_map/ppermute | solution.py:341
  82.6 3.5 %collective-permute-start.13 = (f32[1,512,128]{2,1,0:T(8,128)S(1)}, f32[1,512,128]{2,1,0:T(8,128)S(1)}, u32[]{:S(2)}, u32[]{:S(2)}) collective-permute-start(f32[1,512,128]{2,1,0:T(8,128)S(1)} %slice.8), channel_id=1, source_target_pairs={{0,32},{2,34},{4,36},{6,38},{8,40},{10,42},{12,44},{14,46},{16,48}... | collective-permute-start | bytes 786440 | tf_op jit(solution)/shard_map/ppermute | solution.py:341

commit v4 on v3

--- a/solution.py
+++ b/solution.py
@@ -104,18 +104,6 @@
     return pl.ds(pl.multiple_of(start, LEV), size)
 
 
-def pack_mats(mix_a, mix_b, across, core, sems):
-    k = lax.rem(lax.axis_index("row"), 2)
-    run_copies(
-        [
-            (mix_b, across.at[pl.ds(0, 4)]),
-            (mix_a.at[pl.ds(6 * k, 2)], across.at[pl.ds(4, 2)]),
-            (mix_a.at[pl.ds(6 - 6 * k, 2)], core),
-        ],
-        sems,
-    )
-
-
 def pack_first(cov, first, sems):
     l = side()
     at = rows_of(1 - l, 0)
@@ -123,9 +111,14 @@
     run_copies(copies + [(cov.at[rows(at, 256), lanes(3 - 3 * l)], first.at[3])], sems)
 
 
-def pack_near(cov, mix_b, near, sems):
-    l = side()
-    copies = []
+def pack_second(cov, mix_a, mix_b, across, near, core, sems):
+    l = side()
+    k = lax.rem(lax.axis_index("row"), 2)
+    copies = [
+        (mix_b, across.at[pl.ds(0, 4)]),
+        (mix_a.at[pl.ds(6 * k, 2)], across.at[pl.ds(4, 2)]),
+        (mix_a.at[pl.ds(6 - 6 * k, 2)], core),
+    ]
     for c in range(2):
         for i in range(3):
             copies.append((cov.at[rows(rows_of(l, c), 256), lanes(l + i)], near.at[3 * c + i]))
@@ -144,9 +137,12 @@
     run_copies(copies + [(cov.at[rows(at, 256), lanes(3 - 3 * l)], second.at[3])], sems)
 
 
-def pack_edge(across, out, sems):
-    l = side()
-    run_copies([(across.at[pl.ds(2 - 2 * l, 2)], out)], sems)
+def pack_far(pair, across, out, sems):
+    l = side()
+    copies = [(pair.at[pl.ds(0, 3)], out.at[pl.ds(0, 3)])]
+    for m in range(2):
+        copies.append((across.at[2 - 2 * l + m], out.at[3, pl.ds(m * LEV, LEV)]))
+    run_copies(copies, sems)
 
 
 def write_coefficients(l, base, tracer, table, winds, barriers, coef, flow):
@@ -230,7 +226,7 @@
 
 def sweep_b(chunk, *refs):
     if chunk == 0:
-        coef, weights, cov, pair, near, far, edge_far, kept, sent, ends, window, other, edge, sems = refs
+        coef, weights, cov, pair, near, far, kept, sent, ends, window, other, edge, sems = refs
     else:
         (coef, weights, cov, pair, near, far, ends, kept_before, sent_before,
          kept, sent, same, cross, window, other, sems, late) = refs
@@ -247,7 +243,7 @@
     if chunk == 0:
         for m in range(2):
             copies.append((near.at[6, pl.ds(m * LEV, LEV)], edge.at[m]))
-            copies.append((edge_far.at[m], edge.at[2 + m]))
+            copies.append((far.at[3, pl.ds(m * LEV, LEV)], edge.at[2 + m]))
     run_copies(copies, sems)
     if chunk == 0:
         for place in range(2):
@@ -344,21 +340,17 @@
     piece = lambda n: shaped(n, 256, LEV)
     out_0 = pack(pack_first, piece(4), 1, 4, "pack_first")(covariance)
     pair_0 = send(out_0, swap_y)
-    mix_a, mix_b, out_0 = lax.optimization_barrier((mix_a, mix_b, out_0))
-    out_across, out_core = pack(
-        pack_mats, (shaped(6, LEV, LEV), shaped(2, LEV, LEV)), 2, 3, "pack_mats"
-    )(mix_a, mix_b)
+    covariance, mix_a, mix_b, out_0 = lax.optimization_barrier((covariance, mix_a, mix_b, out_0))
+    out_across, out_near, out_core = pack(
+        pack_second, (shaped(6, LEV, LEV), piece(7), shaped(2, LEV, LEV)), 3, 11, "pack_second"
+    )(covariance, mix_a, mix_b)
     across = send(out_across, functools.partial(mats_across, x_size))
-    core = send(out_core, mats_core)
+    near = send(out_near, near_z)
     covariance, out_across = lax.optimization_barrier((covariance, out_across))
-    out_near = pack(pack_near, piece(7), 2, 8, "pack_near")(covariance, mix_b)
-    near = send(out_near, near_z)
     out_1, out_far_1 = pack(pack_rest, (piece(4), piece(3)), 1, 7, "pack_rest")(covariance)
-    out_1, core = lax.optimization_barrier((out_1, core))
     pair_1 = send(out_1, swap_y)
-    pair_0, across = lax.optimization_barrier((pair_0, across))
-    far_0 = send(pair_0[:3], far_z)
-    edge_far = send(pack(pack_edge, shaped(2, LEV, LEV), 1, 1, "pack_edge")(across), far_z)
+    out_far_0 = pack(pack_far, piece(4), 2, 3, "pack_far")(pair_0, across)
+    far_0 = send(out_far_0, far_z)
     out_far_1, pair_1 = lax.optimization_barrier((out_far_1, pair_1))
     far_1 = send(out_far_1, far_direct)
 
@@ -369,27 +361,29 @@
         prepare_b, (weight, shaped(144)), [SMEM] * 3 + [VMEM] * 2, (VMEM, SMEM), prep_scratch, 10**3,
         "prepare_b",
     )(table, winds, barriers, across, mix_b)
+    weights_b, far_0, pair_1 = lax.optimization_barrier((weights_b, far_0, pair_1))
+    block = shaped(2, 512, LEV)
+    field = pltpu.VMEM((WINDOW, 256, LEV), F32)
+    kept_0, sent_0, ends_b = call(
+        functools.partial(sweep_b, 0), (block, block, ends), [SMEM, VMEM] + [ANY] * 4, (VMEM,) * 3,
+        [field, field, pltpu.VMEM((4, LEV, LEV), F32), dma(18)], COST, "sweep_b0",
+    )(coef_b, weights_b, covariance, pair_0, near, far_0)
+    got_0 = send(sent_0, swap_y)
+    kept_1, sent_1, out_same, out_cross = call(
+        functools.partial(sweep_b, 1), (block, block, shaped(3, 512, LEV), shaped(3, 512, LEV)),
+        [SMEM, VMEM] + [ANY] * 4 + [VMEM, ANY, ANY], (VMEM, VMEM, ANY, ANY),
+        [field, field, dma(14), dma(4)], COST, "sweep_b1",
+    )(coef_b, weights_b, covariance, pair_1, near, far_1, ends_b, kept_0, sent_0)
+    got_1 = send(sent_1, swap_y)
+    cross = send(out_cross, halo_cross)
+    out_same, out_core, got_0 = lax.optimization_barrier((out_same, out_core, got_0))
+    same = send(out_same, halo_same)
+    core = send(out_core, mats_core)
     weights_a, ends_a, coef_a = call(
         prepare_a, (weight, ends, shaped(144)), [SMEM] * 3 + [VMEM] * 3, (VMEM, VMEM, SMEM),
         prep_scratch, 10**3, "prepare_a",
     )(table, winds, barriers, mix_a, across, core)
-    weights_b, weights_a, far_0, pair_1 = lax.optimization_barrier((weights_b, weights_a, far_0, pair_1))
-    block = shaped(2, 512, LEV)
-    field = pltpu.VMEM((WINDOW, 256, LEV), F32)
-    kept_0, sent_0, ends_b = call(
-        functools.partial(sweep_b, 0), (block, block, ends), [SMEM, VMEM] + [ANY] * 5, (VMEM,) * 3,
-        [field, field, pltpu.VMEM((4, LEV, LEV), F32), dma(18)], COST, "sweep_b0",
-    )(coef_b, weights_b, covariance, pair_0, near, far_0, edge_far)
-    got_0 = send(sent_0, swap_y)
-    kept_1, sent_1, out_same, out_cross = call(
-        functools.partial(sweep_b, 1), (block,) * 2 + (shaped(3, 512, LEV),) * 2,
-        [SMEM, VMEM] + [ANY] * 4 + [VMEM] + [ANY] * 2, (VMEM, VMEM, ANY, ANY),
-        [field, field, dma(14), dma(4)], COST, "sweep_b1",
-    )(coef_b, weights_b, covariance, pair_1, near, far_1, ends_b, kept_0, sent_0)
-    got_1 = send(sent_1, swap_y)
-    out_same, got_0 = lax.optimization_barrier((out_same, got_0))
-    same = send(out_same, halo_same)
-    cross = send(out_cross, halo_cross)
+    got_0, weights_a = lax.optimization_barrier((got_0, weights_a))
     relay_0 = send(got_0, relay_core)
     relay_1 = send(got_1[1:], relay_core)
 

time: 91.7 us -> 85.7 us (0.935)
  waiting for transfers between devices: 24.7 us -> 13.8 us
  starting transfers between devices: 43 us -> 49.1 us
  local copies, waits for them, and re-layouts: 2.7 us -> 1.64 us
    ppermute x14 -> x13, waiting for transfers between devices: 24.7 us -> 13.8 us  [per_device(): lax.ppermute(value, AXES, pairs(move, x_size, z_size))]
    ppermute x14 -> x13, starting transfers between devices: 43 us -> 49.1 us  [per_device(): lax.ppermute(value, AXES, pairs(move, x_size, z_size))]
    unnamed x16 -> x14, local copies, waits for them, and re-layouts: 2.66 us -> 1.62 us
    pallas_call x4 -> x3, Pallas kernels: 5.27 us -> 5.35 us  [the longest x1 4.19 us: per_device(): call(functools.partial(sweep_b, 1), (block, block, shaped(3, 512, LEV), s...]
  transfers between devices with their start and end apart: 14 -> 13, of which waited for: 7 -> 5; matrix products, arithmetic and copies ran while one was open for 0% -> 0% of each run, Pallas kernels for 17% -> 18%
where the time goes in v4:
time: 85.7 us; the launch traced here: 85.2 us
  starting transfers between devices  49.1 us (57%)
  Pallas kernels  20.5 us (24%)
  waiting for transfers between devices  13.8 us (16%)
  local copies, waits for them, and re-layouts  1.64 us (2%)
    ppermute x13, starting transfers between devices, per_device(): lax.ppermute(value, AXES, pairs(move, x_size, z_size))  49.1 us
    ppermute x13, waiting for transfers between devices, per_device(): lax.ppermute(value, AXES, pairs(move, x_size, z_size))  13.8 us
    pallas_call x1, Pallas kernels, per_device(): call(sweep_a, shaped(512, 1024), [SMEM, VMEM, VMEM] + [ANY] * 8, VMEM, [f...  5.17 us
    pallas_call x1, Pallas kernels, per_device(): call(functools.partial(sweep_b, 0), (block, block, ends), [SMEM, VMEM] +...  4.54 us
    pallas_call x1, Pallas kernels, per_device(): call(functools.partial(sweep_b, 1), (block, block, shaped(3, 512, LEV), s...  4.19 us
    pallas_call x1, Pallas kernels, per_device(): call(prepare_a, (weight, ends, shaped(144)), [SMEM] * 3 + [VMEM] * 3, (VM...  2.61 us
    pallas_call x1, Pallas kernels, per_device(): call(prepare_b, (weight, shaped(144)), [SMEM] * 3 + [VMEM] * 2, (VMEM, SM...  2.46 us
  transfers between devices with their start and end apart: 13, of which 5 were waited for; matrix products, arithmetic and copies ran while one was open for 0% of the time, Pallas kernels for 18%

profile of v4, /device:TPU:105, one launch (start us, length us, event | category | flops | bytes accessed | tf_op | source)
XLA Modules:
  0.0 85.2 jit_solution(5834302098277510635)
XLA Ops:
  0.0 1.6 %copy-done = f32[1024,512]{1,0:T(8,128)S(1)} copy-done((f32[1024,512]{1,0:T(8,128)S(1)}, f32[1024,512]{1,0:T(8,128)}, u32[]{:S(2)}) %copy-start) | copy-done | bytes 2097176
  1.7 2.2 %collective-permute-start.1 = (f32[4,256,128]{2,1,0:T(8,128)S(1)}, f32[4,256,128]{2,1,0:T(8,128)S(1)}, u32[]{:S(2)}, u32[]{:S(2)}) collective-permute-start(f32[4,256,128]{2,1,0:T(8,128)S(1)} %pack_first.1), channel_id=1, source_target_pairs={{0,1},{1,0},{2,3},{3,2},{4,5},{5,4},{6,7},{7,6},{8,9},{9,8},{10,11... | collective-permute-start | bytes 1572872 | tf_op jit(solution)/shard_map/ppermute | solution.py:337
  4.8 5.0 %collective-permute-start = (f32[6,128,128]{2,1,0:T(8,128)S(1)}, f32[6,128,128]{2,1,0:T(8,128)S(1)}, u32[]{:S(2)}, u32[]{:S(2)}) collective-permute-start(f32[6,128,128]{2,1,0:T(8,128)S(1)} %get-tuple-element.39), channel_id=1, source_target_pairs={{0,481},{1,480},{2,483},{3,482},{4,485},{5,484},{6,487},{7,486},{8... | collective-permute-start | bytes 1179656 | tf_op jit(solution)/shard_map/ppermute | solution.py:337
  9.8 4.9 %collective-permute-start.4 = (f32[7,256,128]{2,1,0:T(8,128)S(1)}, f32[7,256,128]{2,1,0:T(8,128)S(1)}, u32[]{:S(2)}, u32[]{:S(2)}) collective-permute-start(f32[7,256,128]{2,1,0:T(8,128)S(1)} %get-tuple-element.48), channel_id=1, source_target_pairs={{1,3},{2,0},{3,5},{4,2},{5,7},{6,4},{7,9},{8,6},{9,11},{10,8},{11,... | collective-permute-start | bytes 2752520 | tf_op jit(solution)/shard_map/ppermute | solution.py:337
  14.9 1.9 %collective-permute-start.3 = (f32[4,256,128]{2,1,0:T(8,128)S(1)}, f32[4,256,128]{2,1,0:T(8,128)S(1)}, u32[]{:S(2)}, u32[]{:S(2)}) collective-permute-start(f32[4,256,128]{2,1,0:T(8,128)S(1)} %get-tuple-element.44), channel_id=1, source_target_pairs={{0,1},{1,0},{2,3},{3,2},{4,5},{5,4},{6,7},{7,6},{8,9},{9,8},{10,11... | collective-permute-start | bytes 1572872 | tf_op jit(solution)/shard_map/ppermute | solution.py:337
  16.9 2.9 %collective-permute-done.across = f32[6,128,128]{2,1,0:T(8,128)S(1)} collective-permute-done((f32[6,128,128]{2,1,0:T(8,128)S(1)}, f32[6,128,128]{2,1,0:T(8,128)S(1)}, u32[]{:S(2)}, u32[]{:S(2)}) %collective-permute-start) | collective-permute-done | bytes 393248 | tf_op jit(solution)/shard_map/ppermute | solution.py:337
  20.1 1.9 %collective-permute-start.2 = (f32[4,256,128]{2,1,0:T(8,128)S(1)}, f32[4,256,128]{2,1,0:T(8,128)S(1)}, u32[]{:S(2)}, u32[]{:S(2)}) collective-permute-start(f32[4,256,128]{2,1,0:T(8,128)S(1)} %pack_far.1), channel_id=1, source_target_pairs={{0,2},{2,4},{3,1},{4,6},{5,3},{6,8},{7,5},{8,10},{9,7},{10,12},{11... | collective-permute-start | bytes 1572872 | tf_op jit(solution)/shard_map/ppermute | solution.py:337
  22.1 2.5 %prepare_b.1 = (bf16[8,256,256]{2,1,0:T(8,128)(2,1)S(1)}, f32[144]{0:T(256)S(1)}) custom-call(f32[8,128]{1,0:T(8,128)S(1)} %copy-done.4, s32[2,3]{1,0:T(2,128)S(1)} %copy-done.5, s32[4]{0:T(128)S(1)} %copy-done.6, f32[6,128,128]{2,1,0:T(8,128)S(1)} %collective-permute-done.across, f32[4,128,128]{2,1,0:T(8,128)S(1)} %copy-done.3), custom_call_target="tpu_custom_call" | custom-call | flops 1000 | bytes 1024 | tf_op jit(solution)/shard_map/prepare_b/pallas_call | solution.py:360
  24.6 3.6 %collective-permute-done.3.refs_3_ = f32[4,256,128]{2,1,0:T(8,128)S(1)} collective-permute-done((f32[4,256,128]{2,1,0:T(8,128)S(1)}, f32[4,256,128]{2,1,0:T(8,128)S(1)}, u32[]{:S(2)}, u32[]{:S(2)}) %collective-permute-start.3) | collective-permute-done | bytes 524320 | tf_op jit(solution)/shard_map/ppermute | solution.py:337
  28.2 3.5 %collective-permute-start.5 = (f32[3,256,128]{2,1,0:T(8,128)S(1)}, f32[3,256,128]{2,1,0:T(8,128)S(1)}, u32[]{:S(2)}, u32[]{:S(2)}) collective-permute-start(f32[3,256,128]{2,1,0:T(8,128)S(1)} %get-tuple-element.49), channel_id=1, source_target_pairs={{1,2},{2,1},{3,4},{4,3},{5,6},{6,5},{7,8},{8,7},{9,10},{10,9},{11,... | collective-permute-start | bytes 1179656 | tf_op jit(solution)/shard_map/ppermute | solution.py:337
  31.8 4.8 %collective-permute-done.2.refs_5_ = f32[4,256,128]{2,1,0:T(8,128)S(1)} collective-permute-done((f32[4,256,128]{2,1,0:T(8,128)S(1)}, f32[4,256,128]{2,1,0:T(8,128)S(1)}, u32[]{:S(2)}, u32[]{:S(2)}) %collective-permute-start.2) | collective-permute-done | bytes 524320 | tf_op jit(solution)/shard_map/ppermute | solution.py:337
  36.5 4.5 %sweep_b0.1 = (f32[2,512,128]{2,1,0:T(8,128)S(1)}, f32[2,512,128]{2,1,0:T(8,128)S(1)}, bf16[4,256,256]{2,1,0:T(8,128)(2,1)S(1)}) custom-call(f32[144]{0:T(256)S(1)} %get-tuple-element.40.refs_0_, bf16[8,256,256]{2,1,0:T(8,128)(2,1)S(1)} %get-tuple-element.46.refs_1_, f32[1024,512]{1,0:T(8,128)S(1)} %copy-done.1, ...), custom_call_target="tpu_custom_call" | custom-call | flops 4000000000 | bytes 1024 | tf_op jit(solution)/shard_map/sweep_b0/pallas_call | solution.py:367
  41.1 2.5 %collective-permute-start.6 = (f32[2,512,128]{2,1,0:T(8,128)S(1)}, f32[2,512,128]{2,1,0:T(8,128)S(1)}, u32[]{:S(2)}, u32[]{:S(2)}) collective-permute-start(f32[2,512,128]{2,1,0:T(8,128)S(1)} %get-tuple-element.53.refs_8_), channel_id=1, source_target_pairs={{0,1},{1,0},{2,3},{3,2},{4,5},{5,4},{6,7},{7,6},{8,9},{9,8},{10,11... | collective-permute-start | bytes 1572872 | tf_op jit(solution)/shard_map/ppermute | solution.py:337
  43.6 4.2 %sweep_b1.1 = (f32[2,512,128]{2,1,0:T(8,128)S(1)}, f32[2,512,128]{2,1,0:T(8,128)S(1)}, f32[3,512,128]{2,1,0:T(8,128)S(1)}, f32[3,512,128]{2,1,0:T(8,128)S(1)}) custom-call(f32[144]{0:T(256)S(1)} %get-tuple-element.40.refs_0_, bf16[8,256,256]{2,1,0:T(8,128)(2,1)S(1)} %get-tuple-element.46.refs_1_, f32[1024,512]{1,0:T(8,128)S(1)} %copy-done.1, ...), custom_call_target="tpu_custom_call" | custom-call | flops 4000000000 | bytes 1024 | tf_op jit(solution)/shard_map/sweep_b1/pallas_call | solution.py:372
  47.8 2.8 %collective-permute-start.8 = (f32[2,512,128]{2,1,0:T(8,128)S(1)}, f32[2,512,128]{2,1,0:T(8,128)S(1)}, u32[]{:S(2)}, u32[]{:S(2)}) collective-permute-start(f32[2,512,128]{2,1,0:T(8,128)S(1)} %get-tuple-element.64), channel_id=1, source_target_pairs={{0,1},{1,0},{2,3},{3,2},{4,5},{5,4},{6,7},{7,6},{8,9},{9,8},{10,11... | collective-permute-start | bytes 1572872 | tf_op jit(solution)/shard_map/ppermute | solution.py:337
  50.6 5.5 %collective-permute-start.10 = (f32[3,512,128]{2,1,0:T(8,128)S(1)}, f32[3,512,128]{2,1,0:T(8,128)S(1)}, u32[]{:S(2)}, u32[]{:S(2)}) collective-permute-start(f32[3,512,128]{2,1,0:T(8,128)S(1)} %get-tuple-element.66), channel_id=1, source_target_pairs={{33,64},{35,66},{37,68},{39,70},{41,72},{43,74},{45,76},{47,78},{4... | collective-permute-start | bytes 2359304 | tf_op jit(solution)/shard_map/ppermute | solution.py:337
  56.1 4.5 %collective-permute-start.9 = (f32[3,512,128]{2,1,0:T(8,128)S(1)}, f32[3,512,128]{2,1,0:T(8,128)S(1)}, u32[]{:S(2)}, u32[]{:S(2)}) collective-permute-start(f32[3,512,128]{2,1,0:T(8,128)S(1)} %get-tuple-element.65), channel_id=1, source_target_pairs={{1,33},{3,35},{5,37},{7,39},{9,41},{11,43},{13,45},{15,47},{17,49}... | collective-permute-start | bytes 2359304 | tf_op jit(solution)/shard_map/ppermute | solution.py:337
  60.7 1.9 %collective-permute-start.7 = (f32[2,128,128]{2,1,0:T(8,128)S(1)}, f32[2,128,128]{2,1,0:T(8,128)S(1)}, u32[]{:S(2)}, u32[]{:S(2)}) collective-permute-start(f32[2,128,128]{2,1,0:T(8,128)S(1)} %get-tuple-element.56), channel_id=1, source_target_pairs={{0,32},{1,33},{2,34},{3,35},{4,36},{5,37},{6,38},{7,39},{8,40},{9,... | collective-permute-start | bytes 393224 | tf_op jit(solution)/shard_map/ppermute | solution.py:337
  62.6 1.3 %collective-permute-done.7.core = f32[2,128,128]{2,1,0:T(8,128)S(1)} collective-permute-done((f32[2,128,128]{2,1,0:T(8,128)S(1)}, f32[2,128,128]{2,1,0:T(8,128)S(1)}, u32[]{:S(2)}, u32[]{:S(2)}) %collective-permute-start.7) | collective-permute-done | bytes 131104 | tf_op jit(solution)/shard_map/ppermute | solution.py:337
  63.9 2.6 %prepare_a.1 = (bf16[8,256,256]{2,1,0:T(8,128)(2,1)S(1)}, bf16[4,256,256]{2,1,0:T(8,128)(2,1)S(1)}, f32[144]{0:T(256)S(1)}) custom-call(f32[8,128]{1,0:T(8,128)S(1)} %copy-done.4, s32[2,3]{1,0:T(2,128)S(1)} %copy-done.5, s32[4]{0:T(128)S(1)} %copy-done.6, f32[8,128,128]{2,1,0:T(8,128)S(1)} %copy-done.2, f32[6,128,128]{2,1,0:T(8,128)S(1)} %collective-permute-done.across, ...), custom_call_target="tpu_custom_call" | custom-call | flops 1000 | bytes 1024 | tf_op jit(solution)/shard_map/prepare_a/pallas_call | solution.py:382
  66.5 2.1 %collective-permute-start.11 = (f32[2,512,128]{2,1,0:T(8,128)S(1)}, f32[2,512,128]{2,1,0:T(8,128)S(1)}, u32[]{:S(2)}, u32[]{:S(2)}) collective-permute-start(f32[2,512,128]{2,1,0:T(8,128)S(1)} %collective-permute-done.6.got_0), channel_id=1, source_target_pairs={{0,32},{2,34},{4,36},{6,38},{8,40},{10,42},{12,44},{14,46},{16,48}... | collective-permute-start | bytes 1572872 | tf_op jit(solution)/shard_map/ppermute | solution.py:337
  68.7 10.3 %collective-permute-start.12 = (f32[1,512,128]{2,1,0:T(8,128)S(1)}, f32[1,512,128]{2,1,0:T(8,128)S(1)}, u32[]{:S(2)}, u32[]{:S(2)}) collective-permute-start(f32[1,512,128]{2,1,0:T(8,128)S(1)} %slice.4), channel_id=1, source_target_pairs={{0,32},{2,34},{4,36},{6,38},{8,40},{10,42},{12,44},{14,46},{16,48}... | collective-permute-start | bytes 786440 | tf_op jit(solution)/shard_map/ppermute | solution.py:337
  78.9 1.1 %collective-permute-done.12.relay_1 = f32[1,512,128]{2,1,0:T(8,128)S(1)} collective-permute-done((f32[1,512,128]{2,1,0:T(8,128)S(1)}, f32[1,512,128]{2,1,0:T(8,128)S(1)}, u32[]{:S(2)}, u32[]{:S(2)}) %collective-permute-start.12) | collective-permute-done | bytes 262176 | tf_op jit(solution)/shard_map/ppermute | solution.py:337
  80.1 5.2 %sweep_a.1 = f32[512,1024]{1,0:T(8,128)} custom-call(f32[144]{0:T(256)S(1)} %get-tuple-element.57.coef, bf16[8,256,256]{2,1,0:T(8,128)(2,1)S(1)} %get-tuple-element.60.weights, bf16[4,256,256]{2,1,0:T(8,128)(2,1)S(1)} %get-tuple-element.61.ends, f32[2,512,128]{2,1,0:T(8,128)S(1)} %get-tuple-element.52.refs_7_.kept_0, ...), custom_call_target="tpu_custom_call" | custom-call | flops 4000 | bytes 1024 | tf_op jit(solution)/shard_map/sweep_a/pallas_call | solution.py:391
  (26 shorter events, 1.6 us)
Async XLA Ops:
  0.0 1.6 %copy-start = (f32[1024,512]{1,0:T(8,128)S(1)}, f32[1024,512]{1,0:T(8,128)}, u32[]{:S(2)}) copy-start(f32[1024,512]{1,0:T(8,128)} %refs_2_.1) | copy-start | bytes 6291460
  1.6 2.3 %copy-start.2 = (f32[8,128,128]{2,1,0:T(8,128)S(1)}, f32[8,128,128]{2,1,0:T(8,128)}, u32[]{:S(2)}) copy-start(f32[8,128,128]{2,1,0:T(8,128)} %own.1) | copy-start | bytes 1572868
  1.6 2.4 %copy-start.3 = (f32[4,128,128]{2,1,0:T(8,128)S(1)}, f32[4,128,128]{2,1,0:T(8,128)}, u32[]{:S(2)}) copy-start(f32[4,128,128]{2,1,0:T(8,128)} %own) | copy-start | bytes 786436
  1.7 18.0 %collective-permute-start.1 = (f32[4,256,128]{2,1,0:T(8,128)S(1)}, f32[4,256,128]{2,1,0:T(8,128)S(1)}, u32[]{:S(2)}, u32[]{:S(2)}) collective-permute-start(f32[4,256,128]{2,1,0:T(8,128)S(1)} %pack_first.1), channel_id=1, source_target_pairs={{0,1},{1,0},{2,3},{3,2},{4,5},{5,4},{6,7},{7,6},{8,9},{9,8},{10,11... | collective-permute-start | bytes 1572872 | tf_op jit(solution)/shard_map/ppermute | solution.py:337
  4.7 17.3 %copy-start.4 = (f32[8,128]{1,0:T(8,128)S(1)}, f32[8,128]{1,0:T(8,128)}, u32[]{:S(2)}) copy-start(f32[8,128]{1,0:T(8,128)} %table.3) | copy-start | bytes 12292
  4.8 17.3 %copy-start.5 = (s32[2,3]{1,0:T(2,128)S(1)}, s32[2,3]{1,0:T(2,128)}, u32[]{:S(2)}) copy-start(s32[2,3]{1,0:T(2,128)} %winds.3) | copy-start | bytes 76
  4.8 17.3 %copy-start.6 = (s32[4]{0:T(128)S(1)}, s32[4]{0:T(128)}, u32[]{:S(2)}) copy-start(s32[4]{0:T(128)} %barriers.3) | copy-start | bytes 52
  4.8 15.0 %collective-permute-start = (f32[6,128,128]{2,1,0:T(8,128)S(1)}, f32[6,128,128]{2,1,0:T(8,128)S(1)}, u32[]{:S(2)}, u32[]{:S(2)}) collective-permute-start(f32[6,128,128]{2,1,0:T(8,128)S(1)} %get-tuple-element.39), channel_id=1, source_target_pairs={{0,481},{1,480},{2,483},{3,482},{4,485},{5,484},{6,487},{7,486},{8... | collective-permute-start | bytes 1179656 | tf_op jit(solution)/shard_map/ppermute | solution.py:337
  9.8 26.7 %copy-start.1 = (f32[1024,512]{1,0:T(8,128)S(1)}, f32[1024,512]{1,0:T(8,128)}, u32[]{:S(2)}) copy-start(f32[1024,512]{1,0:T(8,128)} %refs_2_.1) | copy-start | bytes 6291460
  9.8 26.7 %collective-permute-start.4 = (f32[7,256,128]{2,1,0:T(8,128)S(1)}, f32[7,256,128]{2,1,0:T(8,128)S(1)}, u32[]{:S(2)}, u32[]{:S(2)}) collective-permute-start(f32[7,256,128]{2,1,0:T(8,128)S(1)} %get-tuple-element.48), channel_id=1, source_target_pairs={{1,3},{2,0},{3,5},{4,2},{5,7},{6,4},{7,9},{8,6},{9,11},{10,8},{11,... | collective-permute-start | bytes 2752520 | tf_op jit(solution)/shard_map/ppermute | solution.py:337
  14.9 13.3 %collective-permute-start.3 = (f32[4,256,128]{2,1,0:T(8,128)S(1)}, f32[4,256,128]{2,1,0:T(8,128)S(1)}, u32[]{:S(2)}, u32[]{:S(2)}) collective-permute-start(f32[4,256,128]{2,1,0:T(8,128)S(1)} %get-tuple-element.44), channel_id=1, source_target_pairs={{0,1},{1,0},{2,3},{3,2},{4,5},{5,4},{6,7},{7,6},{8,9},{9,8},{10,11... | collective-permute-start | bytes 1572872 | tf_op jit(solution)/shard_map/ppermute | solution.py:337
  20.1 16.4 %collective-permute-start.2 = (f32[4,256,128]{2,1,0:T(8,128)S(1)}, f32[4,256,128]{2,1,0:T(8,128)S(1)}, u32[]{:S(2)}, u32[]{:S(2)}) collective-permute-start(f32[4,256,128]{2,1,0:T(8,128)S(1)} %pack_far.1), channel_id=1, source_target_pairs={{0,2},{2,4},{3,1},{4,6},{5,3},{6,8},{7,5},{8,10},{9,7},{10,12},{11... | collective-permute-start | bytes 1572872 | tf_op jit(solution)/shard_map/ppermute | solution.py:337
  28.2 15.4 %collective-permute-start.5 = (f32[3,256,128]{2,1,0:T(8,128)S(1)}, f32[3,256,128]{2,1,0:T(8,128)S(1)}, u32[]{:S(2)}, u32[]{:S(2)}) collective-permute-start(f32[3,256,128]{2,1,0:T(8,128)S(1)} %get-tuple-element.49), channel_id=1, source_target_pairs={{1,2},{2,1},{3,4},{4,3},{5,6},{6,5},{7,8},{8,7},{9,10},{10,9},{11,... | collective-permute-start | bytes 1179656 | tf_op jit(solution)/shard_map/ppermute | solution.py:337
  41.1 15.0 %collective-permute-start.6 = (f32[2,512,128]{2,1,0:T(8,128)S(1)}, f32[2,512,128]{2,1,0:T(8,128)S(1)}, u32[]{:S(2)}, u32[]{:S(2)}) collective-permute-start(f32[2,512,128]{2,1,0:T(8,128)S(1)} %get-tuple-element.53.refs_8_), channel_id=1, source_target_pairs={{0,1},{1,0},{2,3},{3,2},{4,5},{5,4},{6,7},{7,6},{8,9},{9,8},{10,11... | collective-permute-start | bytes 1572872 | tf_op jit(solution)/shard_map/ppermute | solution.py:337
  47.8 20.8 %collective-permute-start.8 = (f32[2,512,128]{2,1,0:T(8,128)S(1)}, f32[2,512,128]{2,1,0:T(8,128)S(1)}, u32[]{:S(2)}, u32[]{:S(2)}) collective-permute-start(f32[2,512,128]{2,1,0:T(8,128)S(1)} %get-tuple-element.64), channel_id=1, source_target_pairs={{0,1},{1,0},{2,3},{3,2},{4,5},{5,4},{6,7},{7,6},{8,9},{9,8},{10,11... | collective-permute-start | bytes 1572872 | tf_op jit(solution)/shard_map/ppermute | solution.py:337
  50.6 29.5 %collective-permute-start.10 = (f32[3,512,128]{2,1,0:T(8,128)S(1)}, f32[3,512,128]{2,1,0:T(8,128)S(1)}, u32[]{:S(2)}, u32[]{:S(2)}) collective-permute-start(f32[3,512,128]{2,1,0:T(8,128)S(1)} %get-tuple-element.66), channel_id=1, source_target_pairs={{33,64},{35,66},{37,68},{39,70},{41,72},{43,74},{45,76},{47,78},{4... | collective-permute-start | bytes 2359304 | tf_op jit(solution)/shard_map/ppermute | solution.py:337
  56.1 23.9 %collective-permute-start.9 = (f32[3,512,128]{2,1,0:T(8,128)S(1)}, f32[3,512,128]{2,1,0:T(8,128)S(1)}, u32[]{:S(2)}, u32[]{:S(2)}) collective-permute-start(f32[3,512,128]{2,1,0:T(8,128)S(1)} %get-tuple-element.65), channel_id=1, source_target_pairs={{1,33},{3,35},{5,37},{7,39},{9,41},{11,43},{13,45},{15,47},{17,49}... | collective-permute-start | bytes 2359304 | tf_op jit(solution)/shard_map/ppermute | solution.py:337
  60.7 3.2 %collective-permute-start.7 = (f32[2,128,128]{2,1,0:T(8,128)S(1)}, f32[2,128,128]{2,1,0:T(8,128)S(1)}, u32[]{:S(2)}, u32[]{:S(2)}) collective-permute-start(f32[2,128,128]{2,1,0:T(8,128)S(1)} %get-tuple-element.56), channel_id=1, source_target_pairs={{0,32},{1,33},{2,34},{3,35},{4,36},{5,37},{6,38},{7,39},{8,40},{9,... | collective-permute-start | bytes 393224 | tf_op jit(solution)/shard_map/ppermute | solution.py:337
  66.5 13.5 %collective-permute-start.11 = (f32[2,512,128]{2,1,0:T(8,128)S(1)}, f32[2,512,128]{2,1,0:T(8,128)S(1)}, u32[]{:S(2)}, u32[]{:S(2)}) collective-permute-start(f32[2,512,128]{2,1,0:T(8,128)S(1)} %collective-permute-done.6.got_0), channel_id=1, source_target_pairs={{0,32},{2,34},{4,36},{6,38},{8,40},{10,42},{12,44},{14,46},{16,48}... | collective-permute-start | bytes 1572872 | tf_op jit(solution)/shard_map/ppermute | solution.py:337
  68.7 11.4 %collective-permute-start.12 = (f32[1,512,128]{2,1,0:T(8,128)S(1)}, f32[1,512,128]{2,1,0:T(8,128)S(1)}, u32[]{:S(2)}, u32[]{:S(2)}) collective-permute-start(f32[1,512,128]{2,1,0:T(8,128)S(1)} %slice.4), channel_id=1, source_target_pairs={{0,32},{2,34},{4,36},{6,38},{8,40},{10,42},{12,44},{14,46},{16,48}... | collective-permute-start | bytes 786440 | tf_op jit(solution)/shard_map/ppermute | solution.py:337

commit v5 on v4

--- a/solution.py
+++ b/solution.py
@@ -105,10 +105,7 @@
 
 
 def pack_first(cov, first, sems):
-    l = side()
-    at = rows_of(1 - l, 0)
-    copies = [(cov.at[rows(at, 256), lanes(l + i)], first.at[i]) for i in range(3)]
-    run_copies(copies + [(cov.at[rows(at, 256), lanes(3 - 3 * l)], first.at[3])], sems)
+    run_copies([(cov.at[rows(rows_of(1 - side(), 0), 256)], first)], sems)
 
 
 def pack_second(cov, mix_a, mix_b, across, near, core, sems):
@@ -130,16 +127,13 @@
 def pack_rest(cov, second, third, sems):
     l = side()
     at = rows_of(1 - l, 1)
-    copies = []
-    for i in range(3):
-        copies.append((cov.at[rows(at, 256), lanes(l + i)], second.at[i]))
-        copies.append((cov.at[rows(at, 256), lanes(l + i)], third.at[i]))
-    run_copies(copies + [(cov.at[rows(at, 256), lanes(3 - 3 * l)], second.at[3])], sems)
+    copies = [(cov.at[rows(at, 256)], second)]
+    run_copies(copies + [(cov.at[rows(at, 256), lanes(l + i)], third.at[i]) for i in range(3)], sems)
 
 
 def pack_far(pair, across, out, sems):
     l = side()
-    copies = [(pair.at[pl.ds(0, 3)], out.at[pl.ds(0, 3)])]
+    copies = [(pair.at[:, lanes(1 - l + i)], out.at[i]) for i in range(3)]
     for m in range(2):
         copies.append((across.at[2 - 2 * l + m], out.at[3, pl.ds(m * LEV, LEV)]))
     run_copies(copies, sems)
@@ -205,9 +199,9 @@
 def step_latitude(step, p, source, weights, ends, coef):
     weight = weights[p - 3] if 3 <= p <= 10 else ends[p - 1 if p < 3 else p - 9]
     y = (
-        coef[step * 48 + p] * source[p - 1]
-        + coef[step * 48 + 16 + p] * source[p]
-        + coef[step * 48 + 32 + p] * source[p + 1]
+        coef[step * 48 + p] * source(p - 1)
+        + coef[step * 48 + 16 + p] * source(p)
+        + coef[step * 48 + 32 + p] * source(p + 1)
     )
     high = y.astype(BF16)
     low = (y - high.astype(F32)).astype(BF16)
@@ -217,43 +211,39 @@
     return both[:, :LEV] + both[:, LEV:]
 
 
-def first_steps(window, other, weights, ends, coef):
+def first_steps(source, window, other, weights, ends, coef):
     for p in range(1, WINDOW - 1):
-        other[p] = step_latitude(0, p, window, weights, ends, coef)
+        other[p] = step_latitude(0, p, source, weights, ends, coef)
     for p in range(2, WINDOW - 2):
-        window[p] = step_latitude(1, p, other, weights, ends, coef)
+        window[p] = step_latitude(1, p, lambda at: other[at], weights, ends, coef)
 
 
 def sweep_b(chunk, *refs):
     if chunk == 0:
-        coef, weights, cov, pair, near, far, kept, sent, ends, window, other, edge, sems = refs
+        coef, weights, cov, pair, near, far, kept, sent, ends, window, other = refs
     else:
         (coef, weights, cov, pair, near, far, ends, kept_before, sent_before,
-         kept, sent, same, cross, window, other, sems, late) = refs
-    l = side()
-    copies = []
-    for q in range(3):
-        t = turned(l, q, 3)
-        copies.append((near.at[3 * chunk + t], window.at[q]))
-        copies.append((pair.at[t], window.at[3 + q]))
-        copies.append((far.at[t], window.at[11 + q]))
-    copies.append((pair.at[3], window.at[6]))
-    for q in range(4):
-        copies.append((cov.at[rows(rows_of(l, chunk), 256), lanes(turned(l, q, 4))], window.at[7 + q]))
+         kept, sent, same, cross, window, other, late) = refs
+    l = side()
+
+    def source(p):
+        if p < 3:
+            return near[3 * chunk + turned(l, p, 3)]
+        if p < 7:
+            return pair[:, lanes(turned(l, p - 3, 4))]
+        if p < 11:
+            return cov[rows(rows_of(l, chunk), 256), lanes(turned(l, p - 7, 4))]
+        return far[turned(l, p - 11, 3)]
+
     if chunk == 0:
-        for m in range(2):
-            copies.append((near.at[6, pl.ds(m * LEV, LEV)], edge.at[m]))
-            copies.append((far.at[3, pl.ds(m * LEV, LEV)], edge.at[2 + m]))
-    run_copies(copies, sems)
-    if chunk == 0:
-        for place in range(2):
-            for q in range(2):
-                m = turned(l, q, 2)
-                write_weight(ends, 2 * place + q, edge[2 * place + m])
-    first_steps(window, other, weights, ends, coef)
+        for q in range(2):
+            at = rows(turned(l, q, 2) * LEV, LEV)
+            write_weight(ends, q, near[6, at, :])
+            write_weight(ends, 2 + q, far[3, at, :])
+    first_steps(source, window, other, weights, ends, coef)
 
     def finish(p, target, q):
-        z = step_latitude(2, p, window, weights, ends, coef)
+        z = step_latitude(2, p, lambda at: window[at], weights, ends, coef)
         b = turned(l, q, 4)
         for i in range(2):
             u = turned(l, i, 2)
@@ -279,28 +269,30 @@
             window, other, sems):
     l = side()
     k = lax.rem(lax.axis_index("row"), 2)
-    copies = [(same.at[q], window.at[q]) for q in range(3)]
-    for u in range(2):
-        copies.append((kept_1.at[u], window.at[7 + u]))
-        copies.append((kept_0.at[u], window.at[9 + u]))
-        copies.append((got_0.at[u], window.at[4 - u]))
-        copies.append((got_1.at[u], window.at[6 - u]))
-    across = [(cross.at[q], window.at[13 - q]) for q in range(3)]
-    inside = [(relay_1.at[0], window.at[13])] + [(relay_0.at[u], window.at[12 - u]) for u in range(2)]
 
     @pl.when(k == l)
     def _():
-        run_copies(across, sems)
+        run_copies([(cross.at[q], window.at[13 - q]) for q in range(3)], sems)
 
     @pl.when(k != l)
     def _():
-        run_copies(inside, sems)
-
-    run_copies(copies, sems)
-    first_steps(window, other, weights, ends, coef)
-
+        copies = [(relay_0.at[u], window.at[12 - u]) for u in range(2)]
+        run_copies(copies + [(relay_1.at[0], window.at[13])], sems)
+
+    def source(p):
+        if p < 3:
+            return same[p]
+        if p < 7:
+            return (got_0, got_1)[p > 4][p % 2 if p > 4 else 4 - p]
+        if p < 11:
+            return (kept_1, kept_0)[p > 8][1 - p % 2]
+        return window[p]
+
+    first_steps(source, window, other, weights, ends, coef)
     for p in range(3, WINDOW - 3):
-        out[:, lanes(turned(l, p - 3, 8))] = step_latitude(2, p, window, weights, ends, coef)
+        out[:, lanes(turned(l, p - 3, 8))] = step_latitude(
+            2, p, lambda at: window[at], weights, ends, coef
+        )
 
 
 def pack(kernel, outs, operands, copies, name):
@@ -338,7 +330,7 @@
     dma = lambda n: pltpu.SemaphoreType.DMA((n,))
 
     piece = lambda n: shaped(n, 256, LEV)
-    out_0 = pack(pack_first, piece(4), 1, 4, "pack_first")(covariance)
+    out_0 = pack(pack_first, shaped(256, 512), 1, 1, "pack_first")(covariance)
     pair_0 = send(out_0, swap_y)
     covariance, mix_a, mix_b, out_0 = lax.optimization_barrier((covariance, mix_a, mix_b, out_0))
     out_across, out_near, out_core = pack(
@@ -347,11 +339,10 @@
     across = send(out_across, functools.partial(mats_across, x_size))
     near = send(out_near, near_z)
     covariance, out_across = lax.optimization_barrier((covariance, out_across))
-    out_1, out_far_1 = pack(pack_rest, (piece(4), piece(3)), 1, 7, "pack_rest")(covariance)
+    out_1, out_far_1 = pack(pack_rest, (shaped(256, 512), piece(3)), 1, 4, "pack_rest")(covariance)
     pair_1 = send(out_1, swap_y)
-    out_far_0 = pack(pack_far, piece(4), 2, 3, "pack_far")(pair_0, across)
+    out_far_0 = pack(pack_far, piece(4), 2, 5, "pack_far")(pair_0, across)
     far_0 = send(out_far_0, far_z)
-    out_far_1, pair_1 = lax.optimization_barrier((out_far_1, pair_1))
     far_1 = send(out_far_1, far_direct)
 
     weight = shaped(8, 256, 256, dtype=BF16)
@@ -365,14 +356,14 @@
     block = shaped(2, 512, LEV)
     field = pltpu.VMEM((WINDOW, 256, LEV), F32)
     kept_0, sent_0, ends_b = call(
-        functools.partial(sweep_b, 0), (block, block, ends), [SMEM, VMEM] + [ANY] * 4, (VMEM,) * 3,
-        [field, field, pltpu.VMEM((4, LEV, LEV), F32), dma(18)], COST, "sweep_b0",
+        functools.partial(sweep_b, 0), (block, block, ends), [SMEM] + [VMEM] * 5, (VMEM,) * 3,
+        [field, field], COST, "sweep_b0",
     )(coef_b, weights_b, covariance, pair_0, near, far_0)
     got_0 = send(sent_0, swap_y)
     kept_1, sent_1, out_same, out_cross = call(
         functools.partial(sweep_b, 1), (block, block, shaped(3, 512, LEV), shaped(3, 512, LEV)),
-        [SMEM, VMEM] + [ANY] * 4 + [VMEM, ANY, ANY], (VMEM, VMEM, ANY, ANY),
-        [field, field, dma(14), dma(4)], COST, "sweep_b1",
+        [SMEM] + [VMEM] * 6 + [ANY, ANY], (VMEM, VMEM, ANY, ANY),
+        [field, field, dma(4)], COST, "sweep_b1",
     )(coef_b, weights_b, covariance, pair_1, near, far_1, ends_b, kept_0, sent_0)
     got_1 = send(sent_1, swap_y)
     cross = send(out_cross, halo_cross)
@@ -389,7 +380,7 @@
 
     field = pltpu.VMEM((WINDOW, 512, LEV), F32)
     return call(
-        sweep_a, shaped(512, 1024), [SMEM, VMEM, VMEM] + [ANY] * 8, VMEM, [field, field, dma(11)],
+        sweep_a, shaped(512, 1024), [SMEM] + [VMEM] * 7 + [ANY] * 3, VMEM, [field, field, dma(3)],
         4 * 10**3, "sweep_a",
     )(coef_a, weights_a, ends_a, kept_0, kept_1, got_0, got_1, same, cross, relay_0, relay_1)
 

time: 85.7 us -> 84.5 us (0.986)
  the two profiles are of different devices: /device:TPU:105 before, /device:TPU:233 now
where the time goes in v5:
time: 84.5 us; the launch traced here: 84 us
  starting transfers between devices  41.1 us (49%)
  waiting for transfers between devices  25.1 us (30%)
  Pallas kernels  15.9 us (19%)
  local copies, waits for them, and re-layouts  1.64 us (2%)
    ppermute x13, starting transfers between devices, per_device(): lax.ppermute(value, AXES, pairs(move, x_size, z_size))  41.1 us
    ppermute x13, waiting for transfers between devices, per_device(): lax.ppermute(value, AXES, pairs(move, x_size, z_size))  25.1 us
    pallas_call x1, Pallas kernels, per_device(): call(sweep_a, shaped(512, 1024), [SMEM] + [VMEM] * 7 + [ANY] * 3, VMEM, [...  4.9 us
    pallas_call x1, Pallas kernels, per_device(): call(prepare_a, (weight, ends, shaped(144)), [SMEM] * 3 + [VMEM] * 3, (VM...  2.61 us
    pallas_call x1, Pallas kernels, per_device(): call(prepare_b, (weight, shaped(144)), [SMEM] * 3 + [VMEM] * 2, (VMEM, SM...  2.46 us
    pallas_call x1, Pallas kernels, per_device(): call(functools.partial(sweep_b, 1), (block, block, shaped(3, 512, LEV), s...  2.34 us
    pallas_call x1, Pallas kernels, per_device(): call(functools.partial(sweep_b, 0), (block, block, ends), [SMEM] + [VMEM]...  2.32 us
  transfers between devices with their start and end apart: 13, of which 7 were waited for; matrix products, arithmetic and copies ran while one was open for 0% of the time, Pallas kernels for 13%

profile of v5, /device:TPU:233, one launch (start us, length us, event | category | flops | bytes accessed | tf_op | source)
XLA Modules:
  0.0 84.0 jit_solution(3649400696079571926)
XLA Ops:
  0.0 1.6 %copy-done = f32[1024,512]{1,0:T(8,128)S(1)} copy-done((f32[1024,512]{1,0:T(8,128)S(1)}, f32[1024,512]{1,0:T(8,128)}, u32[]{:S(2)}) %copy-start) | copy-done | bytes 2097176
  1.6 2.2 %collective-permute-start.1 = (f32[256,512]{1,0:T(8,128)S(1)}, f32[256,512]{1,0:T(8,128)S(1)}, u32[]{:S(2)}, u32[]{:S(2)}) collective-permute-start(f32[256,512]{1,0:T(8,128)S(1)} %pack_first.1), channel_id=1, source_target_pairs={{0,1},{1,0},{2,3},{3,2},{4,5},{5,4},{6,7},{7,6},{8,9},{9,8},{10,11... | collective-permute-start | bytes 1572872 | tf_op jit(solution)/shard_map/ppermute | solution.py:329
  4.7 5.0 %collective-permute-start = (f32[6,128,128]{2,1,0:T(8,128)S(1)}, f32[6,128,128]{2,1,0:T(8,128)S(1)}, u32[]{:S(2)}, u32[]{:S(2)}) collective-permute-start(f32[6,128,128]{2,1,0:T(8,128)S(1)} %get-tuple-element.37), channel_id=1, source_target_pairs={{0,481},{1,480},{2,483},{3,482},{4,485},{5,484},{6,487},{7,486},{8... | collective-permute-start | bytes 1179656 | tf_op jit(solution)/shard_map/ppermute | solution.py:329
  9.7 4.9 %collective-permute-start.4 = (f32[7,256,128]{2,1,0:T(8,128)S(1)}, f32[7,256,128]{2,1,0:T(8,128)S(1)}, u32[]{:S(2)}, u32[]{:S(2)}) collective-permute-start(f32[7,256,128]{2,1,0:T(8,128)S(1)} %get-tuple-element.44), channel_id=1, source_target_pairs={{1,3},{2,0},{3,5},{4,2},{5,7},{6,4},{7,9},{8,6},{9,11},{10,8},{11,... | collective-permute-start | bytes 2752520 | tf_op jit(solution)/shard_map/ppermute | solution.py:329
  14.8 1.9 %collective-permute-start.3 = (f32[256,512]{1,0:T(8,128)S(1)}, f32[256,512]{1,0:T(8,128)S(1)}, u32[]{:S(2)}, u32[]{:S(2)}) collective-permute-start(f32[256,512]{1,0:T(8,128)S(1)} %get-tuple-element.41), channel_id=1, source_target_pairs={{0,1},{1,0},{2,3},{3,2},{4,5},{5,4},{6,7},{7,6},{8,9},{9,8},{10,11... | collective-permute-start | bytes 1572872 | tf_op jit(solution)/shard_map/ppermute | solution.py:329
  16.7 3.0 %collective-permute-done.across = f32[6,128,128]{2,1,0:T(8,128)S(1)} collective-permute-done((f32[6,128,128]{2,1,0:T(8,128)S(1)}, f32[6,128,128]{2,1,0:T(8,128)S(1)}, u32[]{:S(2)}, u32[]{:S(2)}) %collective-permute-start) | collective-permute-done | bytes 393248 | tf_op jit(solution)/shard_map/ppermute | solution.py:329
  20.0 1.9 %collective-permute-start.2 = (f32[4,256,128]{2,1,0:T(8,128)S(1)}, f32[4,256,128]{2,1,0:T(8,128)S(1)}, u32[]{:S(2)}, u32[]{:S(2)}) collective-permute-start(f32[4,256,128]{2,1,0:T(8,128)S(1)} %pack_far.1), channel_id=1, source_target_pairs={{0,2},{2,4},{3,1},{4,6},{5,3},{6,8},{7,5},{8,10},{9,7},{10,12},{11... | collective-permute-start | bytes 1572872 | tf_op jit(solution)/shard_map/ppermute | solution.py:329
  21.9 6.2 %collective-permute-start.5 = (f32[3,256,128]{2,1,0:T(8,128)S(1)}, f32[3,256,128]{2,1,0:T(8,128)S(1)}, u32[]{:S(2)}, u32[]{:S(2)}) collective-permute-start(f32[3,256,128]{2,1,0:T(8,128)S(1)} %get-tuple-element.45), channel_id=1, source_target_pairs={{1,2},{2,1},{3,4},{4,3},{5,6},{6,5},{7,8},{8,7},{9,10},{10,9},{11,... | collective-permute-start | bytes 1179656 | tf_op jit(solution)/shard_map/ppermute | solution.py:329
  28.1 2.5 %prepare_b.1 = (bf16[8,256,256]{2,1,0:T(8,128)(2,1)S(1)}, f32[144]{0:T(256)S(1)}) custom-call(f32[8,128]{1,0:T(8,128)S(1)} %copy-done.4, s32[2,3]{1,0:T(2,128)S(1)} %copy-done.5, s32[4]{0:T(128)S(1)} %copy-done.6, f32[6,128,128]{2,1,0:T(8,128)S(1)} %collective-permute-done.across, f32[4,128,128]{2,1,0:T(8,128)S(1)} %copy-done.3), custom_call_target="tpu_custom_call" | custom-call | flops 1000 | bytes 1024 | tf_op jit(solution)/shard_map/prepare_b/pallas_call | solution.py:351
  30.6 5.7 %collective-permute-done.2.refs_5_ = f32[4,256,128]{2,1,0:T(8,128)S(1)} collective-permute-done((f32[4,256,128]{2,1,0:T(8,128)S(1)}, f32[4,256,128]{2,1,0:T(8,128)S(1)}, u32[]{:S(2)}, u32[]{:S(2)}) %collective-permute-start.2) | collective-permute-done | bytes 524320 | tf_op jit(solution)/shard_map/ppermute | solution.py:329
  36.3 2.3 %sweep_b0.1 = (f32[2,512,128]{2,1,0:T(8,128)S(1)}, f32[2,512,128]{2,1,0:T(8,128)S(1)}, bf16[4,256,256]{2,1,0:T(8,128)(2,1)S(1)}) custom-call(f32[144]{0:T(256)S(1)} %get-tuple-element.38.refs_0_, bf16[8,256,256]{2,1,0:T(8,128)(2,1)S(1)} %get-tuple-element.42.refs_1_, f32[1024,512]{1,0:T(8,128)S(1)} %copy-done.1, ...), custom_call_target="tpu_custom_call" | custom-call | flops 4000000000 | bytes 1024 | tf_op jit(solution)/shard_map/sweep_b0/pallas_call | solution.py:358
  38.6 2.7 %collective-permute-start.6 = (f32[2,512,128]{2,1,0:T(8,128)S(1)}, f32[2,512,128]{2,1,0:T(8,128)S(1)}, u32[]{:S(2)}, u32[]{:S(2)}) collective-permute-start(f32[2,512,128]{2,1,0:T(8,128)S(1)} %get-tuple-element.49.refs_8_), channel_id=1, source_target_pairs={{0,1},{1,0},{2,3},{3,2},{4,5},{5,4},{6,7},{7,6},{8,9},{9,8},{10,11... | collective-permute-start | bytes 1572872 | tf_op jit(solution)/shard_map/ppermute | solution.py:329
  41.3 1.3 %collective-permute-done.5.refs_5_ = f32[3,256,128]{2,1,0:T(8,128)S(1)} collective-permute-done((f32[3,256,128]{2,1,0:T(8,128)S(1)}, f32[3,256,128]{2,1,0:T(8,128)S(1)}, u32[]{:S(2)}, u32[]{:S(2)}) %collective-permute-start.5) | collective-permute-done | bytes 393248 | tf_op jit(solution)/shard_map/ppermute | solution.py:329
  42.6 2.3 %sweep_b1.1 = (f32[2,512,128]{2,1,0:T(8,128)S(1)}, f32[2,512,128]{2,1,0:T(8,128)S(1)}, f32[3,512,128]{2,1,0:T(8,128)S(1)}, f32[3,512,128]{2,1,0:T(8,128)S(1)}) custom-call(f32[144]{0:T(256)S(1)} %get-tuple-element.38.refs_0_, bf16[8,256,256]{2,1,0:T(8,128)(2,1)S(1)} %get-tuple-element.42.refs_1_, f32[1024,512]{1,0:T(8,128)S(1)} %copy-done.1, ...), custom_call_target="tpu_custom_call" | custom-call | flops 4000000000 | bytes 1024 | tf_op jit(solution)/shard_map/sweep_b1/pallas_call | solution.py:363
  45.0 1.9 %collective-permute-start.8 = (f32[2,512,128]{2,1,0:T(8,128)S(1)}, f32[2,512,128]{2,1,0:T(8,128)S(1)}, u32[]{:S(2)}, u32[]{:S(2)}) collective-permute-start(f32[2,512,128]{2,1,0:T(8,128)S(1)} %get-tuple-element.60), channel_id=1, source_target_pairs={{0,1},{1,0},{2,3},{3,2},{4,5},{5,4},{6,7},{7,6},{8,9},{9,8},{10,11... | collective-permute-start | bytes 1572872 | tf_op jit(solution)/shard_map/ppermute | solution.py:329
  46.9 5.3 %collective-permute-start.10 = (f32[3,512,128]{2,1,0:T(8,128)S(1)}, f32[3,512,128]{2,1,0:T(8,128)S(1)}, u32[]{:S(2)}, u32[]{:S(2)}) collective-permute-start(f32[3,512,128]{2,1,0:T(8,128)S(1)} %get-tuple-element.62), channel_id=1, source_target_pairs={{33,64},{35,66},{37,68},{39,70},{41,72},{43,74},{45,76},{47,78},{4... | collective-permute-start | bytes 2359304 | tf_op jit(solution)/shard_map/ppermute | solution.py:329
  52.2 3.6 %collective-permute-done.6.got_0 = f32[2,512,128]{2,1,0:T(8,128)S(1)} collective-permute-done((f32[2,512,128]{2,1,0:T(8,128)S(1)}, f32[2,512,128]{2,1,0:T(8,128)S(1)}, u32[]{:S(2)}, u32[]{:S(2)}) %collective-permute-start.6) | collective-permute-done | bytes 524320 | tf_op jit(solution)/shard_map/ppermute | solution.py:329
  55.9 2.7 %collective-permute-start.9 = (f32[3,512,128]{2,1,0:T(8,128)S(1)}, f32[3,512,128]{2,1,0:T(8,128)S(1)}, u32[]{:S(2)}, u32[]{:S(2)}) collective-permute-start(f32[3,512,128]{2,1,0:T(8,128)S(1)} %get-tuple-element.61), channel_id=1, source_target_pairs={{1,33},{3,35},{5,37},{7,39},{9,41},{11,43},{13,45},{15,47},{17,49}... | collective-permute-start | bytes 2359304 | tf_op jit(solution)/shard_map/ppermute | solution.py:329
  58.6 1.9 %collective-permute-start.7 = (f32[2,128,128]{2,1,0:T(8,128)S(1)}, f32[2,128,128]{2,1,0:T(8,128)S(1)}, u32[]{:S(2)}, u32[]{:S(2)}) collective-permute-start(f32[2,128,128]{2,1,0:T(8,128)S(1)} %get-tuple-element.52), channel_id=1, source_target_pairs={{0,32},{1,33},{2,34},{3,35},{4,36},{5,37},{6,38},{7,39},{8,40},{9,... | collective-permute-start | bytes 393224 | tf_op jit(solution)/shard_map/ppermute | solution.py:329
  61.8 2.6 %prepare_a.1 = (bf16[8,256,256]{2,1,0:T(8,128)(2,1)S(1)}, bf16[4,256,256]{2,1,0:T(8,128)(2,1)S(1)}, f32[144]{0:T(256)S(1)}) custom-call(f32[8,128]{1,0:T(8,128)S(1)} %copy-done.4, s32[2,3]{1,0:T(2,128)S(1)} %copy-done.5, s32[4]{0:T(128)S(1)} %copy-done.6, f32[8,128,128]{2,1,0:T(8,128)S(1)} %copy-done.2, f32[6,128,128]{2,1,0:T(8,128)S(1)} %collective-permute-done.across, ...), custom_call_target="tpu_custom_call" | custom-call | flops 1000 | bytes 1024 | tf_op jit(solution)/shard_map/prepare_a/pallas_call | solution.py:373
  64.4 2.1 %collective-permute-start.11 = (f32[2,512,128]{2,1,0:T(8,128)S(1)}, f32[2,512,128]{2,1,0:T(8,128)S(1)}, u32[]{:S(2)}, u32[]{:S(2)}) collective-permute-start(f32[2,512,128]{2,1,0:T(8,128)S(1)} %collective-permute-done.6.got_0), channel_id=1, source_target_pairs={{0,32},{2,34},{4,36},{6,38},{8,40},{10,42},{12,44},{14,46},{16,48}... | collective-permute-start | bytes 1572872 | tf_op jit(solution)/shard_map/ppermute | solution.py:329
  66.5 9.0 %collective-permute-done.8.got_1 = f32[2,512,128]{2,1,0:T(8,128)S(1)} collective-permute-done((f32[2,512,128]{2,1,0:T(8,128)S(1)}, f32[2,512,128]{2,1,0:T(8,128)S(1)}, u32[]{:S(2)}, u32[]{:S(2)}) %collective-permute-start.8) | collective-permute-done | bytes 524320 | tf_op jit(solution)/shard_map/ppermute | solution.py:329
  75.6 2.4 %collective-permute-start.12 = (f32[1,512,128]{2,1,0:T(8,128)S(1)}, f32[1,512,128]{2,1,0:T(8,128)S(1)}, u32[]{:S(2)}, u32[]{:S(2)}) collective-permute-start(f32[1,512,128]{2,1,0:T(8,128)S(1)} %slice.4), channel_id=1, source_target_pairs={{0,32},{2,34},{4,36},{6,38},{8,40},{10,42},{12,44},{14,46},{16,48}... | collective-permute-start | bytes 786440 | tf_op jit(solution)/shard_map/ppermute | solution.py:329
  79.1 4.9 %sweep_a.1 = f32[512,1024]{1,0:T(8,128)} custom-call(f32[144]{0:T(256)S(1)} %get-tuple-element.53.coef, bf16[8,256,256]{2,1,0:T(8,128)(2,1)S(1)} %get-tuple-element.56.weights, bf16[4,256,256]{2,1,0:T(8,128)(2,1)S(1)} %get-tuple-element.57.ends, f32[2,512,128]{2,1,0:T(8,128)S(1)} %get-tuple-element.48.refs_7_.kept_0, ...), custom_call_target="tpu_custom_call" | custom-call | flops 4000 | bytes 1024 | tf_op jit(solution)/shard_map/sweep_a/pallas_call | solution.py:382
  (26 shorter events, 3.8 us)
Async XLA Ops:
  0.0 1.6 %copy-start = (f32[1024,512]{1,0:T(8,128)S(1)}, f32[1024,512]{1,0:T(8,128)}, u32[]{:S(2)}) copy-start(f32[1024,512]{1,0:T(8,128)} %refs_2_.1) | copy-start | bytes 6291460
  1.6 2.3 %copy-start.2 = (f32[8,128,128]{2,1,0:T(8,128)S(1)}, f32[8,128,128]{2,1,0:T(8,128)}, u32[]{:S(2)}) copy-start(f32[8,128,128]{2,1,0:T(8,128)} %own.1) | copy-start | bytes 1572868
  1.6 2.3 %copy-start.3 = (f32[4,128,128]{2,1,0:T(8,128)S(1)}, f32[4,128,128]{2,1,0:T(8,128)}, u32[]{:S(2)}) copy-start(f32[4,128,128]{2,1,0:T(8,128)} %own) | copy-start | bytes 786436
  1.6 18.0 %collective-permute-start.1 = (f32[256,512]{1,0:T(8,128)S(1)}, f32[256,512]{1,0:T(8,128)S(1)}, u32[]{:S(2)}, u32[]{:S(2)}) collective-permute-start(f32[256,512]{1,0:T(8,128)S(1)} %pack_first.1), channel_id=1, source_target_pairs={{0,1},{1,0},{2,3},{3,2},{4,5},{5,4},{6,7},{7,6},{8,9},{9,8},{10,11... | collective-permute-start | bytes 1572872 | tf_op jit(solution)/shard_map/ppermute | solution.py:329
  4.7 23.4 %copy-start.4 = (f32[8,128]{1,0:T(8,128)S(1)}, f32[8,128]{1,0:T(8,128)}, u32[]{:S(2)}) copy-start(f32[8,128]{1,0:T(8,128)} %table.3) | copy-start | bytes 12292
  4.7 23.4 %copy-start.5 = (s32[2,3]{1,0:T(2,128)S(1)}, s32[2,3]{1,0:T(2,128)}, u32[]{:S(2)}) copy-start(s32[2,3]{1,0:T(2,128)} %winds.3) | copy-start | bytes 76
  4.7 23.4 %copy-start.6 = (s32[4]{0:T(128)S(1)}, s32[4]{0:T(128)}, u32[]{:S(2)}) copy-start(s32[4]{0:T(128)} %barriers.3) | copy-start | bytes 52
  4.7 15.0 %collective-permute-start = (f32[6,128,128]{2,1,0:T(8,128)S(1)}, f32[6,128,128]{2,1,0:T(8,128)S(1)}, u32[]{:S(2)}, u32[]{:S(2)}) collective-permute-start(f32[6,128,128]{2,1,0:T(8,128)S(1)} %get-tuple-element.37), channel_id=1, source_target_pairs={{0,481},{1,480},{2,483},{3,482},{4,485},{5,484},{6,487},{7,486},{8... | collective-permute-start | bytes 1179656 | tf_op jit(solution)/shard_map/ppermute | solution.py:329
  9.7 26.6 %copy-start.1 = (f32[1024,512]{1,0:T(8,128)S(1)}, f32[1024,512]{1,0:T(8,128)}, u32[]{:S(2)}) copy-start(f32[1024,512]{1,0:T(8,128)} %refs_2_.1) | copy-start | bytes 6291460
  9.7 26.6 %collective-permute-start.4 = (f32[7,256,128]{2,1,0:T(8,128)S(1)}, f32[7,256,128]{2,1,0:T(8,128)S(1)}, u32[]{:S(2)}, u32[]{:S(2)}) collective-permute-start(f32[7,256,128]{2,1,0:T(8,128)S(1)} %get-tuple-element.44), channel_id=1, source_target_pairs={{1,3},{2,0},{3,5},{4,2},{5,7},{6,4},{7,9},{8,6},{9,11},{10,8},{11,... | collective-permute-start | bytes 2752520 | tf_op jit(solution)/shard_map/ppermute | solution.py:329
  14.8 15.8 %collective-permute-start.3 = (f32[256,512]{1,0:T(8,128)S(1)}, f32[256,512]{1,0:T(8,128)S(1)}, u32[]{:S(2)}, u32[]{:S(2)}) collective-permute-start(f32[256,512]{1,0:T(8,128)S(1)} %get-tuple-element.41), channel_id=1, source_target_pairs={{0,1},{1,0},{2,3},{3,2},{4,5},{5,4},{6,7},{7,6},{8,9},{9,8},{10,11... | collective-permute-start | bytes 1572872 | tf_op jit(solution)/shard_map/ppermute | solution.py:329
  20.0 16.3 %collective-permute-start.2 = (f32[4,256,128]{2,1,0:T(8,128)S(1)}, f32[4,256,128]{2,1,0:T(8,128)S(1)}, u32[]{:S(2)}, u32[]{:S(2)}) collective-permute-start(f32[4,256,128]{2,1,0:T(8,128)S(1)} %pack_far.1), channel_id=1, source_target_pairs={{0,2},{2,4},{3,1},{4,6},{5,3},{6,8},{7,5},{8,10},{9,7},{10,12},{11... | collective-permute-start | bytes 1572872 | tf_op jit(solution)/shard_map/ppermute | solution.py:329
  21.9 20.7 %collective-permute-start.5 = (f32[3,256,128]{2,1,0:T(8,128)S(1)}, f32[3,256,128]{2,1,0:T(8,128)S(1)}, u32[]{:S(2)}, u32[]{:S(2)}) collective-permute-start(f32[3,256,128]{2,1,0:T(8,128)S(1)} %get-tuple-element.45), channel_id=1, source_target_pairs={{1,2},{2,1},{3,4},{4,3},{5,6},{6,5},{7,8},{8,7},{9,10},{10,9},{11,... | collective-permute-start | bytes 1179656 | tf_op jit(solution)/shard_map/ppermute | solution.py:329
  38.6 17.3 %collective-permute-start.6 = (f32[2,512,128]{2,1,0:T(8,128)S(1)}, f32[2,512,128]{2,1,0:T(8,128)S(1)}, u32[]{:S(2)}, u32[]{:S(2)}) collective-permute-start(f32[2,512,128]{2,1,0:T(8,128)S(1)} %get-tuple-element.49.refs_8_), channel_id=1, source_target_pairs={{0,1},{1,0},{2,3},{3,2},{4,5},{5,4},{6,7},{7,6},{8,9},{9,8},{10,11... | collective-permute-start | bytes 1572872 | tf_op jit(solution)/shard_map/ppermute | solution.py:329
  45.0 30.6 %collective-permute-start.8 = (f32[2,512,128]{2,1,0:T(8,128)S(1)}, f32[2,512,128]{2,1,0:T(8,128)S(1)}, u32[]{:S(2)}, u32[]{:S(2)}) collective-permute-start(f32[2,512,128]{2,1,0:T(8,128)S(1)} %get-tuple-element.60), channel_id=1, source_target_pairs={{0,1},{1,0},{2,3},{3,2},{4,5},{5,4},{6,7},{7,6},{8,9},{9,8},{10,11... | collective-permute-start | bytes 1572872 | tf_op jit(solution)/shard_map/ppermute | solution.py:329
  46.9 32.2 %collective-permute-start.10 = (f32[3,512,128]{2,1,0:T(8,128)S(1)}, f32[3,512,128]{2,1,0:T(8,128)S(1)}, u32[]{:S(2)}, u32[]{:S(2)}) collective-permute-start(f32[3,512,128]{2,1,0:T(8,128)S(1)} %get-tuple-element.62), channel_id=1, source_target_pairs={{33,64},{35,66},{37,68},{39,70},{41,72},{43,74},{45,76},{47,78},{4... | collective-permute-start | bytes 2359304 | tf_op jit(solution)/shard_map/ppermute | solution.py:329
  55.9 23.2 %collective-permute-start.9 = (f32[3,512,128]{2,1,0:T(8,128)S(1)}, f32[3,512,128]{2,1,0:T(8,128)S(1)}, u32[]{:S(2)}, u32[]{:S(2)}) collective-permute-start(f32[3,512,128]{2,1,0:T(8,128)S(1)} %get-tuple-element.61), channel_id=1, source_target_pairs={{1,33},{3,35},{5,37},{7,39},{9,41},{11,43},{13,45},{15,47},{17,49}... | collective-permute-start | bytes 2359304 | tf_op jit(solution)/shard_map/ppermute | solution.py:329
  58.6 3.2 %collective-permute-start.7 = (f32[2,128,128]{2,1,0:T(8,128)S(1)}, f32[2,128,128]{2,1,0:T(8,128)S(1)}, u32[]{:S(2)}, u32[]{:S(2)}) collective-permute-start(f32[2,128,128]{2,1,0:T(8,128)S(1)} %get-tuple-element.52), channel_id=1, source_target_pairs={{0,32},{1,33},{2,34},{3,35},{4,36},{5,37},{6,38},{7,39},{8,40},{9,... | collective-permute-start | bytes 393224 | tf_op jit(solution)/shard_map/ppermute | solution.py:329
  64.4 14.7 %collective-permute-start.11 = (f32[2,512,128]{2,1,0:T(8,128)S(1)}, f32[2,512,128]{2,1,0:T(8,128)S(1)}, u32[]{:S(2)}, u32[]{:S(2)}) collective-permute-start(f32[2,512,128]{2,1,0:T(8,128)S(1)} %collective-permute-done.6.got_0), channel_id=1, source_target_pairs={{0,32},{2,34},{4,36},{6,38},{8,40},{10,42},{12,44},{14,46},{16,48}... | collective-permute-start | bytes 1572872 | tf_op jit(solution)/shard_map/ppermute | solution.py:329
  75.6 3.5 %collective-permute-start.12 = (f32[1,512,128]{2,1,0:T(8,128)S(1)}, f32[1,512,128]{2,1,0:T(8,128)S(1)}, u32[]{:S(2)}, u32[]{:S(2)}) collective-permute-start(f32[1,512,128]{2,1,0:T(8,128)S(1)} %slice.4), channel_id=1, source_target_pairs={{0,32},{2,34},{4,36},{6,38},{8,40},{10,42},{12,44},{14,46},{16,48}... | collective-permute-start | bytes 786440 | tf_op jit(solution)/shard_map/ppermute | solution.py:329

commit v6 on v5

--- a/solution.py
+++ b/solution.py
@@ -46,10 +46,6 @@
 
 def far_z(x, h, k, z, l):
     return x, h, k, z + (-1 if l else 1), l
-
-
-def far_direct(x, h, k, z, l):
-    return x, h, k, z + (1 if l else -1), 1 - l
 
 
 def mats_across(size, x, h, k, z, l):
@@ -124,11 +120,13 @@
     run_copies(copies, sems)
 
 
-def pack_rest(cov, second, third, sems):
-    l = side()
-    at = rows_of(1 - l, 1)
-    copies = [(cov.at[rows(at, 256)], second)]
-    run_copies(copies + [(cov.at[rows(at, 256), lanes(l + i)], third.at[i]) for i in range(3)], sems)
+def pack_swap(cov, out, sems):
+    run_copies([(cov.at[rows(rows_of(1 - side(), 1), 256)], out)], sems)
+
+
+def pack_halo(pair, out, sems):
+    l = side()
+    run_copies([(pair.at[:, lanes(1 - l + i)], out.at[i]) for i in range(3)], sems)
 
 
 def pack_far(pair, across, out, sems):
@@ -339,11 +337,11 @@
     across = send(out_across, functools.partial(mats_across, x_size))
     near = send(out_near, near_z)
     covariance, out_across = lax.optimization_barrier((covariance, out_across))
-    out_1, out_far_1 = pack(pack_rest, (shaped(256, 512), piece(3)), 1, 4, "pack_rest")(covariance)
+    out_1 = pack(pack_swap, shaped(256, 512), 1, 1, "pack_swap")(covariance)
     pair_1 = send(out_1, swap_y)
     out_far_0 = pack(pack_far, piece(4), 2, 5, "pack_far")(pair_0, across)
     far_0 = send(out_far_0, far_z)
-    far_1 = send(out_far_1, far_direct)
+    out_far_1 = pack(pack_halo, piece(3), 1, 3, "pack_halo")(pair_1)
 
     weight = shaped(8, 256, 256, dtype=BF16)
     ends = shaped(4, 256, 256, dtype=BF16)
@@ -352,7 +350,8 @@
         prepare_b, (weight, shaped(144)), [SMEM] * 3 + [VMEM] * 2, (VMEM, SMEM), prep_scratch, 10**3,
         "prepare_b",
     )(table, winds, barriers, across, mix_b)
-    weights_b, far_0, pair_1 = lax.optimization_barrier((weights_b, far_0, pair_1))
+    far_1 = send(out_far_1, far_z)
+    weights_b, far_0, out_far_1 = lax.optimization_barrier((weights_b, far_0, out_far_1))
     block = shaped(2, 512, LEV)
     field = pltpu.VMEM((WINDOW, 256, LEV), F32)
     kept_0, sent_0, ends_b = call(

time: 84.5 us -> 82.9 us (0.981)
  the two profiles are of different devices: /device:TPU:233 before, /device:TPU:105 now
where the time goes in v6:
time: 82.9 us; the launch traced here: 82.4 us
  starting transfers between devices  37.3 us (45%)
  waiting for transfers between devices  27.3 us (33%)
  Pallas kernels  15.9 us (19%)
  local copies, waits for them, and re-layouts  1.64 us (2%)
    ppermute x13, starting transfers between devices, per_device(): lax.ppermute(value, AXES, pairs(move, x_size, z_size))  37.3 us
    ppermute x13, waiting for transfers between devices, per_device(): lax.ppermute(value, AXES, pairs(move, x_size, z_size))  27.3 us
    pallas_call x1, Pallas kernels, per_device(): call(sweep_a, shaped(512, 1024), [SMEM] + [VMEM] * 7 + [ANY] * 3, VMEM, [...  4.9 us
    pallas_call x1, Pallas kernels, per_device(): call(prepare_a, (weight, ends, shaped(144)), [SMEM] * 3 + [VMEM] * 3, (VM...  2.61 us
    pallas_call x1, Pallas kernels, per_device(): call(prepare_b, (weight, shaped(144)), [SMEM] * 3 + [VMEM] * 2, (VMEM, SM...  2.46 us
    pallas_call x1, Pallas kernels, per_device(): call(functools.partial(sweep_b, 1), (block, block, shaped(3, 512, LEV), s...  2.34 us
    pallas_call x1, Pallas kernels, per_device(): call(functools.partial(sweep_b, 0), (block, block, ends), [SMEM] + [VMEM]...  2.32 us
  transfers between devices with their start and end apart: 13, of which 8 were waited for; matrix products, arithmetic and copies ran while one was open for 0% of the time, Pallas kernels for 13%

profile of v6, /device:TPU:105, one launch (start us, length us, event | category | flops | bytes accessed | tf_op | source)
XLA Modules:
  0.0 82.4 jit_solution(6457290610731507142)
XLA Ops:
  0.0 1.6 %copy-done = f32[1024,512]{1,0:T(8,128)S(1)} copy-done((f32[1024,512]{1,0:T(8,128)S(1)}, f32[1024,512]{1,0:T(8,128)}, u32[]{:S(2)}) %copy-start) | copy-done | bytes 2097176
  1.6 2.2 %collective-permute-start.1 = (f32[256,512]{1,0:T(8,128)S(1)}, f32[256,512]{1,0:T(8,128)S(1)}, u32[]{:S(2)}, u32[]{:S(2)}) collective-permute-start(f32[256,512]{1,0:T(8,128)S(1)} %pack_first.1), channel_id=1, source_target_pairs={{0,1},{1,0},{2,3},{3,2},{4,5},{5,4},{6,7},{7,6},{8,9},{9,8},{10,11... | collective-permute-start | bytes 1572872 | tf_op jit(solution)/shard_map/ppermute | solution.py:327
  4.7 5.0 %collective-permute-start = (f32[6,128,128]{2,1,0:T(8,128)S(1)}, f32[6,128,128]{2,1,0:T(8,128)S(1)}, u32[]{:S(2)}, u32[]{:S(2)}) collective-permute-start(f32[6,128,128]{2,1,0:T(8,128)S(1)} %get-tuple-element.34), channel_id=1, source_target_pairs={{0,481},{1,480},{2,483},{3,482},{4,485},{5,484},{6,487},{7,486},{8... | collective-permute-start | bytes 1179656 | tf_op jit(solution)/shard_map/ppermute | solution.py:327
  9.7 4.8 %collective-permute-start.4 = (f32[7,256,128]{2,1,0:T(8,128)S(1)}, f32[7,256,128]{2,1,0:T(8,128)S(1)}, u32[]{:S(2)}, u32[]{:S(2)}) collective-permute-start(f32[7,256,128]{2,1,0:T(8,128)S(1)} %get-tuple-element.39), channel_id=1, source_target_pairs={{1,3},{2,0},{3,5},{4,2},{5,7},{6,4},{7,9},{8,6},{9,11},{10,8},{11,... | collective-permute-start | bytes 2752520 | tf_op jit(solution)/shard_map/ppermute | solution.py:327
  14.6 2.1 %collective-permute-start.3 = (f32[256,512]{1,0:T(8,128)S(1)}, f32[256,512]{1,0:T(8,128)S(1)}, u32[]{:S(2)}, u32[]{:S(2)}) collective-permute-start(f32[256,512]{1,0:T(8,128)S(1)} %pack_swap.1), channel_id=1, source_target_pairs={{0,1},{1,0},{2,3},{3,2},{4,5},{5,4},{6,7},{7,6},{8,9},{9,8},{10,11... | collective-permute-start | bytes 1572872 | tf_op jit(solution)/shard_map/ppermute | solution.py:327
  16.6 3.0 %collective-permute-done.across = f32[6,128,128]{2,1,0:T(8,128)S(1)} collective-permute-done((f32[6,128,128]{2,1,0:T(8,128)S(1)}, f32[6,128,128]{2,1,0:T(8,128)S(1)}, u32[]{:S(2)}, u32[]{:S(2)}) %collective-permute-start) | collective-permute-done | bytes 393248 | tf_op jit(solution)/shard_map/ppermute | solution.py:327
  20.0 1.9 %collective-permute-start.2 = (f32[4,256,128]{2,1,0:T(8,128)S(1)}, f32[4,256,128]{2,1,0:T(8,128)S(1)}, u32[]{:S(2)}, u32[]{:S(2)}) collective-permute-start(f32[4,256,128]{2,1,0:T(8,128)S(1)} %pack_far.1), channel_id=1, source_target_pairs={{0,2},{2,4},{3,1},{4,6},{5,3},{6,8},{7,5},{8,10},{9,7},{10,12},{11... | collective-permute-start | bytes 1572872 | tf_op jit(solution)/shard_map/ppermute | solution.py:327
  21.9 2.5 %prepare_b.1 = (bf16[8,256,256]{2,1,0:T(8,128)(2,1)S(1)}, f32[144]{0:T(256)S(1)}) custom-call(f32[8,128]{1,0:T(8,128)S(1)} %copy-done.4, s32[2,3]{1,0:T(2,128)S(1)} %copy-done.5, s32[4]{0:T(128)S(1)} %copy-done.6, f32[6,128,128]{2,1,0:T(8,128)S(1)} %collective-permute-done.across, f32[4,128,128]{2,1,0:T(8,128)S(1)} %copy-done.3), custom_call_target="tpu_custom_call" | custom-call | flops 1000 | bytes 1024 | tf_op jit(solution)/shard_map/prepare_b/pallas_call | solution.py:349
  24.4 3.6 %collective-permute-done.3.pair.refs_3_ = f32[256,512]{1,0:T(8,128)S(1)} collective-permute-done((f32[256,512]{1,0:T(8,128)S(1)}, f32[256,512]{1,0:T(8,128)S(1)}, u32[]{:S(2)}, u32[]{:S(2)}) %collective-permute-start.3) | collective-permute-done | bytes 524320 | tf_op jit(solution)/shard_map/ppermute | solution.py:327
  28.1 1.9 %collective-permute-start.5 = (f32[3,256,128]{2,1,0:T(8,128)S(1)}, f32[3,256,128]{2,1,0:T(8,128)S(1)}, u32[]{:S(2)}, u32[]{:S(2)}) collective-permute-start(f32[3,256,128]{2,1,0:T(8,128)S(1)} %pack_halo.1), channel_id=1, source_target_pairs={{0,2},{2,4},{3,1},{4,6},{5,3},{6,8},{7,5},{8,10},{9,7},{10,12},{11... | collective-permute-start | bytes 1179656 | tf_op jit(solution)/shard_map/ppermute | solution.py:327
  30.0 6.2 %collective-permute-done.2.refs_5_ = f32[4,256,128]{2,1,0:T(8,128)S(1)} collective-permute-done((f32[4,256,128]{2,1,0:T(8,128)S(1)}, f32[4,256,128]{2,1,0:T(8,128)S(1)}, u32[]{:S(2)}, u32[]{:S(2)}) %collective-permute-start.2) | collective-permute-done | bytes 524320 | tf_op jit(solution)/shard_map/ppermute | solution.py:327
  36.2 2.3 %sweep_b0.1 = (f32[2,512,128]{2,1,0:T(8,128)S(1)}, f32[2,512,128]{2,1,0:T(8,128)S(1)}, bf16[4,256,256]{2,1,0:T(8,128)(2,1)S(1)}) custom-call(f32[144]{0:T(256)S(1)} %get-tuple-element.35.refs_0_, bf16[8,256,256]{2,1,0:T(8,128)(2,1)S(1)} %get-tuple-element.38.refs_1_, f32[1024,512]{1,0:T(8,128)S(1)} %copy-done.1, ...), custom_call_target="tpu_custom_call" | custom-call | flops 4000000000 | bytes 1024 | tf_op jit(solution)/shard_map/sweep_b0/pallas_call | solution.py:357
  38.5 3.1 %collective-permute-start.6 = (f32[2,512,128]{2,1,0:T(8,128)S(1)}, f32[2,512,128]{2,1,0:T(8,128)S(1)}, u32[]{:S(2)}, u32[]{:S(2)}) collective-permute-start(f32[2,512,128]{2,1,0:T(8,128)S(1)} %get-tuple-element.43.refs_8_), channel_id=1, source_target_pairs={{0,1},{1,0},{2,3},{3,2},{4,5},{5,4},{6,7},{7,6},{8,9},{9,8},{10,11... | collective-permute-start | bytes 1572872 | tf_op jit(solution)/shard_map/ppermute | solution.py:327
  41.6 2.4 %collective-permute-done.5.refs_5_ = f32[3,256,128]{2,1,0:T(8,128)S(1)} collective-permute-done((f32[3,256,128]{2,1,0:T(8,128)S(1)}, f32[3,256,128]{2,1,0:T(8,128)S(1)}, u32[]{:S(2)}, u32[]{:S(2)}) %collective-permute-start.5) | collective-permute-done | bytes 393248 | tf_op jit(solution)/shard_map/ppermute | solution.py:327
  44.0 2.3 %sweep_b1.1 = (f32[2,512,128]{2,1,0:T(8,128)S(1)}, f32[2,512,128]{2,1,0:T(8,128)S(1)}, f32[3,512,128]{2,1,0:T(8,128)S(1)}, f32[3,512,128]{2,1,0:T(8,128)S(1)}) custom-call(f32[144]{0:T(256)S(1)} %get-tuple-element.35.refs_0_, bf16[8,256,256]{2,1,0:T(8,128)(2,1)S(1)} %get-tuple-element.38.refs_1_, f32[1024,512]{1,0:T(8,128)S(1)} %copy-done.1, ...), custom_call_target="tpu_custom_call" | custom-call | flops 4000000000 | bytes 1024 | tf_op jit(solution)/shard_map/sweep_b1/pallas_call | solution.py:362
  46.4 3.3 %collective-permute-start.8 = (f32[2,512,128]{2,1,0:T(8,128)S(1)}, f32[2,512,128]{2,1,0:T(8,128)S(1)}, u32[]{:S(2)}, u32[]{:S(2)}) collective-permute-start(f32[2,512,128]{2,1,0:T(8,128)S(1)} %get-tuple-element.54), channel_id=1, source_target_pairs={{0,1},{1,0},{2,3},{3,2},{4,5},{5,4},{6,7},{7,6},{8,9},{9,8},{10,11... | collective-permute-start | bytes 1572872 | tf_op jit(solution)/shard_map/ppermute | solution.py:327
  49.7 3.4 %collective-permute-start.10 = (f32[3,512,128]{2,1,0:T(8,128)S(1)}, f32[3,512,128]{2,1,0:T(8,128)S(1)}, u32[]{:S(2)}, u32[]{:S(2)}) collective-permute-start(f32[3,512,128]{2,1,0:T(8,128)S(1)} %get-tuple-element.56), channel_id=1, source_target_pairs={{33,64},{35,66},{37,68},{39,70},{41,72},{43,74},{45,76},{47,78},{4... | collective-permute-start | bytes 2359304 | tf_op jit(solution)/shard_map/ppermute | solution.py:327
  54.0 2.9 %collective-permute-start.9 = (f32[3,512,128]{2,1,0:T(8,128)S(1)}, f32[3,512,128]{2,1,0:T(8,128)S(1)}, u32[]{:S(2)}, u32[]{:S(2)}) collective-permute-start(f32[3,512,128]{2,1,0:T(8,128)S(1)} %get-tuple-element.55), channel_id=1, source_target_pairs={{1,33},{3,35},{5,37},{7,39},{9,41},{11,43},{13,45},{15,47},{17,49}... | collective-permute-start | bytes 2359304 | tf_op jit(solution)/shard_map/ppermute | solution.py:327
  56.9 1.9 %collective-permute-start.7 = (f32[2,128,128]{2,1,0:T(8,128)S(1)}, f32[2,128,128]{2,1,0:T(8,128)S(1)}, u32[]{:S(2)}, u32[]{:S(2)}) collective-permute-start(f32[2,128,128]{2,1,0:T(8,128)S(1)} %get-tuple-element.46), channel_id=1, source_target_pairs={{0,32},{1,33},{2,34},{3,35},{4,36},{5,37},{6,38},{7,39},{8,40},{9,... | collective-permute-start | bytes 393224 | tf_op jit(solution)/shard_map/ppermute | solution.py:327
  60.1 2.6 %prepare_a.1 = (bf16[8,256,256]{2,1,0:T(8,128)(2,1)S(1)}, bf16[4,256,256]{2,1,0:T(8,128)(2,1)S(1)}, f32[144]{0:T(256)S(1)}) custom-call(f32[8,128]{1,0:T(8,128)S(1)} %copy-done.4, s32[2,3]{1,0:T(2,128)S(1)} %copy-done.5, s32[4]{0:T(128)S(1)} %copy-done.6, f32[8,128,128]{2,1,0:T(8,128)S(1)} %copy-done.2, f32[6,128,128]{2,1,0:T(8,128)S(1)} %collective-permute-done.across, ...), custom_call_target="tpu_custom_call" | custom-call | flops 1000 | bytes 1024 | tf_op jit(solution)/shard_map/prepare_a/pallas_call | solution.py:372
  62.7 2.1 %collective-permute-start.11 = (f32[2,512,128]{2,1,0:T(8,128)S(1)}, f32[2,512,128]{2,1,0:T(8,128)S(1)}, u32[]{:S(2)}, u32[]{:S(2)}) collective-permute-start(f32[2,512,128]{2,1,0:T(8,128)S(1)} %collective-permute-done.6.got_0), channel_id=1, source_target_pairs={{0,32},{2,34},{4,36},{6,38},{8,40},{10,42},{12,44},{14,46},{16,48}... | collective-permute-start | bytes 1572872 | tf_op jit(solution)/shard_map/ppermute | solution.py:327
  64.8 8.8 %collective-permute-done.8.got_1 = f32[2,512,128]{2,1,0:T(8,128)S(1)} collective-permute-done((f32[2,512,128]{2,1,0:T(8,128)S(1)}, f32[2,512,128]{2,1,0:T(8,128)S(1)}, u32[]{:S(2)}, u32[]{:S(2)}) %collective-permute-start.8) | collective-permute-done | bytes 524320 | tf_op jit(solution)/shard_map/ppermute | solution.py:327
  73.6 2.7 %collective-permute-start.12 = (f32[1,512,128]{2,1,0:T(8,128)S(1)}, f32[1,512,128]{2,1,0:T(8,128)S(1)}, u32[]{:S(2)}, u32[]{:S(2)}) collective-permute-start(f32[1,512,128]{2,1,0:T(8,128)S(1)} %slice.4), channel_id=1, source_target_pairs={{0,32},{2,34},{4,36},{6,38},{8,40},{10,42},{12,44},{14,46},{16,48}... | collective-permute-start | bytes 786440 | tf_op jit(solution)/shard_map/ppermute | solution.py:327
  77.5 4.9 %sweep_a.1 = f32[512,1024]{1,0:T(8,128)} custom-call(f32[144]{0:T(256)S(1)} %get-tuple-element.47.coef, bf16[8,256,256]{2,1,0:T(8,128)(2,1)S(1)} %get-tuple-element.50.weights, bf16[4,256,256]{2,1,0:T(8,128)(2,1)S(1)} %get-tuple-element.51.ends, f32[2,512,128]{2,1,0:T(8,128)S(1)} %get-tuple-element.42.refs_7_.kept_0, ...), custom_call_target="tpu_custom_call" | custom-call | flops 4000 | bytes 1024 | tf_op jit(solution)/shard_map/sweep_a/pallas_call | solution.py:381
  (27 shorter events, 4.6 us)
Async XLA Ops:
  0.0 1.6 %copy-start = (f32[1024,512]{1,0:T(8,128)S(1)}, f32[1024,512]{1,0:T(8,128)}, u32[]{:S(2)}) copy-start(f32[1024,512]{1,0:T(8,128)} %refs_2_.1) | copy-start | bytes 6291460
  1.6 2.3 %copy-start.2 = (f32[8,128,128]{2,1,0:T(8,128)S(1)}, f32[8,128,128]{2,1,0:T(8,128)}, u32[]{:S(2)}) copy-start(f32[8,128,128]{2,1,0:T(8,128)} %own.1) | copy-start | bytes 1572868
  1.6 2.3 %copy-start.3 = (f32[4,128,128]{2,1,0:T(8,128)S(1)}, f32[4,128,128]{2,1,0:T(8,128)}, u32[]{:S(2)}) copy-start(f32[4,128,128]{2,1,0:T(8,128)} %own) | copy-start | bytes 786436
  1.6 18.0 %collective-permute-start.1 = (f32[256,512]{1,0:T(8,128)S(1)}, f32[256,512]{1,0:T(8,128)S(1)}, u32[]{:S(2)}, u32[]{:S(2)}) collective-permute-start(f32[256,512]{1,0:T(8,128)S(1)} %pack_first.1), channel_id=1, source_target_pairs={{0,1},{1,0},{2,3},{3,2},{4,5},{5,4},{6,7},{7,6},{8,9},{9,8},{10,11... | collective-permute-start | bytes 1572872 | tf_op jit(solution)/shard_map/ppermute | solution.py:327
  4.7 17.2 %copy-start.4 = (f32[8,128]{1,0:T(8,128)S(1)}, f32[8,128]{1,0:T(8,128)}, u32[]{:S(2)}) copy-start(f32[8,128]{1,0:T(8,128)} %table.3) | copy-start | bytes 12292
  4.7 17.2 %copy-start.5 = (s32[2,3]{1,0:T(2,128)S(1)}, s32[2,3]{1,0:T(2,128)}, u32[]{:S(2)}) copy-start(s32[2,3]{1,0:T(2,128)} %winds.3) | copy-start | bytes 76
  4.7 17.2 %copy-start.6 = (s32[4]{0:T(128)S(1)}, s32[4]{0:T(128)}, u32[]{:S(2)}) copy-start(s32[4]{0:T(128)} %barriers.3) | copy-start | bytes 52
  4.7 15.0 %collective-permute-start = (f32[6,128,128]{2,1,0:T(8,128)S(1)}, f32[6,128,128]{2,1,0:T(8,128)S(1)}, u32[]{:S(2)}, u32[]{:S(2)}) collective-permute-start(f32[6,128,128]{2,1,0:T(8,128)S(1)} %get-tuple-element.34), channel_id=1, source_target_pairs={{0,481},{1,480},{2,483},{3,482},{4,485},{5,484},{6,487},{7,486},{8... | collective-permute-start | bytes 1179656 | tf_op jit(solution)/shard_map/ppermute | solution.py:327
  9.7 26.5 %collective-permute-start.4 = (f32[7,256,128]{2,1,0:T(8,128)S(1)}, f32[7,256,128]{2,1,0:T(8,128)S(1)}, u32[]{:S(2)}, u32[]{:S(2)}) collective-permute-start(f32[7,256,128]{2,1,0:T(8,128)S(1)} %get-tuple-element.39), channel_id=1, source_target_pairs={{1,3},{2,0},{3,5},{4,2},{5,7},{6,4},{7,9},{8,6},{9,11},{10,8},{11,... | collective-permute-start | bytes 2752520 | tf_op jit(solution)/shard_map/ppermute | solution.py:327
  14.6 21.6 %copy-start.1 = (f32[1024,512]{1,0:T(8,128)S(1)}, f32[1024,512]{1,0:T(8,128)}, u32[]{:S(2)}) copy-start(f32[1024,512]{1,0:T(8,128)} %refs_2_.1) | copy-start | bytes 6291460
  14.6 13.4 %collective-permute-start.3 = (f32[256,512]{1,0:T(8,128)S(1)}, f32[256,512]{1,0:T(8,128)S(1)}, u32[]{:S(2)}, u32[]{:S(2)}) collective-permute-start(f32[256,512]{1,0:T(8,128)S(1)} %pack_swap.1), channel_id=1, source_target_pairs={{0,1},{1,0},{2,3},{3,2},{4,5},{5,4},{6,7},{7,6},{8,9},{9,8},{10,11... | collective-permute-start | bytes 1572872 | tf_op jit(solution)/shard_map/ppermute | solution.py:327
  20.0 16.2 %collective-permute-start.2 = (f32[4,256,128]{2,1,0:T(8,128)S(1)}, f32[4,256,128]{2,1,0:T(8,128)S(1)}, u32[]{:S(2)}, u32[]{:S(2)}) collective-permute-start(f32[4,256,128]{2,1,0:T(8,128)S(1)} %pack_far.1), channel_id=1, source_target_pairs={{0,2},{2,4},{3,1},{4,6},{5,3},{6,8},{7,5},{8,10},{9,7},{10,12},{11... | collective-permute-start | bytes 1572872 | tf_op jit(solution)/shard_map/ppermute | solution.py:327
  28.1 16.0 %collective-permute-start.5 = (f32[3,256,128]{2,1,0:T(8,128)S(1)}, f32[3,256,128]{2,1,0:T(8,128)S(1)}, u32[]{:S(2)}, u32[]{:S(2)}) collective-permute-start(f32[3,256,128]{2,1,0:T(8,128)S(1)} %pack_halo.1), channel_id=1, source_target_pairs={{0,2},{2,4},{3,1},{4,6},{5,3},{6,8},{7,5},{8,10},{9,7},{10,12},{11... | collective-permute-start | bytes 1179656 | tf_op jit(solution)/shard_map/ppermute | solution.py:327
  38.5 15.4 %collective-permute-start.6 = (f32[2,512,128]{2,1,0:T(8,128)S(1)}, f32[2,512,128]{2,1,0:T(8,128)S(1)}, u32[]{:S(2)}, u32[]{:S(2)}) collective-permute-start(f32[2,512,128]{2,1,0:T(8,128)S(1)} %get-tuple-element.43.refs_8_), channel_id=1, source_target_pairs={{0,1},{1,0},{2,3},{3,2},{4,5},{5,4},{6,7},{7,6},{8,9},{9,8},{10,11... | collective-permute-start | bytes 1572872 | tf_op jit(solution)/shard_map/ppermute | solution.py:327
  46.4 27.2 %collective-permute-start.8 = (f32[2,512,128]{2,1,0:T(8,128)S(1)}, f32[2,512,128]{2,1,0:T(8,128)S(1)}, u32[]{:S(2)}, u32[]{:S(2)}) collective-permute-start(f32[2,512,128]{2,1,0:T(8,128)S(1)} %get-tuple-element.54), channel_id=1, source_target_pairs={{0,1},{1,0},{2,3},{3,2},{4,5},{5,4},{6,7},{7,6},{8,9},{9,8},{10,11... | collective-permute-start | bytes 1572872 | tf_op jit(solution)/shard_map/ppermute | solution.py:327
  49.7 27.8 %collective-permute-start.10 = (f32[3,512,128]{2,1,0:T(8,128)S(1)}, f32[3,512,128]{2,1,0:T(8,128)S(1)}, u32[]{:S(2)}, u32[]{:S(2)}) collective-permute-start(f32[3,512,128]{2,1,0:T(8,128)S(1)} %get-tuple-element.56), channel_id=1, source_target_pairs={{33,64},{35,66},{37,68},{39,70},{41,72},{43,74},{45,76},{47,78},{4... | collective-permute-start | bytes 2359304 | tf_op jit(solution)/shard_map/ppermute | solution.py:327
  54.0 23.6 %collective-permute-start.9 = (f32[3,512,128]{2,1,0:T(8,128)S(1)}, f32[3,512,128]{2,1,0:T(8,128)S(1)}, u32[]{:S(2)}, u32[]{:S(2)}) collective-permute-start(f32[3,512,128]{2,1,0:T(8,128)S(1)} %get-tuple-element.55), channel_id=1, source_target_pairs={{1,33},{3,35},{5,37},{7,39},{9,41},{11,43},{13,45},{15,47},{17,49}... | collective-permute-start | bytes 2359304 | tf_op jit(solution)/shard_map/ppermute | solution.py:327
  56.9 3.2 %collective-permute-start.7 = (f32[2,128,128]{2,1,0:T(8,128)S(1)}, f32[2,128,128]{2,1,0:T(8,128)S(1)}, u32[]{:S(2)}, u32[]{:S(2)}) collective-permute-start(f32[2,128,128]{2,1,0:T(8,128)S(1)} %get-tuple-element.46), channel_id=1, source_target_pairs={{0,32},{1,33},{2,34},{3,35},{4,36},{5,37},{6,38},{7,39},{8,40},{9,... | collective-permute-start | bytes 393224 | tf_op jit(solution)/shard_map/ppermute | solution.py:327
  62.7 14.8 %collective-permute-start.11 = (f32[2,512,128]{2,1,0:T(8,128)S(1)}, f32[2,512,128]{2,1,0:T(8,128)S(1)}, u32[]{:S(2)}, u32[]{:S(2)}) collective-permute-start(f32[2,512,128]{2,1,0:T(8,128)S(1)} %collective-permute-done.6.got_0), channel_id=1, source_target_pairs={{0,32},{2,34},{4,36},{6,38},{8,40},{10,42},{12,44},{14,46},{16,48}... | collective-permute-start | bytes 1572872 | tf_op jit(solution)/shard_map/ppermute | solution.py:327
  73.6 3.9 %collective-permute-start.12 = (f32[1,512,128]{2,1,0:T(8,128)S(1)}, f32[1,512,128]{2,1,0:T(8,128)S(1)}, u32[]{:S(2)}, u32[]{:S(2)}) collective-permute-start(f32[1,512,128]{2,1,0:T(8,128)S(1)} %slice.4), channel_id=1, source_target_pairs={{0,32},{2,34},{4,36},{6,38},{8,40},{10,42},{12,44},{14,46},{16,48}... | collective-permute-start | bytes 786440 | tf_op jit(solution)/shard_map/ppermute | solution.py:327

commit v7 on v6

--- a/solution.py
+++ b/solution.py
@@ -129,12 +129,8 @@
     run_copies([(pair.at[:, lanes(1 - l + i)], out.at[i]) for i in range(3)], sems)
 
 
-def pack_far(pair, across, out, sems):
-    l = side()
-    copies = [(pair.at[:, lanes(1 - l + i)], out.at[i]) for i in range(3)]
-    for m in range(2):
-        copies.append((across.at[2 - 2 * l + m], out.at[3, pl.ds(m * LEV, LEV)]))
-    run_copies(copies, sems)
+def pack_edge(across, out, sems):
+    run_copies([(across.at[pl.ds(2 - 2 * side(), 2)], out)], sems)
 
 
 def write_coefficients(l, base, tracer, table, winds, barriers, coef, flow):
@@ -218,7 +214,7 @@
 
 def sweep_b(chunk, *refs):
     if chunk == 0:
-        coef, weights, cov, pair, near, far, kept, sent, ends, window, other = refs
+        coef, weights, cov, pair, near, far, edge, kept, sent, ends, window, other = refs
     else:
         (coef, weights, cov, pair, near, far, ends, kept_before, sent_before,
          kept, sent, same, cross, window, other, late) = refs
@@ -235,9 +231,9 @@
 
     if chunk == 0:
         for q in range(2):
-            at = rows(turned(l, q, 2) * LEV, LEV)
-            write_weight(ends, q, near[6, at, :])
-            write_weight(ends, 2 + q, far[3, at, :])
+            m = turned(l, q, 2)
+            write_weight(ends, q, near[6, rows(m * LEV, LEV), :])
+            write_weight(ends, 2 + q, edge[m])
     first_steps(source, window, other, weights, ends, coef)
 
     def finish(p, target, q):
@@ -339,9 +335,9 @@
     covariance, out_across = lax.optimization_barrier((covariance, out_across))
     out_1 = pack(pack_swap, shaped(256, 512), 1, 1, "pack_swap")(covariance)
     pair_1 = send(out_1, swap_y)
-    out_far_0 = pack(pack_far, piece(4), 2, 5, "pack_far")(pair_0, across)
-    far_0 = send(out_far_0, far_z)
-    out_far_1 = pack(pack_halo, piece(3), 1, 3, "pack_halo")(pair_1)
+    pair_0, across = lax.optimization_barrier((pair_0, across))
+    far_0 = send(pack(pack_halo, piece(3), 1, 3, "pack_halo")(pair_0), far_z)
+    edge_far = send(pack(pack_edge, shaped(2, LEV, LEV), 1, 1, "pack_edge")(across), far_z)
 
     weight = shaped(8, 256, 256, dtype=BF16)
     ends = shaped(4, 256, 256, dtype=BF16)
@@ -350,14 +346,16 @@
         prepare_b, (weight, shaped(144)), [SMEM] * 3 + [VMEM] * 2, (VMEM, SMEM), prep_scratch, 10**3,
         "prepare_b",
     )(table, winds, barriers, across, mix_b)
+    pair_1, weights_b = lax.optimization_barrier((pair_1, weights_b))
+    out_far_1 = pack(pack_halo, piece(3), 1, 3, "pack_halo")(pair_1)
     far_1 = send(out_far_1, far_z)
     weights_b, far_0, out_far_1 = lax.optimization_barrier((weights_b, far_0, out_far_1))
     block = shaped(2, 512, LEV)
     field = pltpu.VMEM((WINDOW, 256, LEV), F32)
     kept_0, sent_0, ends_b = call(
-        functools.partial(sweep_b, 0), (block, block, ends), [SMEM] + [VMEM] * 5, (VMEM,) * 3,
+        functools.partial(sweep_b, 0), (block, block, ends), [SMEM] + [VMEM] * 6, (VMEM,) * 3,
         [field, field], COST, "sweep_b0",
-    )(coef_b, weights_b, covariance, pair_0, near, far_0)
+    )(coef_b, weights_b, covariance, pair_0, near, far_0, edge_far)
     got_0 = send(sent_0, swap_y)
     kept_1, sent_1, out_same, out_cross = call(
         functools.partial(sweep_b, 1), (block, block, shaped(3, 512, LEV), shaped(3, 512, LEV)),

time: 82.9 us -> 86.9 us (1.048)
  the two profiles are of different devices: /device:TPU:105 before, /device:TPU:393 now
where the time goes in v7:
time: 86.9 us; the launch traced here: 86.4 us
  starting transfers between devices  42.2 us (49%)
  waiting for transfers between devices  26.3 us (30%)
  Pallas kernels  15.9 us (18%)
  local copies, waits for them, and re-layouts  1.64 us (2%)
    ppermute x14, starting transfers between devices, per_device(): lax.ppermute(value, AXES, pairs(move, x_size, z_size))  42.2 us
    ppermute x14, waiting for transfers between devices, per_device(): lax.ppermute(value, AXES, pairs(move, x_size, z_size))  26.3 us
    pallas_call x1, Pallas kernels, per_device(): call(sweep_a, shaped(512, 1024), [SMEM] + [VMEM] * 7 + [ANY] * 3, VMEM, [...  4.9 us
    pallas_call x1, Pallas kernels, per_device(): call(prepare_a, (weight, ends, shaped(144)), [SMEM] * 3 + [VMEM] * 3, (VM...  2.61 us
    pallas_call x1, Pallas kernels, per_device(): call(prepare_b, (weight, shaped(144)), [SMEM] * 3 + [VMEM] * 2, (VMEM, SM...  2.46 us
    pallas_call x1, Pallas kernels, per_device(): call(functools.partial(sweep_b, 1), (block, block, shaped(3, 512, LEV), s...  2.34 us
    pallas_call x1, Pallas kernels, per_device(): call(functools.partial(sweep_b, 0), (block, block, ends), [SMEM] + [VMEM]...  2.32 us
  transfers between devices with their start and end apart: 14, of which 7 were waited for; matrix products, arithmetic and copies ran while one was open for 0% of the time, Pallas kernels for 13%

profile of v7, /device:TPU:393, one launch (start us, length us, event | category | flops | bytes accessed | tf_op | source)
XLA Modules:
  0.0 86.4 jit_solution(13355975388141080229)
XLA Ops:
  0.0 1.6 %copy-done = f32[1024,512]{1,0:T(8,128)S(1)} copy-done((f32[1024,512]{1,0:T(8,128)S(1)}, f32[1024,512]{1,0:T(8,128)}, u32[]{:S(2)}) %copy-start) | copy-done | bytes 2097176
  1.6 2.2 %collective-permute-start = (f32[256,512]{1,0:T(8,128)S(1)}, f32[256,512]{1,0:T(8,128)S(1)}, u32[]{:S(2)}, u32[]{:S(2)}) collective-permute-start(f32[256,512]{1,0:T(8,128)S(1)} %pack_first.1), channel_id=1, source_target_pairs={{0,1},{1,0},{2,3},{3,2},{4,5},{5,4},{6,7},{7,6},{8,9},{9,8},{10,11... | collective-permute-start | bytes 1572872 | tf_op jit(solution)/shard_map/ppermute | solution.py:323
  4.7 2.8 %collective-permute-start.4 = (f32[7,256,128]{2,1,0:T(8,128)S(1)}, f32[7,256,128]{2,1,0:T(8,128)S(1)}, u32[]{:S(2)}, u32[]{:S(2)}) collective-permute-start(f32[7,256,128]{2,1,0:T(8,128)S(1)} %get-tuple-element.47), channel_id=1, source_target_pairs={{1,3},{2,0},{3,5},{4,2},{5,7},{6,4},{7,9},{8,6},{9,11},{10,8},{11,... | collective-permute-start | bytes 2752520 | tf_op jit(solution)/shard_map/ppermute | solution.py:323
  7.5 6.4 %collective-permute-start.1 = (f32[6,128,128]{2,1,0:T(8,128)S(1)}, f32[6,128,128]{2,1,0:T(8,128)S(1)}, u32[]{:S(2)}, u32[]{:S(2)}) collective-permute-start(f32[6,128,128]{2,1,0:T(8,128)S(1)} %get-tuple-element.38), channel_id=1, source_target_pairs={{0,481},{1,480},{2,483},{3,482},{4,485},{5,484},{6,487},{7,486},{8... | collective-permute-start | bytes 1179656 | tf_op jit(solution)/shard_map/ppermute | solution.py:323
  13.9 2.1 %collective-permute-start.2 = (f32[256,512]{1,0:T(8,128)S(1)}, f32[256,512]{1,0:T(8,128)S(1)}, u32[]{:S(2)}, u32[]{:S(2)}) collective-permute-start(f32[256,512]{1,0:T(8,128)S(1)} %pack_swap.1), channel_id=1, source_target_pairs={{0,1},{1,0},{2,3},{3,2},{4,5},{5,4},{6,7},{7,6},{8,9},{9,8},{10,11... | collective-permute-start | bytes 1572872 | tf_op jit(solution)/shard_map/ppermute | solution.py:323
  16.0 7.8 %collective-permute-done.1.across = f32[6,128,128]{2,1,0:T(8,128)S(1)} collective-permute-done((f32[6,128,128]{2,1,0:T(8,128)S(1)}, f32[6,128,128]{2,1,0:T(8,128)S(1)}, u32[]{:S(2)}, u32[]{:S(2)}) %collective-permute-start.1) | collective-permute-done | bytes 393248 | tf_op jit(solution)/shard_map/ppermute | solution.py:323
  23.9 2.6 %collective-permute-start.3 = (f32[3,256,128]{2,1,0:T(8,128)S(1)}, f32[3,256,128]{2,1,0:T(8,128)S(1)}, u32[]{:S(2)}, u32[]{:S(2)}) collective-permute-start(f32[3,256,128]{2,1,0:T(8,128)S(1)} %pack_halo.2), channel_id=1, source_target_pairs={{0,2},{2,4},{3,1},{4,6},{5,3},{6,8},{7,5},{8,10},{9,7},{10,12},{11... | collective-permute-start | bytes 1179656 | tf_op jit(solution)/shard_map/ppermute | solution.py:323
  26.8 2.6 %collective-permute-start.6 = (f32[2,128,128]{2,1,0:T(8,128)S(1)}, f32[2,128,128]{2,1,0:T(8,128)S(1)}, u32[]{:S(2)}, u32[]{:S(2)}) collective-permute-start(f32[2,128,128]{2,1,0:T(8,128)S(1)} %pack_edge.1), channel_id=1, source_target_pairs={{0,2},{2,4},{3,1},{4,6},{5,3},{6,8},{7,5},{8,10},{9,7},{10,12},{11... | collective-permute-start | bytes 393224 | tf_op jit(solution)/shard_map/ppermute | solution.py:323
  29.4 2.5 %prepare_b.1 = (bf16[8,256,256]{2,1,0:T(8,128)(2,1)S(1)}, f32[144]{0:T(256)S(1)}) custom-call(f32[8,128]{1,0:T(8,128)S(1)} %copy-done.4, s32[2,3]{1,0:T(2,128)S(1)} %copy-done.5, s32[4]{0:T(128)S(1)} %copy-done.6, f32[6,128,128]{2,1,0:T(8,128)S(1)} %collective-permute-done.1.across, f32[4,128,128]{2,1,0:T(8,128)S(1)} %copy-done.3), custom_call_target="tpu_custom_call" | custom-call | flops 1000 | bytes 1024 | tf_op jit(solution)/shard_map/prepare_b/pallas_call | solution.py:345
  32.0 2.6 %collective-permute-start.5 = (f32[3,256,128]{2,1,0:T(8,128)S(1)}, f32[3,256,128]{2,1,0:T(8,128)S(1)}, u32[]{:S(2)}, u32[]{:S(2)}) collective-permute-start(f32[3,256,128]{2,1,0:T(8,128)S(1)} %pack_halo.3), channel_id=1, source_target_pairs={{0,2},{2,4},{3,1},{4,6},{5,3},{6,8},{7,5},{8,10},{9,7},{10,12},{11... | collective-permute-start | bytes 1179656 | tf_op jit(solution)/shard_map/ppermute | solution.py:323
  36.2 2.8 %collective-permute-done.6.refs_6_ = f32[2,128,128]{2,1,0:T(8,128)S(1)} collective-permute-done((f32[2,128,128]{2,1,0:T(8,128)S(1)}, f32[2,128,128]{2,1,0:T(8,128)S(1)}, u32[]{:S(2)}, u32[]{:S(2)}) %collective-permute-start.6) | collective-permute-done | bytes 131104 | tf_op jit(solution)/shard_map/ppermute | solution.py:323
  39.0 2.3 %sweep_b0.1 = (f32[2,512,128]{2,1,0:T(8,128)S(1)}, f32[2,512,128]{2,1,0:T(8,128)S(1)}, bf16[4,256,256]{2,1,0:T(8,128)(2,1)S(1)}) custom-call(f32[144]{0:T(256)S(1)} %get-tuple-element.40.refs_0_, bf16[8,256,256]{2,1,0:T(8,128)(2,1)S(1)} %get-tuple-element.46.refs_1_, f32[1024,512]{1,0:T(8,128)S(1)} %copy-done.1, ...), custom_call_target="tpu_custom_call" | custom-call | flops 4000000000 | bytes 1024 | tf_op jit(solution)/shard_map/sweep_b0/pallas_call | solution.py:355
  41.4 4.5 %collective-permute-start.7 = (f32[2,512,128]{2,1,0:T(8,128)S(1)}, f32[2,512,128]{2,1,0:T(8,128)S(1)}, u32[]{:S(2)}, u32[]{:S(2)}) collective-permute-start(f32[2,512,128]{2,1,0:T(8,128)S(1)} %get-tuple-element.51.refs_8_), channel_id=1, source_target_pairs={{0,1},{1,0},{2,3},{3,2},{4,5},{5,4},{6,7},{7,6},{8,9},{9,8},{10,11... | collective-permute-start | bytes 1572872 | tf_op jit(solution)/shard_map/ppermute | solution.py:323
  45.9 2.3 %sweep_b1.1 = (f32[2,512,128]{2,1,0:T(8,128)S(1)}, f32[2,512,128]{2,1,0:T(8,128)S(1)}, f32[3,512,128]{2,1,0:T(8,128)S(1)}, f32[3,512,128]{2,1,0:T(8,128)S(1)}) custom-call(f32[144]{0:T(256)S(1)} %get-tuple-element.40.refs_0_, bf16[8,256,256]{2,1,0:T(8,128)(2,1)S(1)} %get-tuple-element.46.refs_1_, f32[1024,512]{1,0:T(8,128)S(1)} %copy-done.1, ...), custom_call_target="tpu_custom_call" | custom-call | flops 4000000000 | bytes 1024 | tf_op jit(solution)/shard_map/sweep_b1/pallas_call | solution.py:360
  48.3 5.5 %collective-permute-start.9 = (f32[2,512,128]{2,1,0:T(8,128)S(1)}, f32[2,512,128]{2,1,0:T(8,128)S(1)}, u32[]{:S(2)}, u32[]{:S(2)}) collective-permute-start(f32[2,512,128]{2,1,0:T(8,128)S(1)} %get-tuple-element.62), channel_id=1, source_target_pairs={{0,1},{1,0},{2,3},{3,2},{4,5},{5,4},{6,7},{7,6},{8,9},{9,8},{10,11... | collective-permute-start | bytes 1572872 | tf_op jit(solution)/shard_map/ppermute | solution.py:323
  53.8 1.9 %collective-permute-start.11 = (f32[3,512,128]{2,1,0:T(8,128)S(1)}, f32[3,512,128]{2,1,0:T(8,128)S(1)}, u32[]{:S(2)}, u32[]{:S(2)}) collective-permute-start(f32[3,512,128]{2,1,0:T(8,128)S(1)} %get-tuple-element.64), channel_id=1, source_target_pairs={{33,64},{35,66},{37,68},{39,70},{41,72},{43,74},{45,76},{47,78},{4... | collective-permute-start | bytes 2359304 | tf_op jit(solution)/shard_map/ppermute | solution.py:323
  55.7 2.7 %collective-permute-done.7.got_0 = f32[2,512,128]{2,1,0:T(8,128)S(1)} collective-permute-done((f32[2,512,128]{2,1,0:T(8,128)S(1)}, f32[2,512,128]{2,1,0:T(8,128)S(1)}, u32[]{:S(2)}, u32[]{:S(2)}) %collective-permute-start.7) | collective-permute-done | bytes 524320 | tf_op jit(solution)/shard_map/ppermute | solution.py:323
  58.4 1.9 %collective-permute-start.10 = (f32[3,512,128]{2,1,0:T(8,128)S(1)}, f32[3,512,128]{2,1,0:T(8,128)S(1)}, u32[]{:S(2)}, u32[]{:S(2)}) collective-permute-start(f32[3,512,128]{2,1,0:T(8,128)S(1)} %get-tuple-element.63), channel_id=1, source_target_pairs={{1,33},{3,35},{5,37},{7,39},{9,41},{11,43},{13,45},{15,47},{17,49}... | collective-permute-start | bytes 2359304 | tf_op jit(solution)/shard_map/ppermute | solution.py:323
  60.3 2.5 %collective-permute-start.8 = (f32[2,128,128]{2,1,0:T(8,128)S(1)}, f32[2,128,128]{2,1,0:T(8,128)S(1)}, u32[]{:S(2)}, u32[]{:S(2)}) collective-permute-start(f32[2,128,128]{2,1,0:T(8,128)S(1)} %get-tuple-element.54), channel_id=1, source_target_pairs={{0,32},{1,33},{2,34},{3,35},{4,36},{5,37},{6,38},{7,39},{8,40},{9,... | collective-permute-start | bytes 393224 | tf_op jit(solution)/shard_map/ppermute | solution.py:323
  63.7 2.6 %prepare_a.1 = (bf16[8,256,256]{2,1,0:T(8,128)(2,1)S(1)}, bf16[4,256,256]{2,1,0:T(8,128)(2,1)S(1)}, f32[144]{0:T(256)S(1)}) custom-call(f32[8,128]{1,0:T(8,128)S(1)} %copy-done.4, s32[2,3]{1,0:T(2,128)S(1)} %copy-done.5, s32[4]{0:T(128)S(1)} %copy-done.6, f32[8,128,128]{2,1,0:T(8,128)S(1)} %copy-done.2, f32[6,128,128]{2,1,0:T(8,128)S(1)} %collective-permute-done.1.across, ...), custom_call_target="tpu_custom_call" | custom-call | flops 1000 | bytes 1024 | tf_op jit(solution)/shard_map/prepare_a/pallas_call | solution.py:370
  66.3 2.3 %collective-permute-start.12 = (f32[2,512,128]{2,1,0:T(8,128)S(1)}, f32[2,512,128]{2,1,0:T(8,128)S(1)}, u32[]{:S(2)}, u32[]{:S(2)}) collective-permute-start(f32[2,512,128]{2,1,0:T(8,128)S(1)} %collective-permute-done.7.got_0), channel_id=1, source_target_pairs={{0,32},{2,34},{4,36},{6,38},{8,40},{10,42},{12,44},{14,46},{16,48}... | collective-permute-start | bytes 1572872 | tf_op jit(solution)/shard_map/ppermute | solution.py:323
  68.6 9.3 %collective-permute-done.9.got_1 = f32[2,512,128]{2,1,0:T(8,128)S(1)} collective-permute-done((f32[2,512,128]{2,1,0:T(8,128)S(1)}, f32[2,512,128]{2,1,0:T(8,128)S(1)}, u32[]{:S(2)}, u32[]{:S(2)}) %collective-permute-start.9) | collective-permute-done | bytes 524320 | tf_op jit(solution)/shard_map/ppermute | solution.py:323
  78.0 2.3 %collective-permute-start.13 = (f32[1,512,128]{2,1,0:T(8,128)S(1)}, f32[1,512,128]{2,1,0:T(8,128)S(1)}, u32[]{:S(2)}, u32[]{:S(2)}) collective-permute-start(f32[1,512,128]{2,1,0:T(8,128)S(1)} %slice.4), channel_id=1, source_target_pairs={{0,32},{2,34},{4,36},{6,38},{8,40},{10,42},{12,44},{14,46},{16,48}... | collective-permute-start | bytes 786440 | tf_op jit(solution)/shard_map/ppermute | solution.py:323
  81.5 4.9 %sweep_a.1 = f32[512,1024]{1,0:T(8,128)} custom-call(f32[144]{0:T(256)S(1)} %get-tuple-element.55.coef, bf16[8,256,256]{2,1,0:T(8,128)(2,1)S(1)} %get-tuple-element.58.weights, bf16[4,256,256]{2,1,0:T(8,128)(2,1)S(1)} %get-tuple-element.59.ends, f32[2,512,128]{2,1,0:T(8,128)S(1)} %get-tuple-element.50.refs_7_.kept_0, ...), custom_call_target="tpu_custom_call" | custom-call | flops 4000 | bytes 1024 | tf_op jit(solution)/shard_map/sweep_a/pallas_call | solution.py:379
  (30 shorter events, 5.0 us)
Async XLA Ops:
  0.0 1.6 %copy-start = (f32[1024,512]{1,0:T(8,128)S(1)}, f32[1024,512]{1,0:T(8,128)}, u32[]{:S(2)}) copy-start(f32[1024,512]{1,0:T(8,128)} %refs_2_.1) | copy-start | bytes 6291460
  1.6 2.3 %copy-start.2 = (f32[8,128,128]{2,1,0:T(8,128)S(1)}, f32[8,128,128]{2,1,0:T(8,128)}, u32[]{:S(2)}) copy-start(f32[8,128,128]{2,1,0:T(8,128)} %own.1) | copy-start | bytes 1572868
  1.6 2.3 %copy-start.3 = (f32[4,128,128]{2,1,0:T(8,128)S(1)}, f32[4,128,128]{2,1,0:T(8,128)}, u32[]{:S(2)}) copy-start(f32[4,128,128]{2,1,0:T(8,128)} %own) | copy-start | bytes 786436
  1.6 22.2 %collective-permute-start = (f32[256,512]{1,0:T(8,128)S(1)}, f32[256,512]{1,0:T(8,128)S(1)}, u32[]{:S(2)}, u32[]{:S(2)}) collective-permute-start(f32[256,512]{1,0:T(8,128)S(1)} %pack_first.1), channel_id=1, source_target_pairs={{0,1},{1,0},{2,3},{3,2},{4,5},{5,4},{6,7},{7,6},{8,9},{9,8},{10,11... | collective-permute-start | bytes 1572872 | tf_op jit(solution)/shard_map/ppermute | solution.py:323
  4.7 24.7 %copy-start.4 = (f32[8,128]{1,0:T(8,128)S(1)}, f32[8,128]{1,0:T(8,128)}, u32[]{:S(2)}) copy-start(f32[8,128]{1,0:T(8,128)} %table.3) | copy-start | bytes 12292
  4.7 24.7 %copy-start.5 = (s32[2,3]{1,0:T(2,128)S(1)}, s32[2,3]{1,0:T(2,128)}, u32[]{:S(2)}) copy-start(s32[2,3]{1,0:T(2,128)} %winds.3) | copy-start | bytes 76
  4.7 24.7 %copy-start.6 = (s32[4]{0:T(128)S(1)}, s32[4]{0:T(128)}, u32[]{:S(2)}) copy-start(s32[4]{0:T(128)} %barriers.3) | copy-start | bytes 52
  4.7 34.3 %collective-permute-start.4 = (f32[7,256,128]{2,1,0:T(8,128)S(1)}, f32[7,256,128]{2,1,0:T(8,128)S(1)}, u32[]{:S(2)}, u32[]{:S(2)}) collective-permute-start(f32[7,256,128]{2,1,0:T(8,128)S(1)} %get-tuple-element.47), channel_id=1, source_target_pairs={{1,3},{2,0},{3,5},{4,2},{5,7},{6,4},{7,9},{8,6},{9,11},{10,8},{11,... | collective-permute-start | bytes 2752520 | tf_op jit(solution)/shard_map/ppermute | solution.py:323
  7.5 16.3 %collective-permute-start.1 = (f32[6,128,128]{2,1,0:T(8,128)S(1)}, f32[6,128,128]{2,1,0:T(8,128)S(1)}, u32[]{:S(2)}, u32[]{:S(2)}) collective-permute-start(f32[6,128,128]{2,1,0:T(8,128)S(1)} %get-tuple-element.38), channel_id=1, source_target_pairs={{0,481},{1,480},{2,483},{3,482},{4,485},{5,484},{6,487},{7,486},{8... | collective-permute-start | bytes 1179656 | tf_op jit(solution)/shard_map/ppermute | solution.py:323
  13.9 25.1 %copy-start.1 = (f32[1024,512]{1,0:T(8,128)S(1)}, f32[1024,512]{1,0:T(8,128)}, u32[]{:S(2)}) copy-start(f32[1024,512]{1,0:T(8,128)} %refs_2_.1) | copy-start | bytes 6291460
  13.9 18.0 %collective-permute-start.2 = (f32[256,512]{1,0:T(8,128)S(1)}, f32[256,512]{1,0:T(8,128)S(1)}, u32[]{:S(2)}, u32[]{:S(2)}) collective-permute-start(f32[256,512]{1,0:T(8,128)S(1)} %pack_swap.1), channel_id=1, source_target_pairs={{0,1},{1,0},{2,3},{3,2},{4,5},{5,4},{6,7},{7,6},{8,9},{9,8},{10,11... | collective-permute-start | bytes 1572872 | tf_op jit(solution)/shard_map/ppermute | solution.py:323
  23.9 12.3 %collective-permute-start.3 = (f32[3,256,128]{2,1,0:T(8,128)S(1)}, f32[3,256,128]{2,1,0:T(8,128)S(1)}, u32[]{:S(2)}, u32[]{:S(2)}) collective-permute-start(f32[3,256,128]{2,1,0:T(8,128)S(1)} %pack_halo.2), channel_id=1, source_target_pairs={{0,2},{2,4},{3,1},{4,6},{5,3},{6,8},{7,5},{8,10},{9,7},{10,12},{11... | collective-permute-start | bytes 1179656 | tf_op jit(solution)/shard_map/ppermute | solution.py:323
  26.8 12.3 %collective-permute-start.6 = (f32[2,128,128]{2,1,0:T(8,128)S(1)}, f32[2,128,128]{2,1,0:T(8,128)S(1)}, u32[]{:S(2)}, u32[]{:S(2)}) collective-permute-start(f32[2,128,128]{2,1,0:T(8,128)S(1)} %pack_edge.1), channel_id=1, source_target_pairs={{0,2},{2,4},{3,1},{4,6},{5,3},{6,8},{7,5},{8,10},{9,7},{10,12},{11... | collective-permute-start | bytes 393224 | tf_op jit(solution)/shard_map/ppermute | solution.py:323
  32.0 13.9 %collective-permute-start.5 = (f32[3,256,128]{2,1,0:T(8,128)S(1)}, f32[3,256,128]{2,1,0:T(8,128)S(1)}, u32[]{:S(2)}, u32[]{:S(2)}) collective-permute-start(f32[3,256,128]{2,1,0:T(8,128)S(1)} %pack_halo.3), channel_id=1, source_target_pairs={{0,2},{2,4},{3,1},{4,6},{5,3},{6,8},{7,5},{8,10},{9,7},{10,12},{11... | collective-permute-start | bytes 1179656 | tf_op jit(solution)/shard_map/ppermute | solution.py:323
  41.4 17.0 %collective-permute-start.7 = (f32[2,512,128]{2,1,0:T(8,128)S(1)}, f32[2,512,128]{2,1,0:T(8,128)S(1)}, u32[]{:S(2)}, u32[]{:S(2)}) collective-permute-start(f32[2,512,128]{2,1,0:T(8,128)S(1)} %get-tuple-element.51.refs_8_), channel_id=1, source_target_pairs={{0,1},{1,0},{2,3},{3,2},{4,5},{5,4},{6,7},{7,6},{8,9},{9,8},{10,11... | collective-permute-start | bytes 1572872 | tf_op jit(solution)/shard_map/ppermute | solution.py:323
  48.3 29.7 %collective-permute-start.9 = (f32[2,512,128]{2,1,0:T(8,128)S(1)}, f32[2,512,128]{2,1,0:T(8,128)S(1)}, u32[]{:S(2)}, u32[]{:S(2)}) collective-permute-start(f32[2,512,128]{2,1,0:T(8,128)S(1)} %get-tuple-element.62), channel_id=1, source_target_pairs={{0,1},{1,0},{2,3},{3,2},{4,5},{5,4},{6,7},{7,6},{8,9},{9,8},{10,11... | collective-permute-start | bytes 1572872 | tf_op jit(solution)/shard_map/ppermute | solution.py:323
  53.8 27.7 %collective-permute-start.11 = (f32[3,512,128]{2,1,0:T(8,128)S(1)}, f32[3,512,128]{2,1,0:T(8,128)S(1)}, u32[]{:S(2)}, u32[]{:S(2)}) collective-permute-start(f32[3,512,128]{2,1,0:T(8,128)S(1)} %get-tuple-element.64), channel_id=1, source_target_pairs={{33,64},{35,66},{37,68},{39,70},{41,72},{43,74},{45,76},{47,78},{4... | collective-permute-start | bytes 2359304 | tf_op jit(solution)/shard_map/ppermute | solution.py:323
  58.4 23.1 %collective-permute-start.10 = (f32[3,512,128]{2,1,0:T(8,128)S(1)}, f32[3,512,128]{2,1,0:T(8,128)S(1)}, u32[]{:S(2)}, u32[]{:S(2)}) collective-permute-start(f32[3,512,128]{2,1,0:T(8,128)S(1)} %get-tuple-element.63), channel_id=1, source_target_pairs={{1,33},{3,35},{5,37},{7,39},{9,41},{11,43},{13,45},{15,47},{17,49}... | collective-permute-start | bytes 2359304 | tf_op jit(solution)/shard_map/ppermute | solution.py:323
  60.3 3.4 %collective-permute-start.8 = (f32[2,128,128]{2,1,0:T(8,128)S(1)}, f32[2,128,128]{2,1,0:T(8,128)S(1)}, u32[]{:S(2)}, u32[]{:S(2)}) collective-permute-start(f32[2,128,128]{2,1,0:T(8,128)S(1)} %get-tuple-element.54), channel_id=1, source_target_pairs={{0,32},{1,33},{2,34},{3,35},{4,36},{5,37},{6,38},{7,39},{8,40},{9,... | collective-permute-start | bytes 393224 | tf_op jit(solution)/shard_map/ppermute | solution.py:323
  66.3 15.1 %collective-permute-start.12 = (f32[2,512,128]{2,1,0:T(8,128)S(1)}, f32[2,512,128]{2,1,0:T(8,128)S(1)}, u32[]{:S(2)}, u32[]{:S(2)}) collective-permute-start(f32[2,512,128]{2,1,0:T(8,128)S(1)} %collective-permute-done.7.got_0), channel_id=1, source_target_pairs={{0,32},{2,34},{4,36},{6,38},{8,40},{10,42},{12,44},{14,46},{16,48}... | collective-permute-start | bytes 1572872 | tf_op jit(solution)/shard_map/ppermute | solution.py:323
  78.0 3.5 %collective-permute-start.13 = (f32[1,512,128]{2,1,0:T(8,128)S(1)}, f32[1,512,128]{2,1,0:T(8,128)S(1)}, u32[]{:S(2)}, u32[]{:S(2)}) collective-permute-start(f32[1,512,128]{2,1,0:T(8,128)S(1)} %slice.4), channel_id=1, source_target_pairs={{0,32},{2,34},{4,36},{6,38},{8,40},{10,42},{12,44},{14,46},{16,48}... | collective-permute-start | bytes 786440 | tf_op jit(solution)/shard_map/ppermute | solution.py:323

commit v8 on v6

--- a/solution.py
+++ b/solution.py
@@ -264,18 +264,9 @@
 
 
 def sweep_a(coef, weights, ends, kept_0, kept_1, got_0, got_1, same, cross, relay_0, relay_1, out,
-            window, other, sems):
+            window, other):
     l = side()
     k = lax.rem(lax.axis_index("row"), 2)
-
-    @pl.when(k == l)
-    def _():
-        run_copies([(cross.at[q], window.at[13 - q]) for q in range(3)], sems)
-
-    @pl.when(k != l)
-    def _():
-        copies = [(relay_0.at[u], window.at[12 - u]) for u in range(2)]
-        run_copies(copies + [(relay_1.at[0], window.at[13])], sems)
 
     def source(p):
         if p < 3:
@@ -284,7 +275,8 @@
             return (got_0, got_1)[p > 4][p % 2 if p > 4 else 4 - p]
         if p < 11:
             return (kept_1, kept_0)[p > 8][1 - p % 2]
-        return window[p]
+        relayed = relay_1[0] if p == 13 else relay_0[12 - p]
+        return jnp.where(k == l, cross[13 - p], relayed)
 
     first_steps(source, window, other, weights, ends, coef)
     for p in range(3, WINDOW - 3):
@@ -379,7 +371,7 @@
 
     field = pltpu.VMEM((WINDOW, 512, LEV), F32)
     return call(
-        sweep_a, shaped(512, 1024), [SMEM] + [VMEM] * 7 + [ANY] * 3, VMEM, [field, field, dma(3)],
+        sweep_a, shaped(512, 1024), [SMEM] + [VMEM] * 10, VMEM, [field, field],
         4 * 10**3, "sweep_a",
     )(coef_a, weights_a, ends_a, kept_0, kept_1, got_0, got_1, same, cross, relay_0, relay_1)
 

time: 82.9 us -> 83 us (level)
  the two profiles are of different devices: /device:TPU:105 before, /device:TPU:233 now
where the time goes in v8:
time: 83 us; the launch traced here: 82.5 us
  starting transfers between devices  37.3 us (45%)
  waiting for transfers between devices  27.3 us (33%)
  Pallas kernels  16 us (19%)
  local copies, waits for them, and re-layouts  1.64 us (2%)
    ppermute x13, starting transfers between devices, per_device(): lax.ppermute(value, AXES, pairs(move, x_size, z_size))  37.3 us
    ppermute x13, waiting for transfers between devices, per_device(): lax.ppermute(value, AXES, pairs(move, x_size, z_size))  27.3 us
    pallas_call x1, Pallas kernels, per_device(): call(sweep_a, shaped(512, 1024), [SMEM] + [VMEM] * 10, VMEM, [field, fiel...  4.98 us
    pallas_call x1, Pallas kernels, per_device(): call(prepare_a, (weight, ends, shaped(144)), [SMEM] * 3 + [VMEM] * 3, (VM...  2.61 us
    pallas_call x1, Pallas kernels, per_device(): call(prepare_b, (weight, shaped(144)), [SMEM] * 3 + [VMEM] * 2, (VMEM, SM...  2.46 us
    pallas_call x1, Pallas kernels, per_device(): call(functools.partial(sweep_b, 1), (block, block, shaped(3, 512, LEV), s...  2.34 us
    pallas_call x1, Pallas kernels, per_device(): call(functools.partial(sweep_b, 0), (block, block, ends), [SMEM] + [VMEM]...  2.32 us
  transfers between devices with their start and end apart: 13, of which 8 were waited for; matrix products, arithmetic and copies ran while one was open for 0% of the time, Pallas kernels for 13%

profile of v8, /device:TPU:233, one launch (start us, length us, event | category | flops | bytes accessed | tf_op | source)
XLA Modules:
  0.0 82.5 jit_solution(1999378690608290822)
XLA Ops:
  0.0 1.6 %copy-done = f32[1024,512]{1,0:T(8,128)S(1)} copy-done((f32[1024,512]{1,0:T(8,128)S(1)}, f32[1024,512]{1,0:T(8,128)}, u32[]{:S(2)}) %copy-start) | copy-done | bytes 2097176
  1.6 2.2 %collective-permute-start.1 = (f32[256,512]{1,0:T(8,128)S(1)}, f32[256,512]{1,0:T(8,128)S(1)}, u32[]{:S(2)}, u32[]{:S(2)}) collective-permute-start(f32[256,512]{1,0:T(8,128)S(1)} %pack_first.1), channel_id=1, source_target_pairs={{0,1},{1,0},{2,3},{3,2},{4,5},{5,4},{6,7},{7,6},{8,9},{9,8},{10,11... | collective-permute-start | bytes 1572872 | tf_op jit(solution)/shard_map/ppermute | solution.py:319
  4.7 5.0 %collective-permute-start = (f32[6,128,128]{2,1,0:T(8,128)S(1)}, f32[6,128,128]{2,1,0:T(8,128)S(1)}, u32[]{:S(2)}, u32[]{:S(2)}) collective-permute-start(f32[6,128,128]{2,1,0:T(8,128)S(1)} %get-tuple-element.34), channel_id=1, source_target_pairs={{0,481},{1,480},{2,483},{3,482},{4,485},{5,484},{6,487},{7,486},{8... | collective-permute-start | bytes 1179656 | tf_op jit(solution)/shard_map/ppermute | solution.py:319
  9.7 4.8 %collective-permute-start.4 = (f32[7,256,128]{2,1,0:T(8,128)S(1)}, f32[7,256,128]{2,1,0:T(8,128)S(1)}, u32[]{:S(2)}, u32[]{:S(2)}) collective-permute-start(f32[7,256,128]{2,1,0:T(8,128)S(1)} %get-tuple-element.39), channel_id=1, source_target_pairs={{1,3},{2,0},{3,5},{4,2},{5,7},{6,4},{7,9},{8,6},{9,11},{10,8},{11,... | collective-permute-start | bytes 2752520 | tf_op jit(solution)/shard_map/ppermute | solution.py:319
  14.6 2.1 %collective-permute-start.3 = (f32[256,512]{1,0:T(8,128)S(1)}, f32[256,512]{1,0:T(8,128)S(1)}, u32[]{:S(2)}, u32[]{:S(2)}) collective-permute-start(f32[256,512]{1,0:T(8,128)S(1)} %pack_swap.1), channel_id=1, source_target_pairs={{0,1},{1,0},{2,3},{3,2},{4,5},{5,4},{6,7},{7,6},{8,9},{9,8},{10,11... | collective-permute-start | bytes 1572872 | tf_op jit(solution)/shard_map/ppermute | solution.py:319
  16.6 3.0 %collective-permute-done.across = f32[6,128,128]{2,1,0:T(8,128)S(1)} collective-permute-done((f32[6,128,128]{2,1,0:T(8,128)S(1)}, f32[6,128,128]{2,1,0:T(8,128)S(1)}, u32[]{:S(2)}, u32[]{:S(2)}) %collective-permute-start) | collective-permute-done | bytes 393248 | tf_op jit(solution)/shard_map/ppermute | solution.py:319
  20.0 1.9 %collective-permute-start.2 = (f32[4,256,128]{2,1,0:T(8,128)S(1)}, f32[4,256,128]{2,1,0:T(8,128)S(1)}, u32[]{:S(2)}, u32[]{:S(2)}) collective-permute-start(f32[4,256,128]{2,1,0:T(8,128)S(1)} %pack_far.1), channel_id=1, source_target_pairs={{0,2},{2,4},{3,1},{4,6},{5,3},{6,8},{7,5},{8,10},{9,7},{10,12},{11... | collective-permute-start | bytes 1572872 | tf_op jit(solution)/shard_map/ppermute | solution.py:319
  21.9 2.5 %prepare_b.1 = (bf16[8,256,256]{2,1,0:T(8,128)(2,1)S(1)}, f32[144]{0:T(256)S(1)}) custom-call(f32[8,128]{1,0:T(8,128)S(1)} %copy-done.4, s32[2,3]{1,0:T(2,128)S(1)} %copy-done.5, s32[4]{0:T(128)S(1)} %copy-done.6, f32[6,128,128]{2,1,0:T(8,128)S(1)} %collective-permute-done.across, f32[4,128,128]{2,1,0:T(8,128)S(1)} %copy-done.3), custom_call_target="tpu_custom_call" | custom-call | flops 1000 | bytes 1024 | tf_op jit(solution)/shard_map/prepare_b/pallas_call | solution.py:341
  24.4 3.6 %collective-permute-done.3.pair.refs_3_ = f32[256,512]{1,0:T(8,128)S(1)} collective-permute-done((f32[256,512]{1,0:T(8,128)S(1)}, f32[256,512]{1,0:T(8,128)S(1)}, u32[]{:S(2)}, u32[]{:S(2)}) %collective-permute-start.3) | collective-permute-done | bytes 524320 | tf_op jit(solution)/shard_map/ppermute | solution.py:319
  28.1 1.9 %collective-permute-start.5 = (f32[3,256,128]{2,1,0:T(8,128)S(1)}, f32[3,256,128]{2,1,0:T(8,128)S(1)}, u32[]{:S(2)}, u32[]{:S(2)}) collective-permute-start(f32[3,256,128]{2,1,0:T(8,128)S(1)} %pack_halo.1), channel_id=1, source_target_pairs={{0,2},{2,4},{3,1},{4,6},{5,3},{6,8},{7,5},{8,10},{9,7},{10,12},{11... | collective-permute-start | bytes 1179656 | tf_op jit(solution)/shard_map/ppermute | solution.py:319
  30.0 6.2 %collective-permute-done.2.refs_5_ = f32[4,256,128]{2,1,0:T(8,128)S(1)} collective-permute-done((f32[4,256,128]{2,1,0:T(8,128)S(1)}, f32[4,256,128]{2,1,0:T(8,128)S(1)}, u32[]{:S(2)}, u32[]{:S(2)}) %collective-permute-start.2) | collective-permute-done | bytes 524320 | tf_op jit(solution)/shard_map/ppermute | solution.py:319
  36.2 2.3 %sweep_b0.1 = (f32[2,512,128]{2,1,0:T(8,128)S(1)}, f32[2,512,128]{2,1,0:T(8,128)S(1)}, bf16[4,256,256]{2,1,0:T(8,128)(2,1)S(1)}) custom-call(f32[144]{0:T(256)S(1)} %get-tuple-element.35.refs_0_, bf16[8,256,256]{2,1,0:T(8,128)(2,1)S(1)} %get-tuple-element.38.refs_1_, f32[1024,512]{1,0:T(8,128)S(1)} %copy-done.1, ...), custom_call_target="tpu_custom_call" | custom-call | flops 4000000000 | bytes 1024 | tf_op jit(solution)/shard_map/sweep_b0/pallas_call | solution.py:349
  38.5 3.1 %collective-permute-start.6 = (f32[2,512,128]{2,1,0:T(8,128)S(1)}, f32[2,512,128]{2,1,0:T(8,128)S(1)}, u32[]{:S(2)}, u32[]{:S(2)}) collective-permute-start(f32[2,512,128]{2,1,0:T(8,128)S(1)} %get-tuple-element.43.refs_8_), channel_id=1, source_target_pairs={{0,1},{1,0},{2,3},{3,2},{4,5},{5,4},{6,7},{7,6},{8,9},{9,8},{10,11... | collective-permute-start | bytes 1572872 | tf_op jit(solution)/shard_map/ppermute | solution.py:319
  41.6 2.4 %collective-permute-done.5.refs_5_ = f32[3,256,128]{2,1,0:T(8,128)S(1)} collective-permute-done((f32[3,256,128]{2,1,0:T(8,128)S(1)}, f32[3,256,128]{2,1,0:T(8,128)S(1)}, u32[]{:S(2)}, u32[]{:S(2)}) %collective-permute-start.5) | collective-permute-done | bytes 393248 | tf_op jit(solution)/shard_map/ppermute | solution.py:319
  44.0 2.3 %sweep_b1.1 = (f32[2,512,128]{2,1,0:T(8,128)S(1)}, f32[2,512,128]{2,1,0:T(8,128)S(1)}, f32[3,512,128]{2,1,0:T(8,128)S(1)}, f32[3,512,128]{2,1,0:T(8,128)S(1)}) custom-call(f32[144]{0:T(256)S(1)} %get-tuple-element.35.refs_0_, bf16[8,256,256]{2,1,0:T(8,128)(2,1)S(1)} %get-tuple-element.38.refs_1_, f32[1024,512]{1,0:T(8,128)S(1)} %copy-done.1, ...), custom_call_target="tpu_custom_call" | custom-call | flops 4000000000 | bytes 1024 | tf_op jit(solution)/shard_map/sweep_b1/pallas_call | solution.py:354
  46.4 3.3 %collective-permute-start.8 = (f32[2,512,128]{2,1,0:T(8,128)S(1)}, f32[2,512,128]{2,1,0:T(8,128)S(1)}, u32[]{:S(2)}, u32[]{:S(2)}) collective-permute-start(f32[2,512,128]{2,1,0:T(8,128)S(1)} %get-tuple-element.54), channel_id=1, source_target_pairs={{0,1},{1,0},{2,3},{3,2},{4,5},{5,4},{6,7},{7,6},{8,9},{9,8},{10,11... | collective-permute-start | bytes 1572872 | tf_op jit(solution)/shard_map/ppermute | solution.py:319
  49.7 3.4 %collective-permute-start.10 = (f32[3,512,128]{2,1,0:T(8,128)S(1)}, f32[3,512,128]{2,1,0:T(8,128)S(1)}, u32[]{:S(2)}, u32[]{:S(2)}) collective-permute-start(f32[3,512,128]{2,1,0:T(8,128)S(1)} %get-tuple-element.56), channel_id=1, source_target_pairs={{33,64},{35,66},{37,68},{39,70},{41,72},{43,74},{45,76},{47,78},{4... | collective-permute-start | bytes 2359304 | tf_op jit(solution)/shard_map/ppermute | solution.py:319
  54.0 2.9 %collective-permute-start.9 = (f32[3,512,128]{2,1,0:T(8,128)S(1)}, f32[3,512,128]{2,1,0:T(8,128)S(1)}, u32[]{:S(2)}, u32[]{:S(2)}) collective-permute-start(f32[3,512,128]{2,1,0:T(8,128)S(1)} %get-tuple-element.55), channel_id=1, source_target_pairs={{1,33},{3,35},{5,37},{7,39},{9,41},{11,43},{13,45},{15,47},{17,49}... | collective-permute-start | bytes 2359304 | tf_op jit(solution)/shard_map/ppermute | solution.py:319
  56.9 1.9 %collective-permute-start.7 = (f32[2,128,128]{2,1,0:T(8,128)S(1)}, f32[2,128,128]{2,1,0:T(8,128)S(1)}, u32[]{:S(2)}, u32[]{:S(2)}) collective-permute-start(f32[2,128,128]{2,1,0:T(8,128)S(1)} %get-tuple-element.46), channel_id=1, source_target_pairs={{0,32},{1,33},{2,34},{3,35},{4,36},{5,37},{6,38},{7,39},{8,40},{9,... | collective-permute-start | bytes 393224 | tf_op jit(solution)/shard_map/ppermute | solution.py:319
  60.1 2.6 %prepare_a.1 = (bf16[8,256,256]{2,1,0:T(8,128)(2,1)S(1)}, bf16[4,256,256]{2,1,0:T(8,128)(2,1)S(1)}, f32[144]{0:T(256)S(1)}) custom-call(f32[8,128]{1,0:T(8,128)S(1)} %copy-done.4, s32[2,3]{1,0:T(2,128)S(1)} %copy-done.5, s32[4]{0:T(128)S(1)} %copy-done.6, f32[8,128,128]{2,1,0:T(8,128)S(1)} %copy-done.2, f32[6,128,128]{2,1,0:T(8,128)S(1)} %collective-permute-done.across, ...), custom_call_target="tpu_custom_call" | custom-call | flops 1000 | bytes 1024 | tf_op jit(solution)/shard_map/prepare_a/pallas_call | solution.py:364
  62.7 2.1 %collective-permute-start.11 = (f32[2,512,128]{2,1,0:T(8,128)S(1)}, f32[2,512,128]{2,1,0:T(8,128)S(1)}, u32[]{:S(2)}, u32[]{:S(2)}) collective-permute-start(f32[2,512,128]{2,1,0:T(8,128)S(1)} %collective-permute-done.6.got_0), channel_id=1, source_target_pairs={{0,32},{2,34},{4,36},{6,38},{8,40},{10,42},{12,44},{14,46},{16,48}... | collective-permute-start | bytes 1572872 | tf_op jit(solution)/shard_map/ppermute | solution.py:319
  64.8 8.8 %collective-permute-done.8.got_1 = f32[2,512,128]{2,1,0:T(8,128)S(1)} collective-permute-done((f32[2,512,128]{2,1,0:T(8,128)S(1)}, f32[2,512,128]{2,1,0:T(8,128)S(1)}, u32[]{:S(2)}, u32[]{:S(2)}) %collective-permute-start.8) | collective-permute-done | bytes 524320 | tf_op jit(solution)/shard_map/ppermute | solution.py:319
  73.6 2.7 %collective-permute-start.12 = (f32[1,512,128]{2,1,0:T(8,128)S(1)}, f32[1,512,128]{2,1,0:T(8,128)S(1)}, u32[]{:S(2)}, u32[]{:S(2)}) collective-permute-start(f32[1,512,128]{2,1,0:T(8,128)S(1)} %slice.4), channel_id=1, source_target_pairs={{0,32},{2,34},{4,36},{6,38},{8,40},{10,42},{12,44},{14,46},{16,48}... | collective-permute-start | bytes 786440 | tf_op jit(solution)/shard_map/ppermute | solution.py:319
  77.5 5.0 %sweep_a.1 = f32[512,1024]{1,0:T(8,128)} custom-call(f32[144]{0:T(256)S(1)} %get-tuple-element.47.coef, bf16[8,256,256]{2,1,0:T(8,128)(2,1)S(1)} %get-tuple-element.50.weights, bf16[4,256,256]{2,1,0:T(8,128)(2,1)S(1)} %get-tuple-element.51.ends, f32[2,512,128]{2,1,0:T(8,128)S(1)} %get-tuple-element.42.refs_7_.kept_0, ...), custom_call_target="tpu_custom_call" | custom-call | flops 4000 | bytes 1024 | tf_op jit(solution)/shard_map/sweep_a/pallas_call | solution.py:373
  (27 shorter events, 4.6 us)
Async XLA Ops:
  0.0 1.6 %copy-start = (f32[1024,512]{1,0:T(8,128)S(1)}, f32[1024,512]{1,0:T(8,128)}, u32[]{:S(2)}) copy-start(f32[1024,512]{1,0:T(8,128)} %refs_2_.1) | copy-start | bytes 6291460
  1.6 2.3 %copy-start.2 = (f32[8,128,128]{2,1,0:T(8,128)S(1)}, f32[8,128,128]{2,1,0:T(8,128)}, u32[]{:S(2)}) copy-start(f32[8,128,128]{2,1,0:T(8,128)} %own.1) | copy-start | bytes 1572868
  1.6 2.3 %copy-start.3 = (f32[4,128,128]{2,1,0:T(8,128)S(1)}, f32[4,128,128]{2,1,0:T(8,128)}, u32[]{:S(2)}) copy-start(f32[4,128,128]{2,1,0:T(8,128)} %own) | copy-start | bytes 786436
  1.6 18.0 %collective-permute-start.1 = (f32[256,512]{1,0:T(8,128)S(1)}, f32[256,512]{1,0:T(8,128)S(1)}, u32[]{:S(2)}, u32[]{:S(2)}) collective-permute-start(f32[256,512]{1,0:T(8,128)S(1)} %pack_first.1), channel_id=1, source_target_pairs={{0,1},{1,0},{2,3},{3,2},{4,5},{5,4},{6,7},{7,6},{8,9},{9,8},{10,11... | collective-permute-start | bytes 1572872 | tf_op jit(solution)/shard_map/ppermute | solution.py:319
  4.7 17.2 %copy-start.4 = (f32[8,128]{1,0:T(8,128)S(1)}, f32[8,128]{1,0:T(8,128)}, u32[]{:S(2)}) copy-start(f32[8,128]{1,0:T(8,128)} %table.3) | copy-start | bytes 12292
  4.7 17.2 %copy-start.5 = (s32[2,3]{1,0:T(2,128)S(1)}, s32[2,3]{1,0:T(2,128)}, u32[]{:S(2)}) copy-start(s32[2,3]{1,0:T(2,128)} %winds.3) | copy-start | bytes 76
  4.7 17.2 %copy-start.6 = (s32[4]{0:T(128)S(1)}, s32[4]{0:T(128)}, u32[]{:S(2)}) copy-start(s32[4]{0:T(128)} %barriers.3) | copy-start | bytes 52
  4.7 15.0 %collective-permute-start = (f32[6,128,128]{2,1,0:T(8,128)S(1)}, f32[6,128,128]{2,1,0:T(8,128)S(1)}, u32[]{:S(2)}, u32[]{:S(2)}) collective-permute-start(f32[6,128,128]{2,1,0:T(8,128)S(1)} %get-tuple-element.34), channel_id=1, source_target_pairs={{0,481},{1,480},{2,483},{3,482},{4,485},{5,484},{6,487},{7,486},{8... | collective-permute-start | bytes 1179656 | tf_op jit(solution)/shard_map/ppermute | solution.py:319
  9.7 26.5 %collective-permute-start.4 = (f32[7,256,128]{2,1,0:T(8,128)S(1)}, f32[7,256,128]{2,1,0:T(8,128)S(1)}, u32[]{:S(2)}, u32[]{:S(2)}) collective-permute-start(f32[7,256,128]{2,1,0:T(8,128)S(1)} %get-tuple-element.39), channel_id=1, source_target_pairs={{1,3},{2,0},{3,5},{4,2},{5,7},{6,4},{7,9},{8,6},{9,11},{10,8},{11,... | collective-permute-start | bytes 2752520 | tf_op jit(solution)/shard_map/ppermute | solution.py:319
  14.6 21.6 %copy-start.1 = (f32[1024,512]{1,0:T(8,128)S(1)}, f32[1024,512]{1,0:T(8,128)}, u32[]{:S(2)}) copy-start(f32[1024,512]{1,0:T(8,128)} %refs_2_.1) | copy-start | bytes 6291460
  14.6 13.4 %collective-permute-start.3 = (f32[256,512]{1,0:T(8,128)S(1)}, f32[256,512]{1,0:T(8,128)S(1)}, u32[]{:S(2)}, u32[]{:S(2)}) collective-permute-start(f32[256,512]{1,0:T(8,128)S(1)} %pack_swap.1), channel_id=1, source_target_pairs={{0,1},{1,0},{2,3},{3,2},{4,5},{5,4},{6,7},{7,6},{8,9},{9,8},{10,11... | collective-permute-start | bytes 1572872 | tf_op jit(solution)/shard_map/ppermute | solution.py:319
  20.0 16.2 %collective-permute-start.2 = (f32[4,256,128]{2,1,0:T(8,128)S(1)}, f32[4,256,128]{2,1,0:T(8,128)S(1)}, u32[]{:S(2)}, u32[]{:S(2)}) collective-permute-start(f32[4,256,128]{2,1,0:T(8,128)S(1)} %pack_far.1), channel_id=1, source_target_pairs={{0,2},{2,4},{3,1},{4,6},{5,3},{6,8},{7,5},{8,10},{9,7},{10,12},{11... | collective-permute-start | bytes 1572872 | tf_op jit(solution)/shard_map/ppermute | solution.py:319
  28.1 16.0 %collective-permute-start.5 = (f32[3,256,128]{2,1,0:T(8,128)S(1)}, f32[3,256,128]{2,1,0:T(8,128)S(1)}, u32[]{:S(2)}, u32[]{:S(2)}) collective-permute-start(f32[3,256,128]{2,1,0:T(8,128)S(1)} %pack_halo.1), channel_id=1, source_target_pairs={{0,2},{2,4},{3,1},{4,6},{5,3},{6,8},{7,5},{8,10},{9,7},{10,12},{11... | collective-permute-start | bytes 1179656 | tf_op jit(solution)/shard_map/ppermute | solution.py:319
  38.5 15.4 %collective-permute-start.6 = (f32[2,512,128]{2,1,0:T(8,128)S(1)}, f32[2,512,128]{2,1,0:T(8,128)S(1)}, u32[]{:S(2)}, u32[]{:S(2)}) collective-permute-start(f32[2,512,128]{2,1,0:T(8,128)S(1)} %get-tuple-element.43.refs_8_), channel_id=1, source_target_pairs={{0,1},{1,0},{2,3},{3,2},{4,5},{5,4},{6,7},{7,6},{8,9},{9,8},{10,11... | collective-permute-start | bytes 1572872 | tf_op jit(solution)/shard_map/ppermute | solution.py:319
  46.4 27.2 %collective-permute-start.8 = (f32[2,512,128]{2,1,0:T(8,128)S(1)}, f32[2,512,128]{2,1,0:T(8,128)S(1)}, u32[]{:S(2)}, u32[]{:S(2)}) collective-permute-start(f32[2,512,128]{2,1,0:T(8,128)S(1)} %get-tuple-element.54), channel_id=1, source_target_pairs={{0,1},{1,0},{2,3},{3,2},{4,5},{5,4},{6,7},{7,6},{8,9},{9,8},{10,11... | collective-permute-start | bytes 1572872 | tf_op jit(solution)/shard_map/ppermute | solution.py:319
  49.7 27.8 %collective-permute-start.10 = (f32[3,512,128]{2,1,0:T(8,128)S(1)}, f32[3,512,128]{2,1,0:T(8,128)S(1)}, u32[]{:S(2)}, u32[]{:S(2)}) collective-permute-start(f32[3,512,128]{2,1,0:T(8,128)S(1)} %get-tuple-element.56), channel_id=1, source_target_pairs={{33,64},{35,66},{37,68},{39,70},{41,72},{43,74},{45,76},{47,78},{4... | collective-permute-start | bytes 2359304 | tf_op jit(solution)/shard_map/ppermute | solution.py:319
  54.0 23.6 %collective-permute-start.9 = (f32[3,512,128]{2,1,0:T(8,128)S(1)}, f32[3,512,128]{2,1,0:T(8,128)S(1)}, u32[]{:S(2)}, u32[]{:S(2)}) collective-permute-start(f32[3,512,128]{2,1,0:T(8,128)S(1)} %get-tuple-element.55), channel_id=1, source_target_pairs={{1,33},{3,35},{5,37},{7,39},{9,41},{11,43},{13,45},{15,47},{17,49}... | collective-permute-start | bytes 2359304 | tf_op jit(solution)/shard_map/ppermute | solution.py:319
  56.9 3.2 %collective-permute-start.7 = (f32[2,128,128]{2,1,0:T(8,128)S(1)}, f32[2,128,128]{2,1,0:T(8,128)S(1)}, u32[]{:S(2)}, u32[]{:S(2)}) collective-permute-start(f32[2,128,128]{2,1,0:T(8,128)S(1)} %get-tuple-element.46), channel_id=1, source_target_pairs={{0,32},{1,33},{2,34},{3,35},{4,36},{5,37},{6,38},{7,39},{8,40},{9,... | collective-permute-start | bytes 393224 | tf_op jit(solution)/shard_map/ppermute | solution.py:319
  62.7 14.8 %collective-permute-start.11 = (f32[2,512,128]{2,1,0:T(8,128)S(1)}, f32[2,512,128]{2,1,0:T(8,128)S(1)}, u32[]{:S(2)}, u32[]{:S(2)}) collective-permute-start(f32[2,512,128]{2,1,0:T(8,128)S(1)} %collective-permute-done.6.got_0), channel_id=1, source_target_pairs={{0,32},{2,34},{4,36},{6,38},{8,40},{10,42},{12,44},{14,46},{16,48}... | collective-permute-start | bytes 1572872 | tf_op jit(solution)/shard_map/ppermute | solution.py:319
  73.6 3.9 %collective-permute-start.12 = (f32[1,512,128]{2,1,0:T(8,128)S(1)}, f32[1,512,128]{2,1,0:T(8,128)S(1)}, u32[]{:S(2)}, u32[]{:S(2)}) collective-permute-start(f32[1,512,128]{2,1,0:T(8,128)S(1)} %slice.4), channel_id=1, source_target_pairs={{0,32},{2,34},{4,36},{6,38},{8,40},{10,42},{12,44},{14,46},{16,48}... | collective-permute-start | bytes 786440 | tf_op jit(solution)/shard_map/ppermute | solution.py:319
